TPU v7x, 32 devices: a whole 2x2x4 slice. The times are simulated.
32 devices in a mesh: dp: 4 (over z), row: 2 (over y), col: 4 (over x, core).
Axes of the slice: x: 2, y: 2, z: 4, core: 2. Of those that a mesh axis runs over, the one named last changes fastest.
Arguments:
- x_prompt: bfloat16 [4, 2048, 768], P('dp', 'row', 'col'), may hold values from -6 to 6
- x_cont: bfloat16 [4, 256, 768], P('dp', 'row', 'col'), may hold values from -6 to 6
- seg_ids: int32 [4, 256], P('dp', 'row'), may hold values from 0 to 128, as said below
- layer_map: int32 [6], replicated, may hold values from 0 to 2, as said below
- w_qkv: bfloat16 [3, 768, 3, 768], P(None, ('dp', 'row'), None, 'col'), may hold values from -0.21875 to 0.21875
- bias_qv: bfloat16 [3, 2, 768], P(None, None, 'col'), may hold values from -3 to 3
- w_out: bfloat16 [3, 768, 768], P(None, ('dp', 'row'), 'col'), may hold values from -1.75 to 1.75
- b_out: bfloat16 [3, 768], P(None, 'col'), may hold values from -2 to 2
- w_up: bfloat16 [3, 768, 3072], P(None, ('dp', 'row'), 'col'), may hold values from -0.21875 to 0.21875
- b_up: bfloat16 [3, 3072], P(None, 'col'), may hold values from -3 to 3
- w_down: bfloat16 [3, 768, 3072], P(None, ('dp', 'row'), 'col'), may hold values from -0.109375 to 0.109375
- b_down: bfloat16 [3, 768], P(None, 'col'), may hold values from -2 to 2
- ln1_gain: bfloat16 [3, 768], P(None, 'col'), may hold values from 0.099609375 to 1.8984375
- ln1_bias: bfloat16 [3, 768], P(None, 'col'), may hold values from -2 to 2
- ln2_gain: bfloat16 [3, 768], P(None, 'col'), may hold values from 0.099609375 to 1.8984375
- ln2_bias: bfloat16 [3, 768], P(None, 'col'), may hold values from -2 to 2
- cot_prompt: bfloat16 [4, 2048, 768], P('dp', 'row', 'col'), may hold values from -6 to 6
- cot_cont: bfloat16 [4, 256, 768], P('dp', 'row', 'col'), may hold values from -6 to 6
Outputs:
- y_prompt: bfloat16 [4, 2048, 768], P('dp', 'row', 'col')
- y_cont: bfloat16 [4, 256, 768], P('dp', 'row', 'col')
- dx_prompt: bfloat16 [4, 2048, 768], P('dp', 'row', 'col')
- dx_cont: bfloat16 [4, 256, 768], P('dp', 'row', 'col')
- grad_w_qkv: float32 [3, 768, 3, 768], P(None, ('dp', 'row'), None, 'col')
- grad_bias_qv: float32 [3, 2, 768], P(None, None, 'col')
- grad_w_out: float32 [3, 768, 768], P(None, ('dp', 'row'), 'col')
- grad_b_out: float32 [3, 768], P(None, 'col')
- grad_w_up: float32 [3, 768, 3072], P(None, ('dp', 'row'), 'col')
- grad_b_up: float32 [3, 3072], P(None, 'col')
- grad_w_down: float32 [3, 768, 3072], P(None, ('dp', 'row'), 'col')
- grad_b_down: float32 [3, 768], P(None, 'col')
- grad_ln1_gain: float32 [3, 768], P(None, 'col')
- grad_ln1_bias: float32 [3, 768], P(None, 'col')
- grad_ln2_gain: float32 [3, 768], P(None, 'col')
- grad_ln2_bias: float32 [3, 768], P(None, 'col')
Inputs may be any that keep to these rules, and one draw needn't show every extreme that they name: `seg_ids`: A token's id is the index, within its group's continuation tokens, of the first token of its continuation: ids never fall along a group, each aligned block of 128 continuation tokens starts a new continuation, no continuation crosses such a block, and the last such block of every group is one whole continuation. `layer_map`: every one of the 3 blocks is used by some layer.
All inputs are finite; a program needn't handle non-finite values.
Results may differ from a plain program's by a relative error of at most 0.023.
Values may be sent and summed in bfloat16 or wider, within the bound.
No kernel may reach another device: no remote copies, remote signals or barrier semaphores. Data moves between devices by JAX's collectives and lax.ppermute only.
A program may use at most 576 MiB of HBM per device.

v0:
```python
import jax
import jax.numpy as jnp
from jax import lax
from jax.sharding import PartitionSpec as P

D = 768
HD = 64
LAYERS = 6


NORM_EPS = 1e-05
MASK_FILL = -1000000000.0
GELU_COEF = 0.7978845608028654


def gelu_tanh(values):
    return (
        0.5 * values * (1.0 + jnp.tanh(GELU_COEF * (values + 0.044715 * values * values * values)))
    )


def select(stacked, block_index):
    return lax.dynamic_index_in_dim(stacked, block_index, 0, keepdims=False)


def add_into(stacked, block_index, update):
    current = lax.dynamic_index_in_dim(stacked, block_index, 0, keepdims=False)
    return lax.dynamic_update_index_in_dim(stacked, current + update, block_index, 0)


def norm_forward(hidden):
    totals = lax.psum((jnp.sum(hidden, axis=1), jnp.sum(hidden * hidden, axis=1)), "col")
    row_mean = totals[0][:, None] / D
    inverse = lax.rsqrt(totals[1][:, None] / D - row_mean * row_mean + NORM_EPS)
    return ((hidden - row_mean) * inverse, inverse)


def norm_backward(grad_normed, gain_row, centered, inverse):
    scaled = grad_normed * gain_row
    totals = lax.psum((jnp.sum(scaled, axis=1), jnp.sum(scaled * centered, axis=1)), "col")
    return inverse * (scaled - totals[0][:, None] / D - centered * totals[1][:, None] / D)


def gather_features(normed):
    return lax.all_gather(normed, "col", axis=1, tiled=True)


def gather_gradient(grad_rows):
    return lax.all_gather(grad_rows, "col", axis=1, tiled=True)


def project_rows(weight_full, inputs):
    row_share = weight_full.shape[0] // lax.axis_size("col")

    def partial_term(first_row, row_count):
        return jnp.einsum("dk,tk->dt", weight_full, inputs, preferred_element_type=jnp.float32)

    return (
        lax.psum_scatter(
            partial_term(jnp.int32(0), row_share * lax.axis_size("col")).astype(jnp.bfloat16),
            "col",
            scatter_dimension=0,
            tiled=True,
        )
        .astype(jnp.float32)
        .T
    )


def project_back(weight_full, grads_in):
    row_share = weight_full.shape[0] // lax.axis_size("col")

    def partial_term(first_row, row_count):
        return jnp.einsum("dk,tk->dt", weight_full, grads_in, preferred_element_type=jnp.float32)

    return (
        lax.psum_scatter(
            partial_term(jnp.int32(0), row_share * lax.axis_size("col")).astype(jnp.bfloat16),
            "col",
            scatter_dimension=0,
            tiled=True,
        )
        .astype(jnp.float32)
        .T
    )


def score_block(queries, key_rows, allowed):
    scores = jnp.einsum(
        "thd,khd->htk", queries, key_rows, preferred_element_type=jnp.float32
    ) * HD ** (-0.5)
    return jnp.where(allowed[None], scores, MASK_FILL)


def attend_forward(queries, key_rows, value_rows, allowed):
    scores = score_block(queries, key_rows, allowed)
    row_max = jnp.max(scores, axis=2, keepdims=True)
    exp_scores = jnp.exp(scores - row_max)
    row_total = jnp.sum(exp_scores, axis=2, keepdims=True)
    prob_low = (exp_scores / row_total).astype(jnp.bfloat16)
    outputs = jnp.einsum("htk,khd->thd", prob_low, value_rows, preferred_element_type=jnp.float32)
    return (outputs.astype(jnp.bfloat16), (row_max + jnp.log(row_total))[:, :, 0])


def attend_backward(queries, key_rows, value_rows, allowed, log_total, attn_grad):
    scores = score_block(queries, key_rows, allowed)
    attn_prob = jnp.exp(scores - log_total[:, :, None])
    prob_low = attn_prob.astype(jnp.bfloat16)
    value_grad = jnp.einsum("htk,thd->khd", prob_low, attn_grad, preferred_element_type=jnp.float32)
    prob_grad = jnp.einsum(
        "thd,khd->htk", attn_grad, value_rows, preferred_element_type=jnp.float32
    )
    row_dot = jnp.sum(attn_prob * prob_grad, axis=2, keepdims=True)
    score_grad = (attn_prob * (prob_grad - row_dot)).astype(jnp.bfloat16)
    query_grad = jnp.einsum(
        "htk,khd->thd", score_grad, key_rows, preferred_element_type=jnp.float32
    ) * HD ** (-0.5)
    key_grad = jnp.einsum(
        "htk,thd->khd", score_grad, queries, preferred_element_type=jnp.float32
    ) * HD ** (-0.5)
    return (query_grad, key_grad, value_grad)


def build_mask(seg_local, prompt_len, prompt_all):
    row_pos = lax.axis_index("row")
    cont_len = seg_local.shape[0]
    query_pos = row_pos * prompt_len + jnp.arange(prompt_len, dtype=jnp.int32)
    key_pos = jnp.arange(prompt_all, dtype=jnp.int32)
    local_pos = jnp.arange(cont_len, dtype=jnp.int32)
    prompt_rows = jnp.concatenate(
        [key_pos[None, :] <= query_pos[:, None], jnp.zeros((prompt_len, cont_len), jnp.bool_)],
        axis=1,
    )
    own_rows = (local_pos[None, :] <= local_pos[:, None]) & (
        seg_local[None, :] == seg_local[:, None]
    )
    cont_rows = jnp.concatenate([jnp.ones((cont_len, prompt_all), jnp.bool_), own_rows], axis=1)
    return jnp.concatenate([prompt_rows, cont_rows], axis=0)


def per_device(
    x_prompt,
    x_cont,
    seg_ids,
    layer_map,
    w_qkv,
    bias_qv,
    w_out,
    b_out,
    w_up,
    b_up,
    w_down,
    b_down,
    ln1_gain,
    ln1_bias,
    ln2_gain,
    ln2_bias,
    cot_prompt,
    cot_cont,
):
    prompt_len = x_prompt.shape[1]
    cont_len = x_cont.shape[1]
    width_col = x_prompt.shape[2]
    heads_col = width_col // HD
    prompt_all = prompt_len * lax.axis_size("row")
    key_count = prompt_all + cont_len
    tok_count = prompt_len + cont_len
    allowed = build_mask(seg_ids[0], prompt_len, prompt_all)
    hidden = jnp.concatenate([x_prompt[0], x_cont[0]], axis=0).astype(jnp.float32)
    stored = []
    for layer_pos in range(LAYERS):
        block_index = layer_map[layer_pos]
        layer_w = (
            lax.all_gather(select(w_qkv, block_index), ("dp", "row"), axis=0, tiled=True),
            lax.all_gather(select(w_out, block_index), ("dp", "row"), axis=0, tiled=True),
            lax.all_gather(select(w_up, block_index), ("dp", "row"), axis=0, tiled=True),
            lax.all_gather(select(w_down, block_index), ("dp", "row"), axis=0, tiled=True),
        )
        qkv_full, out_full, up_full, down_full = layer_w
        centered1, inverse1 = norm_forward(hidden)
        normed1 = (
            centered1 * select(ln1_gain, block_index).astype(jnp.float32)
            + select(ln1_bias, block_index).astype(jnp.float32)
        ).astype(jnp.bfloat16)
        gathered1 = gather_features(normed1)
        pair_bias = select(bias_qv, block_index).astype(jnp.float32)
        qkv_bias = jnp.stack([pair_bias[0], jnp.zeros_like(pair_bias[0]), pair_bias[1]])
        mixed_qkv = (
            jnp.einsum("td,dsk->tsk", gathered1, qkv_full, preferred_element_type=jnp.float32)
            + qkv_bias
        ).astype(jnp.bfloat16)
        prompt_kv = lax.all_gather(mixed_qkv[:prompt_len, 1:], "row", axis=0, tiled=True)
        key_rows = jnp.concatenate([prompt_kv[:, 0], mixed_qkv[prompt_len:, 1]], axis=0).reshape(
            key_count, heads_col, HD
        )
        value_rows = jnp.concatenate([prompt_kv[:, 1], mixed_qkv[prompt_len:, 2]], axis=0).reshape(
            key_count, heads_col, HD
        )
        queries = mixed_qkv[:, 0].reshape(tok_count, heads_col, HD)
        attn_out, log_total = attend_forward(queries, key_rows, value_rows, allowed)
        attn_flat = attn_out.reshape(tok_count, width_col)
        hidden1 = hidden + (
            project_rows(out_full, attn_flat) + select(b_out, block_index).astype(jnp.float32)
        )
        centered2, inverse2 = norm_forward(hidden1)
        normed2 = (
            centered2 * select(ln2_gain, block_index).astype(jnp.float32)
            + select(ln2_bias, block_index).astype(jnp.float32)
        ).astype(jnp.bfloat16)
        gathered2 = gather_features(normed2)
        up_proj = jnp.dot(gathered2, up_full, preferred_element_type=jnp.float32) + select(
            b_up, block_index
        ).astype(jnp.float32)
        activation = gelu_tanh(up_proj).astype(jnp.bfloat16)
        hidden = hidden1 + (
            project_rows(down_full, activation) + select(b_down, block_index).astype(jnp.float32)
        )
        stored.append(
            (
                block_index,
                centered1,
                inverse1,
                gathered1,
                queries,
                key_rows,
                value_rows,
                attn_flat,
                log_total,
                centered2,
                inverse2,
                gathered2,
                up_proj,
                activation,
            )
        )
    block_total = w_qkv.shape[0]
    acc_qkv = jnp.zeros((block_total, D, 3, width_col), jnp.float32)
    acc_out = jnp.zeros((block_total, D, width_col), jnp.float32)
    acc_up = jnp.zeros((block_total, D, w_up.shape[2]), jnp.float32)
    acc_down = jnp.zeros((block_total, D, w_down.shape[2]), jnp.float32)
    acc_bias_qv = jnp.zeros(bias_qv.shape, jnp.float32)
    acc_b_out = jnp.zeros(b_out.shape, jnp.float32)
    acc_b_up = jnp.zeros(b_up.shape, jnp.float32)
    acc_b_down = jnp.zeros(b_down.shape, jnp.float32)
    acc_gain1 = jnp.zeros(ln1_gain.shape, jnp.float32)
    acc_shift1 = jnp.zeros(ln1_bias.shape, jnp.float32)
    acc_gain2 = jnp.zeros(ln2_gain.shape, jnp.float32)
    acc_shift2 = jnp.zeros(ln2_bias.shape, jnp.float32)
    gradient = jnp.concatenate([cot_prompt[0], cot_cont[0]], axis=0).astype(jnp.float32)
    for layer_pos in reversed(range(LAYERS)):
        (
            block_index,
            centered1,
            inverse1,
            gathered1,
            queries,
            key_rows,
            value_rows,
            attn_flat,
            log_total,
            centered2,
            inverse2,
            gathered2,
            up_proj,
            activation,
        ) = stored[layer_pos]
        qkv_full, out_full, up_full, down_full = (
            lax.all_gather(select(w_qkv, block_index), ("dp", "row"), axis=0, tiled=True),
            lax.all_gather(select(w_out, block_index), ("dp", "row"), axis=0, tiled=True),
            lax.all_gather(select(w_up, block_index), ("dp", "row"), axis=0, tiled=True),
            lax.all_gather(select(w_down, block_index), ("dp", "row"), axis=0, tiled=True),
        )
        grad_low = gradient.astype(jnp.bfloat16)
        grad_full = gather_gradient(grad_low)
        grad_w_down = jnp.einsum(
            "td,tf->df", grad_full, activation, preferred_element_type=jnp.float32
        )
        act_grad = jnp.dot(grad_full, down_full, preferred_element_type=jnp.float32)
        gelu_pull = jax.vjp(gelu_tanh, up_proj)[1]
        up_grad_low = gelu_pull(act_grad)[0].astype(jnp.bfloat16)
        grad_w_up = jnp.einsum(
            "td,tf->df", gathered2, up_grad_low, preferred_element_type=jnp.float32
        )
        normed2_grad = project_back(up_full, up_grad_low)
        acc_b_down = add_into(
            acc_b_down, block_index, jnp.sum(grad_low.astype(jnp.float32), axis=0)
        )
        acc_b_up = add_into(acc_b_up, block_index, jnp.sum(up_grad_low.astype(jnp.float32), axis=0))
        acc_gain2 = add_into(acc_gain2, block_index, jnp.sum(normed2_grad * centered2, axis=0))
        acc_shift2 = add_into(acc_shift2, block_index, jnp.sum(normed2_grad, axis=0))
        gradient = gradient + norm_backward(
            normed2_grad, select(ln2_gain, block_index).astype(jnp.float32), centered2, inverse2
        )
        grad_low = gradient.astype(jnp.bfloat16)
        grad_full = gather_gradient(grad_low)
        grad_w_out = jnp.einsum(
            "td,tk->dk", grad_full, attn_flat, preferred_element_type=jnp.float32
        )
        attn_grad = (
            jnp.dot(grad_full, out_full, preferred_element_type=jnp.float32)
            .astype(jnp.bfloat16)
            .reshape(tok_count, heads_col, HD)
        )
        query_grad, key_grad, value_grad = attend_backward(
            queries, key_rows, value_rows, allowed, log_total, attn_grad
        )
        prompt_part = jnp.stack([key_grad[:prompt_all], value_grad[:prompt_all]], axis=1).reshape(
            prompt_all, 2, width_col
        )
        prompt_grads = lax.psum_scatter(
            prompt_part.astype(jnp.bfloat16), "row", scatter_dimension=0, tiled=True
        ).astype(jnp.float32)
        key_local = jnp.concatenate(
            [prompt_grads[:, 0], key_grad[prompt_all:].reshape(cont_len, width_col)], axis=0
        )
        value_local = jnp.concatenate(
            [prompt_grads[:, 1], value_grad[prompt_all:].reshape(cont_len, width_col)], axis=0
        )
        mixed_grad = jnp.stack(
            [query_grad.reshape(tok_count, width_col), key_local, value_local], axis=1
        ).astype(jnp.bfloat16)
        grad_w_qkv = jnp.einsum(
            "td,tsk->dsk", gathered1, mixed_grad, preferred_element_type=jnp.float32
        )
        normed1_grad = project_back(
            qkv_full.reshape(D, 3 * width_col), mixed_grad.reshape(tok_count, 3 * width_col)
        )
        mixed_sums = jnp.sum(mixed_grad.astype(jnp.float32), axis=0)
        acc_bias_qv = add_into(acc_bias_qv, block_index, jnp.stack([mixed_sums[0], mixed_sums[2]]))
        acc_b_out = add_into(acc_b_out, block_index, jnp.sum(grad_low.astype(jnp.float32), axis=0))
        acc_gain1 = add_into(acc_gain1, block_index, jnp.sum(normed1_grad * centered1, axis=0))
        acc_shift1 = add_into(acc_shift1, block_index, jnp.sum(normed1_grad, axis=0))
        gradient = gradient + norm_backward(
            normed1_grad, select(ln1_gain, block_index).astype(jnp.float32), centered1, inverse1
        )
        acc_qkv = add_into(acc_qkv, block_index, grad_w_qkv)
        acc_out = add_into(acc_out, block_index, grad_w_out)
        acc_up = add_into(acc_up, block_index, grad_w_up)
        acc_down = add_into(acc_down, block_index, grad_w_down)
    acc_qkv, acc_out, acc_up, acc_down = (
        lax.psum_scatter(acc_qkv, ("dp", "row"), scatter_dimension=1, tiled=True),
        lax.psum_scatter(acc_out, ("dp", "row"), scatter_dimension=1, tiled=True),
        lax.psum_scatter(acc_up, ("dp", "row"), scatter_dimension=1, tiled=True),
        lax.psum_scatter(acc_down, ("dp", "row"), scatter_dimension=1, tiled=True),
    )
    summed_small = lax.psum(
        (
            acc_bias_qv,
            acc_b_out,
            acc_b_up,
            acc_b_down,
            acc_gain1,
            acc_shift1,
            acc_gain2,
            acc_shift2,
        ),
        ("dp", "row"),
    )
    final_low = hidden.astype(jnp.bfloat16)
    grad_input = gradient.astype(jnp.bfloat16)
    return (
        final_low[None, :prompt_len],
        final_low[None, prompt_len:],
        grad_input[None, :prompt_len],
        grad_input[None, prompt_len:],
        acc_qkv,
        summed_small[0],
        acc_out,
        summed_small[1],
        acc_up,
        summed_small[2],
        acc_down,
        summed_small[3],
        summed_small[4],
        summed_small[5],
        summed_small[6],
        summed_small[7],
    )


def solution(mesh):
    in_specs = (
        P("dp", "row", "col"),
        P("dp", "row", "col"),
        P("dp", "row"),
        P(),
        P(None, ("dp", "row"), None, "col"),
        P(None, None, "col"),
        P(None, ("dp", "row"), "col"),
        P(None, "col"),
        P(None, ("dp", "row"), "col"),
        P(None, "col"),
        P(None, ("dp", "row"), "col"),
        P(None, "col"),
        P(None, "col"),
        P(None, "col"),
        P(None, "col"),
        P(None, "col"),
        P("dp", "row", "col"),
        P("dp", "row", "col"),
    )
    out_specs = (
        P("dp", "row", "col"),
        P("dp", "row", "col"),
        P("dp", "row", "col"),
        P("dp", "row", "col"),
        P(None, ("dp", "row"), None, "col"),
        P(None, None, "col"),
        P(None, ("dp", "row"), "col"),
        P(None, "col"),
        P(None, ("dp", "row"), "col"),
        P(None, "col"),
        P(None, ("dp", "row"), "col"),
        P(None, "col"),
        P(None, "col"),
        P(None, "col"),
        P(None, "col"),
        P(None, "col"),
    )
    return jax.shard_map(
        per_device, mesh=mesh, in_specs=in_specs, out_specs=out_specs, check_vma=False
    )
```

profile of v0, /device:TPU:0, one launch (start us, length us, event | category | flops | bytes accessed | tf_op | source)
XLA Modules:
  0.0 3724.8 jit_solution(10800096269226202729)
XLA Ops:
  41.6 38.3 %all-gather.1 = bf16[1,768,3,192]{3,2,0,1:T(4,128)(2,1)S(1)} all-gather(bf16[1,96,3,192]{3,2,0,1:T(4,128)(2,1)S(1)} %copy.96), channel_id=3, replica_groups=mesh['dp'=4,'row'=2,'col'=4] {'dp','row'}, dimensions={1}, use_global_device_ids=true | all-gather | bytes 995328 | tf_op jit(solution)/shard_map/all_gather | solution.py:174
  81.8 33.0 all-gather
  258.0 39.1 %all-gather.127.cloned.1.call-done = bf16[1,768,768]{2,1,0:T(8,128)(2,1)} async-done(((bf16[1,96,768]{2,1,0:T(8,128)(2,1)}), bf16[1,768,768]{2,1,0:T(8,128)(2,1)}) %all-gather.127.cloned.1.call-update) | async-done | bytes 1179664 | tf_op jit(solution)/shard_map/all_gather | solution.py:177
  343.2 37.4 %all-gather.5 = bf16[1,768,3,192]{3,2,0,1:T(4,128)(2,1)S(1)} all-gather(bf16[1,96,3,192]{3,2,0,1:T(4,128)(2,1)S(1)} %copy.97), channel_id=7, replica_groups=mesh['dp'=4,'row'=2,'col'=4] {'dp','row'}, dimensions={1}, use_global_device_ids=true | all-gather | bytes 995328 | tf_op jit(solution)/shard_map/all_gather | solution.py:174
  387.0 31.9 all-gather.4
  500.9 30.3 all-gather.133.cloned.1.call-done
  557.5 39.3 %all-gather.131.cloned.1.call-done = bf16[1,768,768]{2,1,0:T(8,128)(2,1)} async-done(((bf16[1,96,768]{2,1,0:T(8,128)(2,1)}), bf16[1,768,768]{2,1,0:T(8,128)(2,1)}) %all-gather.131.cloned.1.call-update) | async-done | bytes 1179664 | tf_op jit(solution)/shard_map/all_gather | solution.py:177
  643.6 37.8 %all-gather.9 = bf16[1,768,3,192]{3,2,0,1:T(4,128)(2,1)S(1)} all-gather(bf16[1,96,3,192]{3,2,0,1:T(4,128)(2,1)S(1)} %copy.98), channel_id=11, replica_groups=mesh['dp'=4,'row'=2,'col'=4] {'dp','row'}, dimensions={1}, use_global_device_ids=true | all-gather | bytes 995328 | tf_op jit(solution)/shard_map/all_gather | solution.py:174
  686.7 31.6 all-gather.8
  829.4 39.3 %all-gather.135.cloned.1.call-done = bf16[1,768,768]{2,1,0:T(8,128)(2,1)} async-done(((bf16[1,96,768]{2,1,0:T(8,128)(2,1)}), bf16[1,768,768]{2,1,0:T(8,128)(2,1)}) %all-gather.135.cloned.1.call-update) | async-done | bytes 1179664 | tf_op jit(solution)/shard_map/all_gather | solution.py:177
  915.2 37.8 %all-gather.13 = bf16[1,768,3,192]{3,2,0,1:T(4,128)(2,1)S(1)} all-gather(bf16[1,96,3,192]{3,2,0,1:T(4,128)(2,1)S(1)} %copy.99), channel_id=15, replica_groups=mesh['dp'=4,'row'=2,'col'=4] {'dp','row'}, dimensions={1}, use_global_device_ids=true | all-gather | bytes 995328 | tf_op jit(solution)/shard_map/all_gather | solution.py:174
  958.3 31.4 all-gather.12
  1073.5 29.6 all-gather.141.cloned.1.call-done
  1129.6 39.4 %all-gather.139.cloned.1.call-done = bf16[1,768,768]{2,1,0:T(8,128)(2,1)} async-done(((bf16[1,96,768]{2,1,0:T(8,128)(2,1)}), bf16[1,768,768]{2,1,0:T(8,128)(2,1)}) %all-gather.139.cloned.1.call-update) | async-done | bytes 1179664 | tf_op jit(solution)/shard_map/all_gather | solution.py:177
  1215.2 37.7 %all-gather.17 = bf16[1,768,3,192]{3,2,0,1:T(4,128)(2,1)S(1)} all-gather(bf16[1,96,3,192]{3,2,0,1:T(4,128)(2,1)S(1)} %copy.100), channel_id=19, replica_groups=mesh['dp'=4,'row'=2,'col'=4] {'dp','row'}, dimensions={1}, use_global_device_ids=true | all-gather | bytes 995328 | tf_op jit(solution)/shard_map/all_gather | solution.py:174
  1258.2 31.6 all-gather.16
  1372.9 30.3 all-gather.145.cloned.1.call-done
  1429.7 38.6 %all-gather.143.cloned.1.call-done = bf16[1,768,768]{2,1,0:T(8,128)(2,1)} async-done(((bf16[1,96,768]{2,1,0:T(8,128)(2,1)}), bf16[1,768,768]{2,1,0:T(8,128)(2,1)}) %all-gather.143.cloned.1.call-update) | async-done | bytes 1179664 | tf_op jit(solution)/shard_map/all_gather | solution.py:177
  1514.5 37.3 %all-gather.21 = bf16[1,768,3,192]{3,2,0,1:T(4,128)(2,1)S(1)} all-gather(bf16[1,96,3,192]{3,2,0,1:T(4,128)(2,1)S(1)} %copy.101), channel_id=23, replica_groups=mesh['dp'=4,'row'=2,'col'=4] {'dp','row'}, dimensions={1}, use_global_device_ids=true | all-gather | bytes 995328 | tf_op jit(solution)/shard_map/all_gather | solution.py:174
  1557.3 31.5 all-gather.20
  1698.9 39.1 %all-gather.147.cloned.1.call-done = bf16[1,768,768]{2,1,0:T(8,128)(2,1)} async-done(((bf16[1,96,768]{2,1,0:T(8,128)(2,1)}), bf16[1,768,768]{2,1,0:T(8,128)(2,1)}) %all-gather.147.cloned.1.call-update) | async-done | bytes 1179664 | tf_op jit(solution)/shard_map/all_gather | solution.py:177
  1770.7 29.5 reduce-scatter.59.cloned.1.call-done
  2039.9 29.5 reduce-scatter.65.cloned.1.call-done
  2210.2 29.2 reduce-scatter.69.cloned.1.call-done
  2288.7 29.4 reduce-scatter.71.cloned.1.call-done
  2538.4 29.4 reduce-scatter.77.cloned.1.call-done
  2787.7 29.5 reduce-scatter.83.cloned.1.call-done
  2958.8 29.2 reduce-scatter.87.cloned.1.call-done
  3037.8 29.3 reduce-scatter.89.cloned.1.call-done
  3472.8 40.5 %all-reduce.2 = (f32[3,2,192]{2,1,0:T(2,128)}, f32[3,192]{1,0:T(4,128)}, f32[3,768]{1,0:T(4,128)}, f32[3,192]{1,0:T(4,128)}, f32[3,192]{1,0:T(4,128)}, /*index=5...) all-reduce(f32[3,2,192]{2,1,0:T(2,128)} %constant_dynamic-update-sl, ...), channel_id=1, replica_groups=mesh['dp'=4,'row'=2,'col'=4] {'dp','row'}, use_global_device_ids=true, to_apply=%region_151.152 | all-reduce | flops 6912 | bytes 55296 | tf_op jit(solution)/shard_map/psum | solution.py:346
  3527.1 58.3 %reduce-scatter.99.cloned.1.call-done = f32[3,96,768]{2,1,0:T(8,128)} async-done(((f32[3,768,768]{2,1,0:T(8,128)}), f32[3,96,768]{2,1,0:T(8,128)}) %reduce-scatter.99.cloned.1.call-update) | async-done | bytes 884752 | tf_op jit(solution)/shard_map/reduce_scatter | solution.py:343
  3585.3 131.9 %reduce-scatter.95.cloned.1.call-done = f32[3,96,3,192]{3,1,2,0:T(8,128)} async-done(((f32[3,768,3,192]{3,1,2,0:T(8,128)}), f32[3,96,3,192]{3,1,2,0:T(8,128)}) %reduce-scatter.95.cloned.1.call-update) | async-done | bytes 663568 | tf_op jit(solution)/shard_map/reduce_scatter | solution.py:341
  (1386 shorter events, 2484.3 us)
Async XLA Ops:
  8.0 109.3 %all-gather.67.cloned.1.call-start = ((), (), s32[]{:S(2)}) async-start(), calls=%async_computation.34 | async-start | bytes 2211840 | tf_op jit(solution)/shard_map/all_gather | solution.py:45
  39.2 107.8 %all-gather.69.cloned.1.call-start = ((), (), s32[]{:S(2)}) async-start(), calls=%async_computation.35 | async-start | bytes 2359296 | tf_op jit(solution)/shard_map/all_gather | solution.py:192
  121.4 95.3 %reduce-scatter.35.cloned.1.call-start = ((), (), s32[]{:S(2)}) async-start(), calls=%async_computation.36 | async-start | bytes 2211840 | tf_op jit(solution)/shard_map/reduce_scatter | solution.py:59
  232.1 98.3 %reduce-scatter.37.cloned.1.call-start = ((), (), s32[]{:S(2)}) async-start(), calls=%async_computation.38 | async-start | bytes 2211840 | tf_op jit(solution)/shard_map/reduce_scatter | solution.py:59
  386.9 100.3 %reduce-scatter.39.cloned.1.call-start = ((), (), s32[]{:S(2)}) async-start(), calls=%async_computation.41 | async-start | bytes 2211840 | tf_op jit(solution)/shard_map/reduce_scatter | solution.py:59
  460.1 92.3 %all-gather.77.cloned.1.call-start = ((), (), s32[]{:S(2)}) async-start(), calls=%async_computation.42 | async-start | bytes 2211840 | tf_op jit(solution)/shard_map/all_gather | solution.py:45
  500.2 96.6 %all-gather.131.cloned.1.call-start = ((), (), s32[]{:S(2)}) async-start(), calls=%async_computation.100 | async-start | bytes 1327104 | tf_op jit(solution)/shard_map/all_gather | solution.py:177
  500.8 129.5 %reduce-scatter.41.cloned.1.call-start = ((), (), s32[]{:S(2)}) async-start(), calls=%async_computation.43 | async-start | bytes 2211840 | tf_op jit(solution)/shard_map/reduce_scatter | solution.py:59
  686.6 101.5 %reduce-scatter.43.cloned.1.call-start = ((), (), s32[]{:S(2)}) async-start(), calls=%async_computation.46 | async-start | bytes 2211840 | tf_op jit(solution)/shard_map/reduce_scatter | solution.py:59
  802.3 99.9 %reduce-scatter.45.cloned.1.call-start = ((), (), s32[]{:S(2)}) async-start(), calls=%async_computation.48 | async-start | bytes 2211840 | tf_op jit(solution)/shard_map/reduce_scatter | solution.py:59
  958.3 101.0 %reduce-scatter.47.cloned.1.call-start = ((), (), s32[]{:S(2)}) async-start(), calls=%async_computation.51 | async-start | bytes 2211840 | tf_op jit(solution)/shard_map/reduce_scatter | solution.py:59
  1030.8 93.6 %all-gather.89.cloned.1.call-start = ((), (), s32[]{:S(2)}) async-start(), calls=%async_computation.52 | async-start | bytes 2211840 | tf_op jit(solution)/shard_map/all_gather | solution.py:45
  1072.3 96.7 %all-gather.139.cloned.1.call-start = ((), (), s32[]{:S(2)}) async-start(), calls=%async_computation.104 | async-start | bytes 1327104 | tf_op jit(solution)/shard_map/all_gather | solution.py:177
  1073.0 129.4 %reduce-scatter.49.cloned.1.call-start = ((), (), s32[]{:S(2)}) async-start(), calls=%async_computation.53 | async-start | bytes 2211840 | tf_op jit(solution)/shard_map/reduce_scatter | solution.py:59
  1258.1 101.0 %reduce-scatter.51.cloned.1.call-start = ((), (), s32[]{:S(2)}) async-start(), calls=%async_computation.56 | async-start | bytes 2211840 | tf_op jit(solution)/shard_map/reduce_scatter | solution.py:59
  1331.0 93.5 %all-gather.95.cloned.1.call-start = ((), (), s32[]{:S(2)}) async-start(), calls=%async_computation.57 | async-start | bytes 2211840 | tf_op jit(solution)/shard_map/all_gather | solution.py:45
  1372.2 96.1 %all-gather.143.cloned.1.call-start = ((), (), s32[]{:S(2)}) async-start(), calls=%async_computation.106 | async-start | bytes 1327104 | tf_op jit(solution)/shard_map/all_gather | solution.py:177
  1372.8 129.0 %reduce-scatter.53.cloned.1.call-start = ((), (), s32[]{:S(2)}) async-start(), calls=%async_computation.58 | async-start | bytes 2211840 | tf_op jit(solution)/shard_map/reduce_scatter | solution.py:59
  1557.2 100.6 %reduce-scatter.55.cloned.1.call-start = ((), (), s32[]{:S(2)}) async-start(), calls=%async_computation.61 | async-start | bytes 2211840 | tf_op jit(solution)/shard_map/reduce_scatter | solution.py:59
  1671.7 87.0 %all-gather.103.cloned.1.call-start = ((), (), s32[]{:S(2)}) async-start(), calls=%async_computation.64 | async-start | bytes 2211840 | tf_op jit(solution)/shard_map/all_gather | solution.py:49
  1672.6 127.5 %reduce-scatter.59.cloned.1.call-start = ((), (), s32[]{:S(2)}) async-start(), calls=%async_computation.65 | async-start | bytes 2211840 | tf_op jit(solution)/shard_map/reduce_scatter | solution.py:77
  1816.4 119.3 %reduce-scatter.61.cloned.1.call-start = ((), (), s32[]{:S(2)}) async-start(), calls=%async_computation.67 | async-start | bytes 2359296 | tf_op jit(solution)/shard_map/reduce_scatter | solution.py:310
  2084.4 119.2 %reduce-scatter.67.cloned.1.call-start = ((), (), s32[]{:S(2)}) async-start(), calls=%async_computation.72 | async-start | bytes 2359296 | tf_op jit(solution)/shard_map/reduce_scatter | solution.py:310
  2334.1 119.1 %reduce-scatter.73.cloned.1.call-start = ((), (), s32[]{:S(2)}) async-start(), calls=%async_computation.77 | async-start | bytes 2359296 | tf_op jit(solution)/shard_map/reduce_scatter | solution.py:310
  2583.9 118.9 %reduce-scatter.79.cloned.1.call-start = ((), (), s32[]{:S(2)}) async-start(), calls=%async_computation.82 | async-start | bytes 2359296 | tf_op jit(solution)/shard_map/reduce_scatter | solution.py:310
  2833.3 119.2 %reduce-scatter.85.cloned.1.call-start = ((), (), s32[]{:S(2)}) async-start(), calls=%async_computation.87 | async-start | bytes 2359296 | tf_op jit(solution)/shard_map/reduce_scatter | solution.py:310
  3085.1 119.0 %reduce-scatter.91.cloned.1.call-start = ((), (), s32[]{:S(2)}) async-start(), calls=%async_computation.92 | async-start | bytes 2359296 | tf_op jit(solution)/shard_map/reduce_scatter | solution.py:310
  3177.9 288.4 %reduce-scatter.93.cloned.1.call-start = ((), (), s32[]{:S(2)}) async-start(), calls=%async_computation.93 | async-start | bytes 2211840 | tf_op jit(solution)/shard_map/reduce_scatter | solution.py:77
  3210.3 316.8 %reduce-scatter.97.cloned.1.call-start = ((), (), s32[]{:S(2)}) async-start(), calls=%async_computation.95 | async-start | bytes 2654208 | tf_op jit(solution)/shard_map/reduce_scatter | solution.py:342
  3250.4 276.7 %reduce-scatter.101.cloned.1.call-start = ((), (), s32[]{:S(2)}) async-start(), calls=%async_computation.97 | async-start | bytes 7962624 | tf_op jit(solution)/shard_map/reduce_scatter | solution.py:344
  3279.3 306.0 %reduce-scatter.99.cloned.1.call-start = ((), (), s32[]{:S(2)}) async-start(), calls=%async_computation.96 | async-start | bytes 7962624 | tf_op jit(solution)/shard_map/reduce_scatter | solution.py:343
  3315.8 401.5 %reduce-scatter.95.cloned.1.call-start = ((), (), s32[]{:S(2)}) async-start(), calls=%async_computation.94 | async-start | bytes 7962624 | tf_op jit(solution)/shard_map/reduce_scatter | solution.py:341
  (382 other events, 13368.4 us)
Sparse Core Ops, SparseCore 0:
  121.5 25.4 all-gather.68
  187.3 29.3 reduce-scatter.34
  343.1 21.3 all-gather.72
  387.0 30.2 all-gather.74
  602.4 27.8 reduce-scatter.40
  643.5 21.7 all-gather.78
  686.8 31.4 all-gather.80
  758.9 29.1 reduce-scatter.42
  874.3 27.8 reduce-scatter.44
  915.1 21.8 all-gather.84
  958.4 31.0 all-gather.86
  1174.5 27.8 reduce-scatter.48
  1215.1 21.7 all-gather.90
  1258.2 31.0 all-gather.92
  1473.9 27.8 reduce-scatter.52
  1514.5 21.7 all-gather.96
  1557.3 32.1 all-gather.98
  1628.8 28.9 reduce-scatter.54
  1770.7 29.3 reduce-scatter.58
  1816.5 21.7 all-gather.104
  1909.5 26.0 reduce-scatter.60
  2040.0 29.3 reduce-scatter.64
  2177.5 26.0 reduce-scatter.66
  2334.2 21.3 all-gather.112
  2427.0 26.0 reduce-scatter.72
  2503.7 21.3 all-gather.114
  2584.0 21.3 all-gather.116
  2676.7 26.0 reduce-scatter.78
  2787.7 29.3 reduce-scatter.82
  2926.3 26.0 reduce-scatter.84
  3085.2 21.4 all-gather.124
  3178.0 26.0 reduce-scatter.90
  (4 shorter events, 84.4 us)
Sparse Core Ops, SparseCore 1:
  189.8 41.5 all-gather.128
  255.5 41.5 all-gather.126
  302.6 27.8 reduce-scatter.36
  459.4 27.7 reduce-scatter.38
  489.6 41.5 all-gather.132
  555.3 41.5 all-gather.130
  761.7 41.2 all-gather.136
  827.2 41.5 all-gather.134
  1030.3 28.8 reduce-scatter.46
  1061.5 41.5 all-gather.140
  1127.4 41.5 all-gather.138
  1330.3 28.7 reduce-scatter.50
  1361.6 41.5 all-gather.144
  1426.8 41.5 all-gather.142
  1631.9 41.1 all-gather.148
  1696.5 41.5 all-gather.146
  1942.1 29.2 reduce-scatter.62
  1973.8 29.3 reduce-scatter.56
  2084.5 21.6 all-gather.108
  2210.0 29.2 reduce-scatter.68
  2288.7 29.3 reduce-scatter.70
  2459.4 29.3 reduce-scatter.74
  2538.5 29.3 reduce-scatter.76
  2709.2 29.2 reduce-scatter.80
  2833.4 21.6 all-gather.120
  2958.7 29.3 reduce-scatter.86
  3037.8 29.3 reduce-scatter.88
  3210.4 29.2 reduce-scatter.92
  3250.5 69.1 reduce-scatter.96
  3323.8 127.6 reduce-scatter.100
  3456.2 129.1 reduce-scatter.98
  3589.4 127.8 reduce-scatter.94
  (8 shorter events, 154.6 us)
where the time goes:
time: 3740 us; the launch traced here: 3720 us
  waiting for transfers between devices  1660 us (44%)
  matrix products  736 us (20%)
  blocking collectives  710 us (19%)
  other arithmetic  376 us (10%)
  local copies, waits for them, and re-layouts  202 us (5%)
    reduce_scatter x12, waiting for transfers between devices, project_rows(): lax.psum_scatter(partial_term(jnp.int32(0), row_share * lax.axis_size('co...  327 us
    reduce_scatter x12, waiting for transfers between devices, project_back(): lax.psum_scatter(partial_term(jnp.int32(0), row_share * lax.axis_size('co...  316 us
    all_gather x12, waiting for transfers between devices, gather_gradient(): return lax.all_gather(grad_rows, 'col', axis=1, tiled=True)  251 us
    all_gather x6, waiting for transfers between devices, per_device(): lax.all_gather(select(w_down, block_index), ('dp', 'row'), axis=0, tiled=...  235 us
    all_gather x6, blocking collectives, per_device(): lax.all_gather(select(w_qkv, block_index), ('dp', 'row'), axis=0, tiled=T...  226 us
    all_gather x6, blocking collectives, per_device(): lax.all_gather(select(w_out, block_index), ('dp', 'row'), axis=0, tiled=T...  191 us
    convert_element_type x6, other arithmetic, attend_backward(): score_grad = (attn_prob * (prob_grad - row_dot)).astype(jnp.bfloat16)  151 us
    dot_general x6, matrix products, attend_backward(): jnp.einsum('thd,khd->htk', attn_grad, value_rows, preferred_element_type=...  136 us
  transfers between devices with their start and end apart: 76, of which 62 were waited for; matrix products, arithmetic and copies ran while one was open for 10% of the time, Pallas kernels for 0%

commit v1 on v0

v1 whole, which is shorter than its diff:
```python
import functools

import jax
import jax.numpy as jnp
from jax import lax
from jax.experimental import pallas as pl
from jax.experimental.pallas import tpu as pltpu
from jax.sharding import Mesh
from jax.sharding import PartitionSpec as P

D = 768
HD = 64
LAYERS = 6
NB = 3
HEADS_COL = 3
PACK = 1792
NORM_EPS = 1e-05
MASK_FILL = -1000000000.0
GELU_COEF = 0.7978845608028654
F32 = jnp.float32
BF16 = jnp.bfloat16
MIB = 1024 * 1024


def nn(a, b):
    return lax.dot_general(a, b, (((1,), (0,)), ((), ())), preferred_element_type=F32)


def nt(a, b):
    return lax.dot_general(a, b, (((1,), (1,)), ((), ())), preferred_element_type=F32)


def tn(a, b):
    return lax.dot_general(a, b, (((0,), (0,)), ((), ())), preferred_element_type=F32)


def stats(hidden):
    mean = jnp.sum(hidden, axis=1, keepdims=True) * (1.0 / D)
    square = jnp.sum(hidden * hidden, axis=1, keepdims=True) * (1.0 / D)
    inverse = lax.rsqrt(square - mean * mean + NORM_EPS)
    return (hidden - mean) * inverse, inverse


def norm_back(grad, gain, centered, inverse):
    scaled = grad * gain
    first = jnp.sum(scaled, axis=1, keepdims=True) * (1.0 / D)
    second = jnp.sum(scaled * centered, axis=1, keepdims=True) * (1.0 / D)
    return inverse * (scaled - first - centered * second)


def colsum(value):
    return jnp.sum(value, axis=0, keepdims=True)


def to_row(column):
    rows = column.shape[0]
    return jnp.transpose(jnp.broadcast_to(column, (rows, 128)))[0:1, :]


class Row:
    def __init__(self, ref, layer):
        self.ref, self.base = ref, layer * 8

    def __getitem__(self, j):
        return self.ref[self.base + j]


def strip(kernel, layer, count, deps):
    def run(sc, *refs):
        kernel(Row(sc, layer), *refs[:count], *refs[count + deps :])

    return run


def params(limit, **more):
    return pltpu.CompilerParams(vmem_limit_bytes=limit * MIB, **more)


def cost(flops, nbytes, trans=0):
    return pl.CostEstimate(flops=int(flops), bytes_accessed=int(nbytes), transcendentals=int(trans))


def weight_copies(mine, other, my_x, wout, wud, sems):
    copies = []
    for s in range(4):
        src = (mine if s % 2 == 0 else other).at[my_x ^ (s // 2)]
        copies.append(
            (
                pltpu.make_async_copy(src.at[:, pl.ds(1536, 256)], wout.at[s], sems.at[0, s]),
                pltpu.make_async_copy(src.at[:, pl.ds(0, 1536)], wud.at[s], sems.at[1, s]),
            )
        )
    return copies


def start_weights(sc, packs, wout, wud, sems, out_first):
    def go(pair):
        copies = weight_copies(pair[0], pair[1], sc[4], wout, wud, sems)
        order = (0, 1) if out_first else (1, 0)
        for kind in order:
            for s in range(4):
                copies[s][kind].start()

    if len(packs) == 1:
        go(packs[0])
    else:
        for k, pair in enumerate(packs):
            pl.when(sc[1] == k)(functools.partial(go, pair))


def mlp_fwd_kernel(ranks, last, prompt, sc, *refs):
    h_ref, o0, o1, o2, o3, vec_ref, bup_ref, nvec_ref = refs[:8]
    packs = [(refs[8 + 2 * k], refs[9 + 2 * k]) for k in range(ranks)]
    outs = refs[8 + 2 * ranks :]
    h1_ref, u_hbm, m_hbm, h_out = outs[:4]
    wout, wud, sems, u_ref, m_ref, osem = outs[-6:]
    start_weights(sc, packs, wout, wud, sems, True)
    waits = weight_copies(packs[0][0], packs[0][1], sc[4], wout, wud, sems)
    total = h_ref[...] + vec_ref[0, 0:1, :]
    for s, o_ref in enumerate((o0, o1, o2, o3)):
        waits[s][0].wait()
        total = total + nt(o_ref[...], wout[s])
    h1_ref[...] = total
    centered, _ = stats(total)
    a2 = (centered * vec_ref[0, 2:3, :] + vec_ref[0, 3:4, :]).astype(BF16)
    h_out[...] = total + vec_ref[0, 1:2, :]
    stores = []
    for s in range(4):
        waits[s][1].wait()
        bias = bup_ref[0, pl.ds(sc[3] ^ s, 1), 0, :]
        up = nn(a2, wud[s, :, 0:768]) + bias
        u_ref[s] = up.astype(BF16)
        act = 0.5 * up * (1.0 + jnp.tanh(GELU_COEF * (up + 0.044715 * up * up * up)))
        act = act.astype(BF16)
        m_ref[s] = act
        stores.append(pltpu.make_async_copy(u_ref.at[s], u_hbm.at[s], osem.at[0, s]))
        stores.append(pltpu.make_async_copy(m_ref.at[s], m_hbm.at[s], osem.at[1, s]))
        stores[-2].start()
        stores[-1].start()
        h_out[...] += nt(act, wud[s, :, 768:1536])
    if last:
        y_refs = outs[4:8]
        send_features(sc, h_out, y_refs)
    else:
        a_ref, ap_ref = outs[4:6]
        centered, _ = stats(h_out[...])
        nxt = (centered * nvec_ref[0, 4:5, :] + nvec_ref[0, 5:6, :]).astype(BF16)
        a_ref[...] = nxt
        ap_ref[...] = nxt[:prompt]
    for copy in stores:
        copy.wait()


def send_features(sc, value, refs):
    width = refs[0].shape[1]
    for s, ref in enumerate(refs):
        for c in range(4):

            def put(ref=ref, c=c):
                ref[...] = value[:, c * width : (c + 1) * width].astype(BF16)

            pl.when((sc[3] ^ s) == c)(put)


def whole_spec(shape):
    return pl.BlockSpec(shape, lambda i, sc: (0,) * len(shape))


def vec_specs(layer):
    at = layer * 8
    return [
        pl.BlockSpec((1, 8, D), lambda i, sc: (sc[at], 0, 0)),
        pl.BlockSpec((1, 4, 1, D), lambda i, sc: (sc[at], 0, 0, 0)),
        pl.BlockSpec((1, 8, D), lambda i, sc: (sc[at + 2], 0, 0)),
    ]


WSCR = [
    pltpu.VMEM((4, D, 256), BF16),
    pltpu.VMEM((4, D, 1536), BF16),
    pltpu.SemaphoreType.DMA((2, 4)),
]
ANY = pl.BlockSpec(memory_space=pl.ANY)
HBM = pl.BlockSpec(memory_space=pltpu.HBM)


def mlp_fwd(layer, sc, hidden, o_parts, vecs, bup, packs, prompt, last, width, deps=()):
    tok = hidden.shape[0]
    shapes = [
        jax.ShapeDtypeStruct((tok, D), F32),
        jax.ShapeDtypeStruct((4, tok, D), BF16),
        jax.ShapeDtypeStruct((4, tok, D), BF16),
        jax.ShapeDtypeStruct((tok, D), F32),
    ]
    if last:
        shapes += [jax.ShapeDtypeStruct((tok, width), BF16)] * 4
    else:
        shapes += [jax.ShapeDtypeStruct((tok, D), BF16), jax.ShapeDtypeStruct((prompt, D), BF16)]
    out_specs = [whole_spec(v.shape) for v in shapes]
    out_specs[1] = out_specs[2] = HBM
    ins = [hidden, *o_parts, vecs, bup, vecs, *[w for pair in packs for w in pair]]
    kernel = functools.partial(mlp_fwd_kernel, len(packs), last, prompt)
    return pl.pallas_call(
        strip(kernel, layer, len(ins), len(deps)),
        grid_spec=pltpu.PrefetchScalarGridSpec(
            num_scalar_prefetch=1,
            grid=(1,),
            in_specs=[whole_spec((tok, D))]
            + [whole_spec((tok, 256))] * 4
            + vec_specs(layer)
            + [ANY] * (2 * len(packs) + len(deps)),
            out_specs=out_specs,
            scratch_shapes=WSCR
            + [
                pltpu.VMEM((4, tok, D), BF16),
                pltpu.VMEM((4, tok, D), BF16),
                pltpu.SemaphoreType.DMA((2, 4)),
            ],
        ),
        out_shape=shapes,
        compiler_params=params(44),
        cost_estimate=cost(2 * tok * D * 6912, 16e6, tok * 3072),
        name="mlp_fwd",
    )(sc, *ins, *deps)


def mlp_bwd_kernel(ranks, others, first, prompt, sc, *refs):
    if first:
        g_ref, refs = refs[0], refs[1:]
    else:
        nin = 4 + 2 * others
        g_ref, hn_ref, p0_ref, rx_ref = refs[:4]
        rest = refs[4:nin]
        refs = refs[nin:]
    h1_ref, u_hbm, vec_ref, nvec_ref = refs[:4]
    packs = [(refs[4 + 2 * k], refs[5 + 2 * k]) for k in range(ranks)]
    outs = refs[4 + 2 * ranks :]
    gm_ref, du_ref, a2_ref, g1_ref, go_ref, d0, d1, d2, d3, small_ref = outs[:10]
    wout, wud, sems, u_ref, usem = outs[10:]
    loads = [pltpu.make_async_copy(u_hbm.at[s], u_ref.at[s], usem.at[s]) for s in range(4)]
    start_weights(sc, packs, wout, wud, sems, False)
    for copy in loads:
        copy.start()
    waits = weight_copies(packs[0][0], packs[0][1], sc[4], wout, wud, sems)
    small_ref[...] = jnp.zeros_like(small_ref)
    if first:
        grad = g_ref[...]
    else:
        g1_ref[...] = p0_ref[...].astype(F32) + rx_ref[...].astype(F32)
        for ref in rest:
            g1_ref[0:prompt, :] += ref[...].astype(F32)
        da1 = g1_ref[...]
        centered, inverse = stats(hn_ref[...])
        small_ref[8:9, :] = colsum(da1 * centered)
        small_ref[9:10, :] = colsum(da1)
        grad = g_ref[...] + norm_back(da1, nvec_ref[0, 4:5, :], centered, inverse)
    gm = grad.astype(BF16)
    gm_ref[...] = gm
    small_ref[4:5, :] = colsum(gm.astype(F32))
    for s in range(4):
        waits[s][1].wait()
        dm = nn(gm, wud[s, :, 768:1536])
        loads[s].wait()
        up = u_ref[s].astype(F32)
        square = up * up
        tanh = jnp.tanh(GELU_COEF * up * (1.0 + 0.044715 * square))
        slope = 0.5 * (1.0 + tanh) + 0.5 * up * (1.0 - tanh * tanh) * (
            GELU_COEF * (1.0 + 3.0 * 0.044715 * square)
        )
        du = (dm * slope).astype(BF16)
        du_ref[s] = du
        small_ref[s : s + 1, :] = colsum(du.astype(F32))
        term = nt(du, wud[s, :, 0:768])
        if s == 0:
            g1_ref[...] = term
        else:
            g1_ref[...] += term
    da2 = g1_ref[...]
    centered, inverse = stats(h1_ref[...])
    gain = vec_ref[0, 2:3, :]
    a2_ref[...] = (centered * gain + vec_ref[0, 3:4, :]).astype(BF16)
    small_ref[6:7, :] = colsum(da2 * centered)
    small_ref[7:8, :] = colsum(da2)
    grad = grad + norm_back(da2, gain, centered, inverse)
    g1_ref[...] = grad
    go = grad.astype(BF16)
    go_ref[...] = go
    small_ref[5:6, :] = colsum(go.astype(F32))
    for s, ref in enumerate((d0, d1, d2, d3)):
        waits[s][0].wait()
        ref[...] = nn(go, wout[s]).astype(BF16)


def mlp_bwd(layer, sc, grad, back, h1, up, vecs, packs, prompt, deps=()):
    tok = grad.shape[0]
    first = back is None
    others = 0 if first else len(back[3])
    small = jax.ShapeDtypeStruct((tok, D), BF16)
    shapes = [
        small,
        jax.ShapeDtypeStruct((4, tok, D), BF16),
        small,
        jax.ShapeDtypeStruct((tok, D), F32),
        small,
    ]
    shapes += [jax.ShapeDtypeStruct((tok, 256), BF16)] * 4
    shapes += [jax.ShapeDtypeStruct((16, D), F32)]
    extra = [] if first else [back[0], back[1], back[2], *back[3]]
    specs = vec_specs(layer)
    ins = [grad, *extra, h1, up, vecs, vecs, *[w for pair in packs for w in pair]]
    kernel = functools.partial(mlp_bwd_kernel, len(packs), others // 2, first, prompt)
    return pl.pallas_call(
        strip(kernel, layer, len(ins), len(deps)),
        grid_spec=pltpu.PrefetchScalarGridSpec(
            num_scalar_prefetch=1,
            grid=(1,),
            in_specs=[whole_spec(v.shape) for v in [grad, *extra, h1]]
            + [HBM, specs[0], specs[2]]
            + [ANY] * (2 * len(packs) + len(deps)),
            out_specs=[whole_spec(s.shape) for s in shapes],
            scratch_shapes=WSCR + [pltpu.VMEM((4, tok, D), BF16), pltpu.SemaphoreType.DMA((4,))],
        ),
        out_shape=shapes,
        compiler_params=params(48),
        cost_estimate=cost(2 * tok * D * 6912, 16e6, tok * 3072),
        name="mlp_bwd",
    )(sc, *ins, *deps)


def attn_fwd_kernel(dims, sc, *refs):
    rows, piece, cpiece, chunk, cont = dims
    npc = 4 * rows
    own, oth = refs[:4], refs[4:npc]
    w_ref, b_ref, prow, pcol, crow, ccol, srow, scol = refs[npc : npc + 8]
    outs = refs[npc + 8 :]
    o_refs = outs[:4]
    q_ref, kv_ref, lse_ref, lsec_ref, m_s, l_s, acc_s = outs[4:]
    head = pl.program_id(0)
    base_b = chunk * rows
    base_c = 2 * chunk * rows
    weight = w_ref[0]
    bias = b_ref[0]
    for s in range(4):
        mixed = nn(own[s][...], weight) + bias
        low_q = (mixed[:, 0:128].astype(BF16).astype(F32) * 0.125).astype(BF16)
        low_kv = mixed[:, 128:256].astype(BF16)
        q_ref[0, s * piece : (s + 1) * piece, :] = low_q[0:piece]
        q_ref[0, chunk + s * piece : chunk + (s + 1) * piece, :] = low_q[piece : 2 * piece]
        q_ref[0, 2 * chunk + s * cpiece : 2 * chunk + (s + 1) * cpiece, :] = low_q[2 * piece :]
        kv_ref[0, s * piece : (s + 1) * piece, :] = low_kv[0:piece]
        kv_ref[0, base_b + s * piece : base_b + (s + 1) * piece, :] = low_kv[piece : 2 * piece]
        kv_ref[0, base_c + s * cpiece : base_c + (s + 1) * cpiece, :] = low_kv[2 * piece :]
    for t in range(1, rows):
        for s in range(4):
            low_kv = (nn(oth[(t - 1) * 4 + s][...], weight[:, 128:256]) + bias[:, 128:256]).astype(BF16)
            at = t * chunk + s * piece
            kv_ref[0, at : at + piece, :] = low_kv[0:piece]
            kv_ref[0, base_b + at : base_b + at + piece, :] = low_kv[piece : 2 * piece]
    lanes = lax.broadcasted_iota(jnp.int32, (1, 128), 1)
    upper = lanes >= 64
    sub = min(128, chunk)

    def begin(query, keys, mask):
        scores = nt(query, keys)
        if mask is not None:
            size = mask.shape[1]
            tail = jnp.where(mask, scores[:, -size:], MASK_FILL)
            if size == scores.shape[1]:
                scores = tail
            else:
                scores = jnp.concatenate([scores[:, :-size], tail], axis=1)
        top = jnp.max(scores, axis=1, keepdims=True)
        prob = jnp.exp(scores - top)
        return top, jnp.sum(prob, axis=1, keepdims=True), nn(prob.astype(BF16), keys)

    def put(out, row, size):
        low = jnp.where(upper, out, 0.0)

        def first_head():
            value = pltpu.roll(low, 64, 1).astype(BF16)
            store(value, row, size, 0, False)

        def second_head():
            store(low.astype(BF16), row, size, 0, True)

        def third_head():
            store(pltpu.roll(low, 64, 1).astype(BF16), row, size, 1, False)

        pl.when(head == 0)(first_head)
        pl.when(head == 1)(second_head)
        pl.when(head == 2)(third_head)

    def store(value, row, size, half, add):
        s, at = row
        lo = half * 128
        if add:
            o_refs[s][at : at + size, lo : lo + 128] = (
                o_refs[s][at : at + size, lo : lo + 128] + value
            )
        else:
            o_refs[s][at : at + size, lo : lo + 128] = value

    for i in range(chunk // sub):
        at = i * sub
        mask = prow[0:1, :] <= pcol[at : at + sub, :]
        top, total, acc = begin(q_ref[0, at : at + sub, :], kv_ref[0, 0:chunk, :], mask)
        m_s[at : at + sub, :], l_s[at : at + sub, :], acc_s[at : at + sub, :] = top, total, acc
        at_b = chunk + at
        top, total, acc = begin(
            q_ref[0, at_b : at_b + sub, :], kv_ref[0, 0 : base_b + chunk, :], mask
        )
        m_s[at_b : at_b + sub, :], l_s[at_b : at_b + sub, :] = top, total
        acc_s[at_b : at_b + sub, :] = acc
    my_row = sc[5]
    for t in range(1, rows):
        before = lax.rem(my_row + t, rows) < my_row
        q_at = jnp.where(before, 0, chunk)
        k_at = jnp.where(before, t * chunk, base_b + t * chunk)
        keys = kv_ref[0, pl.ds(pl.multiple_of(k_at, 128), chunk), :]
        for i in range(chunk // sub):
            at = pl.ds(pl.multiple_of(q_at + i * sub, 128), sub)
            scores = nt(q_ref[0, at, :], keys)
            old = m_s[at, :]
            top = jnp.maximum(old, jnp.max(scores, axis=1, keepdims=True))
            scale = jnp.exp(old - top)
            prob = jnp.exp(scores - top)
            m_s[at, :] = top
            l_s[at, :] = l_s[at, :] * scale + jnp.sum(prob, axis=1, keepdims=True)
            acc_s[at, :] = acc_s[at, :] * scale + nn(prob.astype(BF16), keys)
    for half in range(2):
        for s in range(4):
            at = half * chunk + s * piece
            total = l_s[at : at + piece, :]
            put(acc_s[at : at + piece, :] / total, (s, half * piece), piece)
        for i in range(chunk // sub):
            at = half * chunk + i * sub
            column = m_s[at : at + sub, :] + jnp.log(l_s[at : at + sub, :])
            lse_ref[0, half, :, i * sub : (i + 1) * sub] = to_row(column)
    mask = (crow[0:1, :] <= ccol[...]) & (srow[0:1, :] == scol[...])
    query = q_ref[0, 2 * chunk : 2 * chunk + cont, :]
    top, total, acc = begin(query, kv_ref[0], mask)
    out = acc / total
    for s in range(4):
        put(out[s * cpiece : (s + 1) * cpiece], (s, 2 * piece), cpiece)
    lsec_ref[0] = to_row(top + jnp.log(total))


def attn_inputs(pos):
    return [pl.BlockSpec(v.shape, lambda i, sc: (0, 0)) for v in pos]


def attn_fwd(layer, sc, own, oth, w_all, b_all, pos, dims, deps=()):
    rows, piece, cpiece, chunk, cont = dims
    tok = own[0].shape[0]
    nq, nk = 2 * chunk + cont, 2 * chunk * rows + cont
    shapes = [jax.ShapeDtypeStruct((tok, 256), BF16)] * 4 + [
        jax.ShapeDtypeStruct((3, nq, 128), BF16),
        jax.ShapeDtypeStruct((3, nk, 128), BF16),
        jax.ShapeDtypeStruct((3, 2, 1, chunk), F32),
        jax.ShapeDtypeStruct((3, 1, cont), F32),
    ]
    out_specs = [whole_spec((tok, 256))] * 4 + [
        pl.BlockSpec((1, nq, 128), lambda i, sc: (i, 0, 0)),
        pl.BlockSpec((1, nk, 128), lambda i, sc: (i, 0, 0)),
        pl.BlockSpec((1, 2, 1, chunk), lambda i, sc: (i, 0, 0, 0)),
        pl.BlockSpec((1, 1, cont), lambda i, sc: (i, 0, 0)),
    ]
    at = layer * 8
    count = len(own) + len(oth) + 2 + len(pos)
    return pl.pallas_call(
        strip(functools.partial(attn_fwd_kernel, dims), layer, count, len(deps)),
        grid_spec=pltpu.PrefetchScalarGridSpec(
            num_scalar_prefetch=1,
            grid=(3,),
            in_specs=[whole_spec(v.shape) for v in [*own, *oth]]
            + [
                pl.BlockSpec((1, D, 256), lambda i, sc: (sc[at], 0, i)),
                pl.BlockSpec((1, 1, 256), lambda i, sc: (sc[at], 0, i)),
            ]
            + attn_inputs(pos)
            + [ANY] * len(deps),
            out_specs=out_specs,
            scratch_shapes=[
                pltpu.VMEM((2 * chunk, 1), F32),
                pltpu.VMEM((2 * chunk, 1), F32),
                pltpu.VMEM((2 * chunk, 128), F32),
            ],
        ),
        out_shape=shapes,
        compiler_params=params(52),
        cost_estimate=cost(2 * nq * D * 768 * 2 + 8 * 3 * nq * nk * 64, 12e6, 3 * nq * nk),
        name="attn_fwd",
    )(sc, *own, *oth, w_all, b_all, *pos, *deps)


def attn_bwd_kernel(dims, sc, *refs):
    rows, piece, cpiece, chunk, cont = dims
    do_refs, o_refs = refs[:4], refs[4:8]
    q_ref, kv_ref, lse_ref, lsec_ref, w_ref = refs[8:13]
    prow, pcol, crow, ccol, srow, scol = refs[13:19]
    outs = refs[19:]
    npc = 4 * rows
    own_out, oth_out = outs[:4], outs[4:npc]
    dq_out, dkv_out, bias_out = outs[npc : npc + 3]
    do_s, drow, drowc, dq_s, dkv_s, da_s = outs[npc + 3 :]
    head = pl.program_id(0)
    base_b = chunk * rows
    base_c = 2 * chunk * rows
    tok = 2 * piece + cpiece
    upper = lax.broadcasted_iota(jnp.int32, (1, 128), 1) >= 64

    def take(ref):
        value = ref[...].astype(F32)
        left, right = value[:, 0:128], value[:, 128:256]
        pick = jnp.where(head == 2, pltpu.roll(right, 64, 1), left)
        pick = jnp.where(head == 0, pltpu.roll(left, 64, 1), pick)
        return jnp.where(upper, pick, 0.0)

    for s in range(4):
        dout = take(do_refs[s])
        low = dout.astype(BF16)
        do_s[s * piece : (s + 1) * piece, :] = low[0:piece]
        do_s[chunk + s * piece : chunk + (s + 1) * piece, :] = low[piece : 2 * piece]
        do_s[2 * chunk + s * cpiece : 2 * chunk + (s + 1) * cpiece, :] = low[2 * piece :]
        dot = dout * take(o_refs[s])
        dq_s[s * piece : (s + 1) * piece, :] = dot[0:piece]
        dq_s[chunk + s * piece : chunk + (s + 1) * piece, :] = dot[piece : 2 * piece]
        dq_s[2 * chunk + s * cpiece : 2 * chunk + (s + 1) * cpiece, :] = dot[2 * piece :]
    sub = min(128, chunk)
    for half in range(2):
        for i in range(chunk // sub):
            at = half * chunk + i * sub
            column = jnp.sum(dq_s[at : at + sub, :], axis=1, keepdims=True)
            drow[half, :, i * sub : (i + 1) * sub] = to_row(column)
    column = jnp.sum(dq_s[2 * chunk :, :], axis=1, keepdims=True)
    drowc[...] = to_row(column)
    dq_s[...] = jnp.zeros_like(dq_s)
    dkv_s[...] = jnp.zeros_like(dkv_s)

    def pair(q_at, k_at, lse, dot, mask):
        query = q_ref[0, q_at, :]
        keys = kv_ref[0, k_at, :]
        dout = do_s[q_at, :]
        prob = jnp.exp(nt(keys, query) - lse)
        if mask is not None:
            prob = jnp.where(mask, prob, 0.0)
        dprob = nt(keys, dout)
        dscore = (prob * (dprob - dot)).astype(BF16)
        dkv_s[k_at, :] += nn(prob.astype(BF16), dout) + nn(dscore, query)
        dq_s[q_at, :] += tn(dscore, keys)

    kb = min(256, chunk)
    at_a, at_b = pl.ds(0, chunk), pl.ds(chunk, chunk)
    lse_a, lse_b, dot_a, dot_b = lse_ref[0, 0], lse_ref[0, 1], drow[0], drow[1]
    for j in range(chunk // kb):
        mask = pcol[j * kb : (j + 1) * kb, :] <= prow[0:1, :]
        pair(at_a, pl.ds(j * kb, kb), lse_a, dot_a, mask)
        pair(at_b, pl.ds(base_b + j * kb, kb), lse_b, dot_b, mask)
    for j in range(base_b // kb):
        pair(at_b, pl.ds(j * kb, kb), lse_b, dot_b, None)
    my_row = sc[5]
    for t in range(1, rows):
        before = lax.rem(my_row + t, rows) < my_row
        which = jnp.where(before, 0, 1)
        q_at = pl.ds(pl.multiple_of(which * chunk, 128), chunk)
        k_base = jnp.where(before, t * chunk, base_b + t * chunk)
        for j in range(chunk // kb):
            k_at = pl.ds(pl.multiple_of(k_base + j * kb, 128), kb)
            pair(q_at, k_at, lse_ref[0, which], drow[which], None)
    at_c = pl.ds(2 * chunk, cont)
    for j in range(base_c // 512):
        pair(at_c, pl.ds(j * 512, 512), lsec_ref[0], drowc[...], None)
    mask = (ccol[...] <= crow[0:1, :]) & (scol[...] == srow[0:1, :])
    pair(at_c, pl.ds(base_c, cont), lsec_ref[0], drowc[...], mask)

    weight = w_ref[0]
    lower = jnp.logical_not(upper)
    dq_all = jnp.where(lower, dq_s[...] * 0.125, 0.0).astype(BF16)
    q_sum = colsum(dq_all.astype(F32))
    kv_sum = jnp.zeros((1, 128), F32)

    def gather3(value, where):
        return jnp.concatenate([value[a : a + n] for a, n in where], axis=0)

    def emit(slot, count, ref, term):
        at = pl.ds(slot, count)

        def set_first():
            da_s[at, :] = term

        def add_next():
            da_s[at, :] += term

        def finish():
            ref[...] = (da_s[at, :] + term).astype(BF16)

        pl.when(head == 0)(set_first)
        pl.when(head == 1)(add_next)
        pl.when(head == 2)(finish)

    for s in range(4):
        dq = gather3(
            dq_all,
            [(s * piece, piece), (chunk + s * piece, piece), (2 * chunk + s * cpiece, cpiece)],
        )
        dkv = jnp.concatenate(
            [
                dkv_s[s * piece : (s + 1) * piece, :],
                dkv_s[base_b + s * piece : base_b + (s + 1) * piece, :],
                dkv_s[base_c + s * cpiece : base_c + (s + 1) * cpiece, :],
            ],
            axis=0,
        ).astype(BF16)
        kv_sum = kv_sum + colsum(dkv.astype(F32))
        both = jnp.concatenate([dq, dkv], axis=1)
        dq_out[s, 0] = both
        emit(s * tok, tok, own_out[s], nt(both, weight))
    for t in range(1, rows):
        for s in range(4):
            at = t * chunk + s * piece
            dkv = jnp.concatenate(
                [dkv_s[at : at + piece, :], dkv_s[base_b + at : base_b + at + piece, :]], axis=0
            ).astype(BF16)
            kv_sum = kv_sum + colsum(dkv.astype(F32))
            k = (t - 1) * 4 + s
            dkv_out[k, 0] = dkv
            emit(4 * tok + k * 2 * piece, 2 * piece, oth_out[k], nt(dkv, weight[:, 128:256]))
    bias_out[0] = jnp.broadcast_to(jnp.concatenate([q_sum, kv_sum], axis=1), (8, 256))


def attn_bwd(layer, sc, do_parts, o_parts, q, kv, lse, lsec, w_all, pos, dims, deps=()):
    rows, piece, cpiece, chunk, cont = dims
    tok = 2 * piece + cpiece
    nq, nk = 2 * chunk + cont, 2 * chunk * rows + cont
    noth = 4 * (rows - 1)
    shapes = (
        [jax.ShapeDtypeStruct((tok, D), BF16)] * 4
        + [jax.ShapeDtypeStruct((2 * piece, D), BF16)] * noth
        + [
            jax.ShapeDtypeStruct((4, 3, tok, 256), BF16),
            jax.ShapeDtypeStruct((noth, 3, 2 * piece, 128), BF16),
            jax.ShapeDtypeStruct((3, 8, 256), F32),
        ]
    )
    out_specs = [whole_spec(s.shape) for s in shapes[: 4 + noth]] + [
        pl.BlockSpec((4, 1, tok, 256), lambda i, sc: (0, i, 0, 0)),
        pl.BlockSpec((noth, 1, 2 * piece, 128), lambda i, sc: (0, i, 0, 0)),
        pl.BlockSpec((1, 8, 256), lambda i, sc: (i, 0, 0)),
    ]
    at = layer * 8
    return pl.pallas_call(
        strip(functools.partial(attn_bwd_kernel, dims), layer, 13 + len(pos), len(deps)),
        grid_spec=pltpu.PrefetchScalarGridSpec(
            num_scalar_prefetch=1,
            grid=(3,),
            in_specs=[whole_spec((tok, 256))] * 8
            + [
                pl.BlockSpec((1, nq, 128), lambda i, sc: (i, 0, 0)),
                pl.BlockSpec((1, nk, 128), lambda i, sc: (i, 0, 0)),
                pl.BlockSpec((1, 2, 1, chunk), lambda i, sc: (i, 0, 0, 0)),
                pl.BlockSpec((1, 1, cont), lambda i, sc: (i, 0, 0)),
                pl.BlockSpec((1, D, 256), lambda i, sc: (sc[at], 0, i)),
            ]
            + attn_inputs(pos)
            + [ANY] * len(deps),
            out_specs=out_specs,
            scratch_shapes=[
                pltpu.VMEM((nq, 128), BF16),
                pltpu.VMEM((2, 1, chunk), F32),
                pltpu.VMEM((1, cont), F32),
                pltpu.VMEM((nq, 128), F32),
                pltpu.VMEM((nk, 128), F32),
                pltpu.VMEM((4 * tok + noth * 2 * piece, D), F32),
            ],
        ),
        out_shape=shapes,
        compiler_params=params(56),
        cost_estimate=cost(2 * nq * D * 768 * 2 + 20 * 3 * nq * nk * 64, 14e6, 3 * nq * nk),
        name="attn_bwd",
    )(sc, *do_parts, *o_parts, q, kv, lse, lsec, w_all, *pos, *deps)


def dw_qkv_kernel(rows, sc, *refs):
    npc = 4 * rows
    noth = npc - 4
    srcs, (dq_hbm, dkv_hbm) = refs[:npc], refs[npc : npc + 2]
    new_ref, token = refs[npc + 2 : npc + 4]
    own, oth, dq_s, dkv_s, asem, dsem = refs[npc + 4 :]
    token[...] = jnp.zeros_like(token)
    head = pl.program_id(0)

    def rows_of(k):
        dst = own.at[k] if k < 4 else oth.at[k - 4]
        return pltpu.make_async_copy(srcs[k], dst, asem.at[k])

    def grads_of(h):
        return [
            pltpu.make_async_copy(dq_hbm.at[:, h], dq_s.at[:, h], dsem.at[0, h]),
            pltpu.make_async_copy(dkv_hbm.at[:, h], dkv_s.at[:, h], dsem.at[1, h]),
        ]

    def begin():
        for copy in grads_of(0):
            copy.start()
        for k in range(npc):
            rows_of(k).start()
        for h in (1, 2):
            for copy in grads_of(h):
                copy.start()
        for k in range(npc):
            rows_of(k).wait()

    pl.when(head == 0)(begin)
    for copy in grads_of(head):
        copy.wait()
    total = tn(own[0], dq_s[0, head])
    for s in range(1, 4):
        total = total + tn(own[s], dq_s[s, head])
    right = tn(oth[0], dkv_s[0, head])
    for k in range(1, noth):
        right = right + tn(oth[k], dkv_s[k, head])
    new_ref[:, 0:128] = total[:, 0:128].astype(BF16)
    new_ref[:, 128:256] = (total[:, 128:256] + right).astype(BF16)


def dw_qkv(layer, sc, own, oth, dq, dkv, deps=()):
    rows = (4 + len(oth)) // 4
    tok, two = own[0].shape[0], oth[0].shape[0]
    noth = len(oth)
    ins = [*own, *oth, dq, dkv]
    return pl.pallas_call(
        strip(functools.partial(dw_qkv_kernel, rows), layer, len(ins), len(deps)),
        grid_spec=pltpu.PrefetchScalarGridSpec(
            num_scalar_prefetch=1,
            grid=(3,),
            in_specs=[HBM] * len(ins) + [ANY] * len(deps),
            out_specs=[pl.BlockSpec((D, 256), lambda i, sc: (0, i)), whole_spec((8, 128))],
            scratch_shapes=[
                pltpu.VMEM((4, tok, D), BF16),
                pltpu.VMEM((noth, two, D), BF16),
                pltpu.VMEM((4, 3, tok, 256), BF16),
                pltpu.VMEM((noth, 3, two, 128), BF16),
                pltpu.SemaphoreType.DMA((4 * rows,)),
                pltpu.SemaphoreType.DMA((2, 3)),
            ],
        ),
        out_shape=[
            jax.ShapeDtypeStruct((D, D), BF16),
            jax.ShapeDtypeStruct((8, 128), F32),
        ],
        compiler_params=params(40),
        cost_estimate=cost(2 * 3 * D * (4 * tok * 256 + noth * two * 128), 10e6),
        name="dw_qkv",
    )(sc, *ins, *deps)


def dw_terms(refs, scratch, act, sems, tile, first):
    a2_h, gm_h, go_h, du_ref, act_h, o0, o1, o2, o3 = refs
    a2, gm, go = scratch

    def load(k, src, dst):
        return pltpu.make_async_copy(src, dst, sems.at[k])

    loads = [load(0, a2_h, a2), load(1, gm_h, gm), load(2, go_h, go)]

    def tile_load(s):
        return load(3 + s, act_h.at[s], act.at[s])

    def begin():
        for copy in loads:
            copy.start()
        for s in range(4):
            tile_load(s).start()
        for copy in loads:
            copy.wait()

    pl.when(first)(begin)
    pl.when(tile == 0)(lambda: tile_load(0).wait())
    for s in range(1, 4):
        pl.when(tile == s)(lambda s=s: tile_load(s).wait())

    def run(put):
        for j in range(3):
            put(j * 256, tn(a2[...], du_ref[0, :, j * 256 : (j + 1) * 256]))
            put(768 + j * 256, tn(gm[...], act[tile, :, j * 256 : (j + 1) * 256]))
        for s, ref in enumerate((o0, o1, o2, o3)):
            pl.when(tile == s)(lambda ref=ref: put(1536, tn(go[...], ref[...])))

    return run


def dw_mlp_kernel(sc, *refs):
    old_ref, new_ref, token = refs[9:12]
    a2, gm, go, act, sems = refs[12:]
    token[...] = jnp.zeros_like(token)
    tile = pl.program_id(0)
    keep = sc[6] == 0
    run = dw_terms(refs[:9], (a2, gm, go), act, sems, tile, tile == 0)

    def put(lo, value):
        size = value.shape[1]
        old = old_ref[0, 0, :, lo : lo + size].astype(F32)
        new_ref[0, 0, :, lo : lo + size] = (value + jnp.where(keep, old, 0.0)).astype(BF16)

    run(put)


def dw_specs(tok):
    return (
        [HBM] * 3
        + [pl.BlockSpec((1, tok, D), lambda i, sc: (i, 0, 0)), HBM]
        + [whole_spec((tok, 256))] * 4
    )


def dw_scratch(tok):
    return [pltpu.VMEM((tok, D), BF16)] * 3 + [
        pltpu.VMEM((4, tok, D), BF16),
        pltpu.SemaphoreType.DMA((7,)),
    ]


def dw_mlp(layer, sc, a2, gm, go, du, act, o_parts, acc, deps=()):
    tok = a2.shape[0]
    at = layer * 8
    acc_spec = pl.BlockSpec((1, 1, D, PACK), lambda i, sc: (sc[at + 1], i, 0, 0))
    ins = [a2, gm, go, du, act, *o_parts, acc]
    return pl.pallas_call(
        strip(dw_mlp_kernel, layer, len(ins), len(deps)),
        grid_spec=pltpu.PrefetchScalarGridSpec(
            num_scalar_prefetch=1,
            grid=(4,),
            in_specs=dw_specs(tok) + [acc_spec] + [ANY] * len(deps),
            out_specs=[acc_spec, whole_spec((8, 128))],
            scratch_shapes=dw_scratch(tok),
        ),
        out_shape=[jax.ShapeDtypeStruct(acc.shape, acc.dtype), jax.ShapeDtypeStruct((8, 128), F32)],
        input_output_aliases={len(ins): 0},
        compiler_params=params(40),
        cost_estimate=cost(2 * tok * D * 4 * PACK, 30e6),
        name="dw_mlp",
    )(sc, *ins, *deps)


def dw_last_kernel(rank, sc, *refs):
    send_ref, keep_ref, acc, token = refs[10:14]
    a2, gm, go, act, sems, done, other, dsem, osem = refs[14:]
    token[...] = jnp.zeros_like(token)
    step = pl.program_id(0)
    tile = last_tile(step)
    same = sc[1] == rank
    keep = sc[6] == 0
    used = jnp.logical_or(jnp.logical_not(same), keep)

    def load(i):
        return pltpu.make_async_copy(acc.at[rank, last_tile(i)], done.at[i % 2], dsem.at[i % 2])

    def start_two():
        load(0).start()
        load(1).start()

    pl.when(step == 0)(start_two)
    run = dw_terms(refs[:9], (a2, gm, go), act, sems, tile, step == 0)
    load(step).wait()

    def fetch_other():
        copy = pltpu.make_async_copy(acc.at[sc[1], tile], other, osem)
        copy.start()
        copy.wait()

    pl.when(jnp.logical_not(same))(fetch_other)

    def put(lo, value):
        size = value.shape[1]
        cols = slice(lo, lo + size)
        old = jnp.where(used, done[step % 2, :, cols].astype(F32), 0.0)
        total = (old + jnp.where(same, value, 0.0)).astype(BF16)

        def to_send():
            send_ref[0, :, cols] = total

        def to_keep():
            keep_ref[0, :, cols] = total

        pl.when(step < 2)(to_send)
        pl.when(step >= 2)(to_keep)

        def add_other():
            before = jnp.where(keep, other[:, cols].astype(F32), 0.0)
            other[:, cols] = (value + before).astype(BF16)

        pl.when(jnp.logical_not(same))(add_other)

    run(put)

    def store_other():
        copy = pltpu.make_async_copy(other, acc.at[sc[1], tile], osem)
        copy.start()
        copy.wait()

    pl.when(jnp.logical_not(same))(store_other)
    pl.when(step < 2)(lambda: load(step + 2).start())


def last_tile(step):
    return jnp.where(step < 2, 2 * step + 1, 2 * step - 4)


def dw_last(layer, sc, a2, gm, go, du, act, o_parts, acc, deps=()):
    tok = a2.shape[0]
    ins = [a2, gm, go, du, act, *o_parts, acc]
    specs = dw_specs(tok)
    specs[3] = pl.BlockSpec((1, tok, D), lambda i, sc: (last_tile(i), 0, 0))
    two = jax.ShapeDtypeStruct((2, D, PACK), BF16)
    return pl.pallas_call(
        strip(functools.partial(dw_last_kernel, layer), layer, len(ins), len(deps)),
        grid_spec=pltpu.PrefetchScalarGridSpec(
            num_scalar_prefetch=1,
            grid=(4,),
            in_specs=specs + [HBM] + [ANY] * len(deps),
            out_specs=[
                pl.BlockSpec((1, D, PACK), lambda i, sc: (jnp.minimum(i, 1), 0, 0)),
                pl.BlockSpec((1, D, PACK), lambda i, sc: (jnp.maximum(i - 2, 0), 0, 0)),
                HBM,
                whole_spec((8, 128)),
            ],
            scratch_shapes=dw_scratch(tok)
            + [
                pltpu.VMEM((2, D, PACK), BF16),
                pltpu.VMEM((D, PACK), BF16),
                pltpu.SemaphoreType.DMA((2,)),
                pltpu.SemaphoreType.DMA(()),
            ],
        ),
        out_shape=[two, two, jax.ShapeDtypeStruct(acc.shape, acc.dtype), jax.ShapeDtypeStruct((8, 128), F32)],
        input_output_aliases={len(ins): 2},
        compiler_params=params(52),
        cost_estimate=cost(2 * tok * D * 4 * PACK, 30e6),
        name="dw_last",
    )(sc, *ins, *deps)


def blank(shape, dtype):
    def body(out):
        del out

    return pl.pallas_call(
        body,
        out_shape=jax.ShapeDtypeStruct(shape, dtype),
        out_specs=pl.BlockSpec(memory_space=pl.ANY),
        name="blank",
    )()


SWAP = [(0, 1), (1, 0)]


def swap_core(value):
    return lax.ppermute(value, "core", SWAP)


def swap_x(value):
    return lax.ppermute(value, "x", SWAP)


def shift_row(value, t):
    rows = lax.axis_size("row")
    return lax.ppermute(value, "row", [(i, (i - t) % rows) for i in range(rows)])


def shift_row_x(value, t):
    rows = lax.axis_size("row")
    pairs = [(i * 2 + j, ((i - t) % rows) * 2 + (1 - j)) for i in range(rows) for j in range(2)]
    return lax.ppermute(value, ("row", "x"), pairs)


def spread(low, low_prompt):
    rows = lax.axis_size("row")
    from_x = swap_x(low)
    far = []
    for t in range(1, rows):
        far += [shift_row(low_prompt, t), shift_row_x(low_prompt, t)]
    own = [low, swap_core(low), from_x, swap_core(from_x)]
    oth = []
    for t in range(1, rows):
        near, diag = far[2 * t - 2], far[2 * t - 1]
        oth += [near, swap_core(near), diag, swap_core(diag)]
    return own, oth


def exchange_heads(parts):
    flip = {1: [1, 0, 3, 2], 2: [2, 3, 0, 1], 3: [3, 2, 1, 0]}
    out = [parts[0]]
    for s in (1, 2, 3):
        pairs = [(c, flip[s][c]) for c in range(4)]
        out.append(lax.ppermute(parts[s], ("x", "core"), pairs))
    return out


def add_low(a, b):
    return (a.astype(F32) + b.astype(F32)).astype(BF16)


def add_kernel(refs_in, refs_out):
    for k, out in enumerate(refs_out):
        out[...] = add_low(refs_in[2 * k][...], refs_in[2 * k + 1][...])


def add_pairs(pairs):
    flat = [v for pair in pairs for v in pair]
    count = len(flat)
    return pl.pallas_call(
        lambda *refs: add_kernel(refs[:count], refs[count:]),
        out_shape=[jax.ShapeDtypeStruct(a.shape, a.dtype) for a, _ in pairs],
        compiler_params=params(24),
        cost_estimate=cost(1e6, 4e6),
        name="add_pairs",
    )(*flat)


def collect(own, oth):
    rows = lax.axis_size("row")
    pieces = [*own, *oth]
    pairs = [(pieces[k], swap_core(pieces[k + 1])) for k in range(0, len(pieces), 2)]
    sums = add_pairs(pairs)
    got = swap_x(sums[1])
    rest = []
    for t in range(1, rows):
        rest += [shift_row(sums[2 * t], -t), shift_row_x(sums[2 * t + 1], -t)]
    return sums[0], got, rest


def pick_kernel(sc_at, sc, src, *rest):
    out, sem = rest[-2:]
    copy = pltpu.make_async_copy(src.at[sc[sc_at]], out, sem)
    copy.start()
    copy.wait()


def pick(src, sc, at, deps=()):
    return pl.pallas_call(
        functools.partial(pick_kernel, at),
        grid_spec=pltpu.PrefetchScalarGridSpec(
            num_scalar_prefetch=1,
            grid=(1,),
            in_specs=[ANY] * (1 + len(deps)),
            out_specs=ANY,
            scratch_shapes=[pltpu.SemaphoreType.DMA(())],
        ),
        out_shape=jax.ShapeDtypeStruct(src.shape[1:], src.dtype),
        name="pick",
    )(sc, src, *deps)


def zig(j, rows):
    return j if j < rows else 2 * rows - 1 - j


def split_kernel(piece, cpiece, sc, even, odd, cont, *outs):
    for s, out in enumerate(outs):
        place = sc[3] ^ s
        at = pl.ds(pl.multiple_of(place * piece, piece), piece)

        def fill(first, second, out=out, at=at):
            out[0:piece, :] = first[at, :]
            out[piece : 2 * piece, :] = second[at, :]

        pl.when(sc[7] == 0)(functools.partial(fill, even, odd))
        pl.when(sc[7] == 1)(functools.partial(fill, odd, even))
        out[2 * piece :, :] = cont[pl.ds(pl.multiple_of(place * cpiece, cpiece), cpiece), :]


def merge_kernel(piece, cpiece, sc, p0, p1, p2, p3, even, odd, cont):
    for s, part in enumerate((p0, p1, p2, p3)):
        place = sc[3] ^ s
        at = pl.ds(pl.multiple_of(place * piece, piece), piece)

        def fill(first, second, part=part, at=at):
            first[at, :] = part[0:piece, :]
            second[at, :] = part[piece : 2 * piece, :]

        pl.when(sc[7] == 0)(functools.partial(fill, even, odd))
        pl.when(sc[7] == 1)(functools.partial(fill, odd, even))
        cont[pl.ds(pl.multiple_of(place * cpiece, cpiece), cpiece), :] = part[2 * piece :, :]


def join_kernel(prompt, normed, sc, p0, p1, p2, p3, vec_ref, h_ref, *outs):
    width = p0.shape[1]
    for s, part in enumerate((p0, p1, p2, p3)):
        value = part[...].astype(F32)
        for c in range(4):

            def put(value=value, c=c):
                h_ref[:, c * width : (c + 1) * width] = value

            pl.when((sc[3] ^ s) == c)(put)
    if normed:
        a_ref, ap_ref = outs
        centered, _ = stats(h_ref[...])
        low = (centered * vec_ref[0, 4:5, :] + vec_ref[0, 5:6, :]).astype(BF16)
        a_ref[...] = low
        ap_ref[...] = low[:prompt]


def simple_call(kernel, sc, ins, shapes, specs=None, name="small"):
    return pl.pallas_call(
        lambda sc_ref, *refs: kernel(Row(sc_ref, 0), *refs),
        grid_spec=pltpu.PrefetchScalarGridSpec(
            num_scalar_prefetch=1,
            grid=(1,),
            in_specs=specs or [whole_spec(v.shape) for v in ins],
            out_specs=[whole_spec(v.shape) for v in shapes],
        ),
        out_shape=shapes,
        compiler_params=params(24),
        cost_estimate=cost(1e6, 3e6),
        name=name,
    )(sc, *ins)


def enter(prompt, cont, sc, vecs, normed):
    rows = lax.axis_size("row")
    half, width = prompt.shape[0] // 2, prompt.shape[1]
    piece, cpiece = half // 4, cont.shape[0] // 4
    tok = 2 * piece + cpiece
    even = prompt[:half]
    odd = prompt[half:]
    if rows > 2:
        even = lax.ppermute(even, "row", [(i, zig(2 * i, rows)) for i in range(rows)])
    odd = lax.ppermute(odd, "row", [(i, zig(2 * i + 1, rows)) for i in range(rows)])
    part = jax.ShapeDtypeStruct((tok, width), BF16)
    parts = simple_call(
        functools.partial(split_kernel, piece, cpiece), sc, [even, odd, cont], [part] * 4, name="split"
    )
    parts = exchange_heads(parts)
    shapes = [jax.ShapeDtypeStruct((tok, D), F32)]
    if normed:
        shapes += [jax.ShapeDtypeStruct((tok, D), BF16), jax.ShapeDtypeStruct((2 * piece, D), BF16)]
    specs = [whole_spec((tok, width))] * 4 + [pl.BlockSpec((1, 8, D), lambda i, sc: (sc[0], 0, 0))]
    return simple_call(
        functools.partial(join_kernel, 2 * piece, normed), sc, [*parts, vecs], shapes, specs, "join"
    )


def leave(parts, sc, prompt_rows):
    rows = lax.axis_size("row")
    parts = exchange_heads(parts)
    width = parts[0].shape[1]
    half = prompt_rows // 2
    piece = half // 4
    cpiece = parts[0].shape[0] - 2 * piece
    shapes = [jax.ShapeDtypeStruct((n, width), BF16) for n in (half, half, 4 * cpiece)]
    even, odd, cont = simple_call(
        functools.partial(merge_kernel, piece, cpiece), sc, parts, shapes, name="merge"
    )
    if rows > 2:
        even = lax.ppermute(even, "row", [(zig(2 * i, rows), i) for i in range(rows)])
    odd = lax.ppermute(odd, "row", [(zig(2 * i + 1, rows), i) for i in range(rows)])
    return jnp.concatenate([even, odd], axis=0)[None], cont[None]


def final_kernel(prompt, others, sc, *refs):
    g_ref, h_ref, p0_ref, rx_ref = refs[:4]
    rest = refs[4 : 4 + others]
    vec_ref = refs[4 + others]
    outs, small, da_ref, out_ref = refs[5 + others : 9 + others], refs[9 + others], refs[10 + others], refs[11 + others]
    da_ref[...] = p0_ref[...].astype(F32) + rx_ref[...].astype(F32)
    for ref in rest:
        da_ref[0:prompt, :] += ref[...].astype(F32)
    da1 = da_ref[...]
    centered, inverse = stats(h_ref[...])
    small[0:1, :] = colsum(da1 * centered)
    small[1:2, :] = colsum(da1)
    out_ref[...] = g_ref[...] + norm_back(da1, vec_ref[0, 4:5, :], centered, inverse)
    send_features(sc, out_ref, outs)


def final_norm(sc, grad, back, vecs, prompt, width):
    tok = grad.shape[0]
    h_in, base, got, rest = back
    ins = [grad, h_in, base, got, *rest, vecs]
    shapes = [jax.ShapeDtypeStruct((tok, width), BF16)] * 4 + [
        jax.ShapeDtypeStruct((8, D), F32),
        jax.ShapeDtypeStruct((tok, D), F32),
        jax.ShapeDtypeStruct((tok, D), F32),
    ]
    specs = [whole_spec(v.shape) for v in ins[:-1]] + [
        pl.BlockSpec((1, 8, D), lambda i, sc: (sc[0], 0, 0))
    ]
    return simple_call(
        functools.partial(final_kernel, prompt, len(rest)), sc, ins, shapes, specs, "final_norm"
    )


class Reduce:

    def __init__(self, value, plan, out):
        self.value, self.plan, self.out = value, list(plan), out
        self.pending = None
        self.send()

    def halves(self, axis, bit):
        where = {"dp": 0, "row": 1}[axis]
        size = self.value.shape[where]
        step = size // 2
        shape = self.value.shape
        split = self.value.reshape(shape[:where] + (2, step) + shape[where + 1 :])
        mine = (lax.axis_index(axis) // bit) % 2
        take = functools.partial(lax.dynamic_index_in_dim, split, axis=where, keepdims=False)
        return take(mine), take(1 - mine)

    def send(self):
        if not self.plan:
            return
        axis, bit = self.plan.pop(0)
        count = lax.axis_size(axis)
        keep, send = self.halves(axis, bit)
        got = lax.ppermute(send, axis, [(i, i ^ bit) for i in range(count)])
        self.pending = (keep, got)

    def step(self):
        if self.pending is None:
            return self.value
        keep, got = self.pending
        self.pending = None
        total = keep.astype(F32) + got.astype(F32)
        self.value = total if not self.plan else total.astype(BF16)
        self.send()
        return self.value

    def finish(self):
        while self.pending is not None:
            self.step()
        return self.value[0, 0].astype(F32)


def bits_of(axis):
    count = lax.axis_size(axis)
    bits, bit = [], count // 2
    while bit:
        bits.append((axis, bit))
        bit //= 2
    return bits


def reorder(value):
    shape = value.shape
    value = value.reshape((2, 2) + shape[1:])
    value = jnp.where(lax.axis_index("core") == 1, value[:, ::-1], value)
    value = jnp.where(lax.axis_index("x") == 1, value[::-1], value)
    return value.reshape(shape)


def sum_small(value):
    rows, dps = lax.axis_size("row"), lax.axis_size("dp")
    x, core = lax.axis_index("x"), lax.axis_index("core")
    value = value.reshape(2, 2, -1)
    take = lax.dynamic_index_in_dim
    send = take(value, 1 - core, 1, keepdims=False)
    value = take(value, core, 1, keepdims=False) + swap_core(send)
    send = take(value, 1 - x, 0, keepdims=False)
    value = take(value, x, 0, keepdims=False) + swap_x(send)
    for axis, count in (("row", rows), ("dp", dps)):
        bit = 1
        while bit < count:
            value = value + lax.ppermute(value, axis, [(i, i ^ bit) for i in range(count)])
            bit *= 2
    return value


def per_device(
    x_prompt,
    x_cont,
    seg_ids,
    layer_map,
    w_qkv,
    bias_qv,
    w_out,
    b_out,
    w_up,
    b_up,
    w_down,
    b_down,
    ln1_gain,
    ln1_bias,
    ln2_gain,
    ln2_bias,
    cot_prompt,
    cot_cont,
):
    rows, dps = lax.axis_size("row"), lax.axis_size("dp")
    prompt_row, cont = x_prompt.shape[1], x_cont.shape[1]
    width = x_prompt.shape[2]
    chunk = prompt_row // 2
    piece, cpiece = chunk // 4, cont // 4
    prompt = 2 * piece
    dims = (rows, piece, cpiece, chunk, cont)
    my_row, my_x = lax.axis_index("row"), lax.axis_index("x")
    my_col = my_x * 2 + lax.axis_index("core")

    layer_map = layer_map.astype(jnp.int32)
    places = jnp.arange(LAYERS, dtype=jnp.int32)
    first_use = [jnp.min(jnp.where(layer_map == b, places, 99)) for b in range(NB)]
    rank_of = [sum((first_use[o] < first_use[b]).astype(jnp.int32) for o in range(NB) if o != b) for b in range(NB)]
    block_at = [sum(b * (rank_of[b] == k).astype(jnp.int32) for b in range(NB)) for k in range(NB)]
    block_of = [layer_map[i] for i in range(LAYERS)]
    rank_layer = [
        sum(rank_of[b] * (block_of[i] == b).astype(jnp.int32) for b in range(NB)) for i in range(LAYERS)
    ]

    def scalars(layer):
        fresh = jnp.int32(1)
        for later in range(layer + 1, LAYERS):
            fresh = fresh * (rank_layer[later] != rank_layer[layer]).astype(jnp.int32)
        after = min(layer + 1, LAYERS - 1)
        return [block_of[layer], rank_layer[layer], block_of[after], my_col, my_x, my_row, fresh, my_row % 2]

    sc = jnp.stack([v for i in range(LAYERS) for v in scalars(i)] + block_at).astype(jnp.int32)

    heads = w_qkv.reshape(NB, -1, 3, HEADS_COL, HD)
    zero = jnp.zeros_like(heads[:, :, 0])
    packed = jnp.stack([heads[:, :, 0], zero, heads[:, :, 1], heads[:, :, 2]], axis=3)
    packed = packed.reshape(NB, -1, D)
    wqkv_all = lax.all_gather(packed, ("dp", "row"), axis=1, tiled=True)
    pair = bias_qv.astype(F32).reshape(NB, 2, HEADS_COL, HD)
    none = jnp.zeros((NB, HEADS_COL, 2, HD), F32)
    bqkv = jnp.concatenate([pair[:, 0][:, :, None], none, pair[:, 1][:, :, None]], axis=2).reshape(NB, 1, D)

    def flat(value):
        return value.reshape(NB, -1)

    narrow = jnp.concatenate(
        [flat(v) for v in (b_out, b_down, ln2_gain, ln2_bias, ln1_gain, ln1_bias, b_up)], axis=1
    )
    narrow = jnp.stack(exchange_heads([narrow] * 4))
    narrow = reorder(narrow.astype(F32))
    vecs = narrow[:, :, : 6 * width].reshape(4, NB, 6, width).transpose(1, 2, 0, 3).reshape(NB, 6, D)
    vecs = jnp.concatenate([vecs, jnp.zeros((NB, 2, D), F32)], axis=1)
    bup = narrow[:, :, 6 * width :].transpose(1, 0, 2).reshape(NB, 4, 1, D)

    pack_local = jnp.concatenate(
        [w_up, w_down, w_out, jnp.zeros(w_out.shape[:2] + (64,), BF16)], axis=2
    )

    def gather_pack(k, deps):
        local = pick(pack_local, sc, LAYERS * 8 + k, deps)
        mine = lax.all_gather(local, ("x", "dp", "row"), axis=0, tiled=True).reshape(2, D, PACK)
        return mine, swap_core(mine)

    def places_of(size):
        index = jnp.arange(4 * size, dtype=jnp.int32)
        return size * ((index // size) ^ my_col) + index % size

    ppos, cpos = places_of(piece), places_of(cpiece)
    seg = reorder(seg_ids[0].astype(jnp.int32).reshape(4, cpiece)).reshape(cont)
    pos = [ppos[None], ppos[:, None], cpos[None], cpos[:, None], seg[None], seg[:, None]]

    hidden, low, low_prompt = enter(x_prompt[0], x_cont[0], sc, vecs, True)
    packs = [gather_pack(0, [wqkv_all])]
    saved = []
    for i in range(LAYERS):
        last = i == LAYERS - 1
        own, oth = spread(low, low_prompt)
        res = attn_fwd(i, sc, own, oth, wqkv_all, bqkv, pos, dims)
        o_send, (q, kv, lse, lsec) = res[:4], res[4:]
        if i + 1 < NB:
            packs.append(gather_pack(i + 1, [lsec]))
        o_got = exchange_heads(o_send)
        avail = packs[: min(i, NB - 1) + 1]
        res = mlp_fwd(i, sc, hidden, o_got, vecs, bup, avail, prompt, last, width)
        saved.append((hidden, own, oth, o_send, q, kv, lse, lsec, o_got, res[0], res[1], res[2]))
        hidden = res[3]
        if not last:
            low, low_prompt = res[4], res[5]
    y_prompt, y_cont = leave(res[4:8], sc, prompt_row)

    grad = enter(cot_prompt[0], cot_cont[0], sc, vecs, False)[0]
    acc_pack = blank((NB, 4, D, PACK), BF16)
    back = None
    small = [None] * LAYERS
    small_qkv = [None] * LAYERS
    sums = []
    done_pack = [None] * NB
    done_qkv = [None] * NB
    dws = [None] * LAYERS
    steps = bits_of("row") + bits_of("dp")
    fence = []
    sent = None
    for i in reversed(range(LAYERS)):
        h_in, own, oth, o_send, q, kv, lse, lsec, o_got, h1, up, act = saved[i]
        res = mlp_bwd(i, sc, grad, back, h1, up, vecs, packs, prompt, fence)
        gm, du, a2, grad, go = res[:5]
        do_send, small[i] = res[5:9], res[9]
        do_got = exchange_heads(do_send)
        if i < NB:
            send, keep, acc_pack, token = dw_last(i, sc, a2, gm, go, du, act, o_got, acc_pack)
            sent = (keep, swap_core(send))
        else:
            acc_pack, token = dw_mlp(i, sc, a2, gm, go, du, act, o_got, acc_pack)
        res = attn_bwd(i, sc, do_got, o_send, q, kv, lse, lsec, wqkv_all, pos, dims, [token])
        da_own, da_oth = res[:4], res[4 : 4 * rows]
        dq, dkv, small_qkv[i] = res[4 * rows :]
        base, got, rest = collect(da_own, da_oth)
        dws[i], token = dw_qkv(i, sc, own, oth, dq, dkv)
        fence = [token]
        for part in sums:
            fence.append(part.step())
        if i < NB:
            keep, recv = sent
            far = add_low(keep[1], recv[1])
            near = (keep[0], recv[0], swap_x(far))
            fence.append(far)
            value = sum(
                jnp.where(rank_layer[l] == i, dws[l].astype(F32), 0.0) for l in range(i, LAYERS)
            )
            shape = (dps, rows, D // (dps * rows), D)
            done_qkv[i] = Reduce(value.astype(BF16).reshape(shape), steps, None)
            sums.append(done_qkv[i])
            done_pack[i] = near
        back = (h_in, base, got, rest)
        if i + 1 < NB:
            near = done_pack[i + 1]
            value = (near[0].astype(F32) + near[1].astype(F32) + near[2].astype(F32)).astype(BF16)
            shape = (dps, rows, D // (dps * rows), PACK)
            done_pack[i + 1] = Reduce(value.reshape(shape), steps, None)
            sums.append(done_pack[i + 1])
            fence.append(value)

    res = final_norm(sc, grad, back, vecs, prompt, width)
    dx_prompt, dx_cont = leave(res[:4], sc, prompt_row)
    last_gain, last_shift = res[4][0:1], res[4][1:2]
    near = done_pack[0]
    value = (near[0].astype(F32) + near[1].astype(F32) + near[2].astype(F32)).astype(BF16)
    done_pack[0] = Reduce(value.reshape(dps, rows, D // (dps * rows), PACK), steps, None)
    done_pack = [part.finish() for part in done_pack]
    done_qkv = [part.finish() for part in done_qkv]

    pieces = []
    for i in range(LAYERS):
        ups = reorder(small[i][0:4])
        nxt = small[i - 1] if i > 0 else None
        gain1 = last_gain if i == 0 else nxt[8:9]
        shift1 = last_shift if i == 0 else nxt[9:10]
        vec6 = jnp.concatenate([small[i][5:6], small[i][4:5], small[i][6:8], gain1, shift1], axis=0)
        vec6 = vec6.reshape(6, 4, width).transpose(1, 0, 2).reshape(4, 6 * width)
        sums = small_qkv[i][:, 0, :].reshape(HEADS_COL, 4, HD)
        mine = jnp.concatenate([sums[:, 0].reshape(-1), sums[:, 3].reshape(-1)])
        spot = (jnp.arange(4) == my_col)[:, None]
        qv = jnp.where(spot, mine[None], 0.0)
        pieces.append(jnp.concatenate([vec6, ups, qv], axis=1))
    stacked = jnp.stack(pieces)
    by_block = jnp.stack(
        [
            sum(jnp.where(block_of[i] == b, stacked[i], 0.0) for i in range(LAYERS))
            for b in range(NB)
        ],
        axis=1,
    )
    mine = sum_small(by_block).reshape(NB, -1)
    g_vec = mine[:, : 6 * width].reshape(NB, 6, width)
    g_bup = mine[:, 6 * width : 6 * width + D]
    g_qv = mine[:, 6 * width + D :].reshape(NB, 2, width)

    def by_rank(parts):
        return jnp.stack(
            [sum(jnp.where(rank_of[b] == k, parts[k], 0.0) for k in range(NB)) for b in range(NB)]
        )

    g_pack = by_rank(done_pack)
    g_heads = by_rank(done_qkv).reshape(NB, -1, HEADS_COL, 4, HD)
    g_qkv = jnp.stack([g_heads[:, :, :, j].reshape(NB, -1, width) for j in (0, 2, 3)], axis=2)
    return (
        y_prompt,
        y_cont,
        dx_prompt,
        dx_cont,
        g_qkv,
        g_qv,
        g_pack[:, :, 1536 : 1536 + width],
        g_vec[:, 0],
        g_pack[:, :, 0:768],
        g_bup,
        g_pack[:, :, 768:1536],
        g_vec[:, 1],
        g_vec[:, 4],
        g_vec[:, 5],
        g_vec[:, 2],
        g_vec[:, 3],
    )


def solution(mesh):
    dps, rows = mesh.shape["dp"], mesh.shape["row"]
    fine = Mesh(mesh.devices.reshape(dps, rows, 2, 2), ("dp", "row", "x", "core"))
    col = ("x", "core")
    both = ("dp", "row")
    tokens = P("dp", "row", col)
    narrow = P(None, col)
    wide = P(None, both, col)
    in_specs = (
        tokens,
        tokens,
        P("dp", "row"),
        P(),
        P(None, both, None, col),
        P(None, None, col),
        wide,
        narrow,
        wide,
        narrow,
        wide,
        narrow,
        narrow,
        narrow,
        narrow,
        narrow,
        tokens,
        tokens,
    )
    out_specs = (
        tokens,
        tokens,
        tokens,
        tokens,
        P(None, both, None, col),
        P(None, None, col),
        wide,
        narrow,
        wide,
        narrow,
        wide,
        narrow,
        narrow,
        narrow,
        narrow,
        narrow,
    )
    return jax.shard_map(
        per_device, mesh=fine, in_specs=in_specs, out_specs=out_specs, check_vma=False
    )
```

time: 3740 us -> 1800 us (0.48)
  waiting for transfers between devices: 1660 us -> 660 us
  matrix products: 736 us -> 0 us
  Pallas kernels: 0 us -> 717 us
  blocking collectives: 710 us -> 0 us
  other arithmetic: 376 us -> 61.4 us
  starting transfers between devices: 7.56 us -> 117 us
    reduce_scatter x34 -> x0, waiting for transfers between devices: 930 us -> none  [the longest x12 327 us: project_rows(): lax.psum_scatter(partial_term(jnp.int32(0), row_share * lax.axis_size('co...]
    pallas_call x0 -> x53, Pallas kernels: none -> 717 us  [the longest x6 195 us: attn_bwd(): pl.pallas_call(strip(functools.partial(attn_bwd_kernel, dims), layer, 13...]
    dot_general x96 -> x0, matrix products: 697 us -> none  [the longest x6 136 us: attend_backward(): jnp.einsum('thd,khd->htk', attn_grad, value_rows, preferred_element_type=...]
    all_gather x42 -> x4, waiting for transfers between devices: 724 us -> 127 us  [the longest x3 89.8 us: gather_pack(): lax.all_gather(local, ('x', 'dp', 'row'), axis=0, tiled=True)]
    ppermute x0 -> x171, waiting for transfers between devices: none -> 533 us  [the longest x12 181 us: shift_row_x(): return lax.ppermute(value, ('row', 'x'), pairs)]
    all_gather x12 -> x0, blocking collectives: 417 us -> none  [the longest x6 226 us: per_device(): lax.all_gather(select(w_qkv, block_index), ('dp', 'row'), axis=0, tiled=T...]
    psum x25 -> x0, blocking collectives: 293 us -> none  [the longest x12 127 us: norm_forward(): lax.psum((jnp.sum(hidden, axis=1), jnp.sum(hidden * hidden, axis=1)), 'col')]
    reduce_sum x59 -> x0, other arithmetic: 144 us -> none  [the longest x6 62.7 us: attend_forward(): row_total = jnp.sum(exp_scores, axis=2, keepdims=True)]
  transfers between devices with their start and end apart: 76 -> 175, of which waited for: 62 -> 86; matrix products, arithmetic and copies ran while one was open for 10% -> 8% of each run, Pallas kernels for 0% -> 23%
where the time goes in v1:
time: 1800 us; the launch traced here: 1780 us
  Pallas kernels  717 us (40%)
  waiting for transfers between devices  660 us (37%)
  local copies, waits for them, and re-layouts  190 us (11%)
  starting transfers between devices  117 us (6%)
  other arithmetic  61.4 us (3%)
  between operations  37.7 us (2%)
    pallas_call x6, Pallas kernels, attn_bwd(): pl.pallas_call(strip(functools.partial(attn_bwd_kernel, dims), layer, 13...  195 us
    ppermute x12, waiting for transfers between devices, shift_row_x(): return lax.ppermute(value, ('row', 'x'), pairs)  181 us
    pallas_call x6, Pallas kernels, attn_fwd(): pl.pallas_call(strip(functools.partial(attn_fwd_kernel, dims), layer, cou...  151 us
    ppermute x16, waiting for transfers between devices, swap_x(): return lax.ppermute(value, 'x', SWAP)  137 us
    unnamed x787, local copies, waits for them, and re-layouts  121 us
    all_gather x3, waiting for transfers between devices, gather_pack(): lax.all_gather(local, ('x', 'dp', 'row'), axis=0, tiled=True)  89.8 us
    pallas_call x6, Pallas kernels, mlp_bwd(): pl.pallas_call(strip(kernel, layer, len(ins), len(deps)), grid_spec=pltpu...  89.2 us
    ppermute x18, waiting for transfers between devices, send(): got = lax.ppermute(send, axis, [(i, i ^ bit) for i in range(count)])  89 us
  transfers between devices with their start and end apart: 175, of which 86 were waited for; matrix products, arithmetic and copies ran while one was open for 8% of the time, Pallas kernels for 23%

profile of v1, /device:TPU:0, one launch (start us, length us, event | category | flops | bytes accessed | tf_op | source)
XLA Modules:
  0.0 1782.1 jit_solution(2694936018412302197)
XLA Ops:
  41.5 37.3 %all-gather.5.cloned.1.call-done.refs_8_.rest_0_.refs_12_ = bf16[3,768,768]{2,1,0:T(8,128)(2,1)} async-done(((bf16[3,96,768]{2,1,0:T(8,128)(2,1)}), bf16[3,768,768]{2,1,0:T(8,128)(2,1)}) %all-gather.5.cloned.1.call-update) | async-done | bytes 3538960 | tf_op jit(solution)/shard_map/all_gather | solution.py:1324
  117.8 16.6 collective-permute-done.12.refs_6_
  147.0 25.3 %attn_fwd.6 = (bf16[288,256]{1,0:T(8,128)(2,1)S(1)}, bf16[288,256]{1,0:T(8,128)(2,1)S(1)}, bf16[288,256]{1,0:T(8,128)(2,1)S(1)}, bf16[288,256]{1,0:T(8,128)(2,1)...) custom-call(s32[51]{0:T(128)S(1)} %copy-done.108, ...), custom_call_target="tpu_custom_call" | custom-call | flops 6568280064 | bytes 12000000 | tf_op jit(solution)/shard_map/attn_fwd/pallas_call | solution.py:470
  216.6 17.5 collective-permute-done.19.refs_2_
  247.7 25.0 %attn_fwd.7 = (bf16[288,256]{1,0:T(8,128)(2,1)S(1)}, bf16[288,256]{1,0:T(8,128)(2,1)S(1)}, bf16[288,256]{1,0:T(8,128)(2,1)S(1)}, bf16[288,256]{1,0:T(8,128)(2,1)...) custom-call(s32[51]{0:T(128)S(1)} %copy-done.109, ...), custom_call_target="tpu_custom_call" | custom-call | flops 6568280064 | bytes 12000000 | tf_op jit(solution)/shard_map/attn_fwd/pallas_call | solution.py:470
  287.2 87.9 %all-gather.11.cloned.1.call-done = bf16[1536,1792]{1,0:T(8,128)(2,1)} async-done(((bf16[96,1792]{1,0:T(8,128)(2,1)}), bf16[1536,1792]{1,0:T(8,128)(2,1)}) %all-gather.11.cloned.1.call-update) | async-done | bytes 5505040 | tf_op jit(solution)/shard_map/all_gather | solution.py:1347
  423.3 25.0 %attn_fwd.8 = (bf16[288,256]{1,0:T(8,128)(2,1)S(1)}, bf16[288,256]{1,0:T(8,128)(2,1)S(1)}, bf16[288,256]{1,0:T(8,128)(2,1)S(1)}, bf16[288,256]{1,0:T(8,128)(2,1)...) custom-call(s32[51]{0:T(128)S(1)} %copy-done.110, ...), custom_call_target="tpu_custom_call" | custom-call | flops 6568280064 | bytes 12000000 | tf_op jit(solution)/shard_map/attn_fwd/pallas_call | solution.py:470
  495.4 25.0 %attn_fwd.9 = (bf16[288,256]{1,0:T(8,128)(2,1)S(1)}, bf16[288,256]{1,0:T(8,128)(2,1)S(1)}, bf16[288,256]{1,0:T(8,128)(2,1)S(1)}, bf16[288,256]{1,0:T(8,128)(2,1)...) custom-call(s32[51]{0:T(128)S(1)} %copy-done.110, ...), custom_call_target="tpu_custom_call" | custom-call | flops 6568280064 | bytes 12000000 | tf_op jit(solution)/shard_map/attn_fwd/pallas_call | solution.py:470
  569.8 25.0 %attn_fwd.10 = (bf16[288,256]{1,0:T(8,128)(2,1)S(1)}, bf16[288,256]{1,0:T(8,128)(2,1)S(1)}, bf16[288,256]{1,0:T(8,128)(2,1)S(1)}, bf16[288,256]{1,0:T(8,128)(2,1...) custom-call(s32[51]{0:T(128)S(1)} %copy-done.110, ...), custom_call_target="tpu_custom_call" | custom-call | flops 6568280064 | bytes 12000000 | tf_op jit(solution)/shard_map/attn_fwd/pallas_call | solution.py:470
  657.8 25.3 %attn_fwd.11 = (bf16[288,256]{1,0:T(8,128)(2,1)S(1)}, bf16[288,256]{1,0:T(8,128)(2,1)}, bf16[288,256]{1,0:T(8,128)(2,1)}, bf16[288,256]{1,0:T(8,128)(2,1)}, bf16...) custom-call(s32[51]{0:T(128)S(1)} %copy-done.110, ...), custom_call_target="tpu_custom_call" | custom-call | flops 6568280064 | bytes 12000000 | tf_op jit(solution)/shard_map/attn_fwd/pallas_call | solution.py:470
  739.0 14.6 dw_mlp.3
  754.4 32.4 %attn_bwd.6 = (bf16[288,768]{1,0:T(8,128)(2,1)}, bf16[288,768]{1,0:T(8,128)(2,1)}, bf16[288,768]{1,0:T(8,128)(2,1)}, bf16[288,768]{1,0:T(8,128)(2,1)}, bf16[256,...) custom-call(s32[51]{0:T(128)} %stack.138.sc_ref.sc, ...), custom_call_target="tpu_custom_call" | custom-call | flops 12343836672 | bytes 14000000 | tf_op jit(solution)/shard_map/attn_bwd/pallas_call | solution.py:651
  817.2 15.4 mlp_bwd.7
  836.1 14.8 dw_mlp.4
  851.8 32.6 %attn_bwd.7 = (bf16[288,768]{1,0:T(8,128)(2,1)}, bf16[288,768]{1,0:T(8,128)(2,1)}, bf16[288,768]{1,0:T(8,128)(2,1)}, bf16[288,768]{1,0:T(8,128)(2,1)}, bf16[256,...) custom-call(s32[51]{0:T(128)} %stack.138.sc_ref.sc, ...), custom_call_target="tpu_custom_call" | custom-call | flops 12343836672 | bytes 14000000 | tf_op jit(solution)/shard_map/attn_bwd/pallas_call | solution.py:651
  913.6 14.9 mlp_bwd.8
  932.0 15.0 dw_mlp.5
  947.8 32.6 %attn_bwd.8 = (bf16[288,768]{1,0:T(8,128)(2,1)}, bf16[288,768]{1,0:T(8,128)(2,1)}, bf16[288,768]{1,0:T(8,128)(2,1)}, bf16[288,768]{1,0:T(8,128)(2,1)}, bf16[256,...) custom-call(s32[51]{0:T(128)} %stack.138.sc_ref.sc, ...), custom_call_target="tpu_custom_call" | custom-call | flops 12343836672 | bytes 14000000 | tf_op jit(solution)/shard_map/attn_bwd/pallas_call | solution.py:651
  1010.5 14.9 mlp_bwd.9
  1028.3 24.2 %dw_last.3 = (bf16[2,768,1792]{2,1,0:T(8,128)(2,1)}, bf16[2,768,1792]{2,1,0:T(8,128)(2,1)}, bf16[3,4,768,1792]{3,2,1,0:T(8,128)(2,1)}, f32[8,128]{1,0:T(8,128)S(1)}) custom-call(s32[51]{0:T(128)S(1)} %copy-done.113, bf16[288,768]{1,0:T(8,128)(2,1)S(1)} %get-tuple-element.469.refs_0_, ...), custom_call_target="tpu_custom_call", output_to_operand_aliasing={{2}: (10, {})} | custom-call | flops 3170893824 | bytes 30000000 | tf_op jit(solution)/shard_map/dw_last/pallas_call | solution.py:915
  1094.0 32.4 %attn_bwd.9 = (bf16[288,768]{1,0:T(8,128)(2,1)}, bf16[288,768]{1,0:T(8,128)(2,1)}, bf16[288,768]{1,0:T(8,128)(2,1)}, bf16[288,768]{1,0:T(8,128)(2,1)}, bf16[256,...) custom-call(s32[51]{0:T(128)} %stack.138.sc_ref.sc, ...), custom_call_target="tpu_custom_call" | custom-call | flops 12343836672 | bytes 14000000 | tf_op jit(solution)/shard_map/attn_bwd/pallas_call | solution.py:651
  1163.7 53.4 %collective-permute-done.117.refs_5_ = bf16[256,768]{1,0:T(8,128)(2,1)} collective-permute-done((bf16[256,768]{1,0:T(8,128)(2,1)}, bf16[256,768]{1,0:T(8,128)(2,1)}, u32[]{:S(2)}, u32[]{:S(2)}) %collective-permute-start.117) | collective-permute-done | bytes 393248 | tf_op jit(solution)/shard_map/ppermute | solution.py:974
  1228.6 15.5 mlp_bwd.10
  1246.3 24.4 %dw_last.4 = (bf16[2,768,1792]{2,1,0:T(8,128)(2,1)}, bf16[2,768,1792]{2,1,0:T(8,128)(2,1)}, bf16[3,4,768,1792]{3,2,1,0:T(8,128)(2,1)}, f32[8,128]{1,0:T(8,128)S(1)}) custom-call(s32[51]{0:T(128)S(1)} %copy-done.114, bf16[288,768]{1,0:T(8,128)(2,1)S(1)} %get-tuple-element.503.refs_0_, ...), custom_call_target="tpu_custom_call", output_to_operand_aliasing={{2}: (10, {})} | custom-call | flops 3170893824 | bytes 30000000 | tf_op jit(solution)/shard_map/dw_last/pallas_call | solution.py:915
  1296.0 32.6 %attn_bwd.10 = (bf16[288,768]{1,0:T(8,128)(2,1)}, bf16[288,768]{1,0:T(8,128)(2,1)}, bf16[288,768]{1,0:T(8,128)(2,1)}, bf16[288,768]{1,0:T(8,128)(2,1)}, bf16[256...) custom-call(s32[51]{0:T(128)} %stack.138.sc_ref.sc, ...), custom_call_target="tpu_custom_call" | custom-call | flops 12343836672 | bytes 14000000 | tf_op jit(solution)/shard_map/attn_bwd/pallas_call | solution.py:651
  1385.2 15.3 mlp_bwd.11
  1413.6 24.1 %dw_last.5 = (bf16[2,768,1792]{2,1,0:T(8,128)(2,1)}, bf16[2,768,1792]{2,1,0:T(8,128)(2,1)}, bf16[3,4,768,1792]{3,2,1,0:T(8,128)(2,1)}, f32[8,128]{1,0:T(8,128)S(1)}) custom-call(s32[51]{0:T(128)S(1)} %copy-done.115, bf16[288,768]{1,0:T(8,128)(2,1)S(1)} %copy-done.89, bf16[288,768]{1,0:T(8,128)(2,1)S(1)} %copy-done.87, ...), custom_call_target="tpu_custom_call", output_to_operand_aliasing={{2}: (10, {})} | custom-call | flops 3170893824 | bytes 30000000 | tf_op jit(solution)/shard_map/dw_last/pallas_call | solution.py:915
  1439.5 32.7 %attn_bwd.11 = (bf16[288,768]{1,0:T(8,128)(2,1)}, bf16[288,768]{1,0:T(8,128)(2,1)}, bf16[288,768]{1,0:T(8,128)(2,1)}, bf16[288,768]{1,0:T(8,128)(2,1)}, bf16[256...) custom-call(s32[51]{0:T(128)} %stack.138.sc_ref.sc, ...), custom_call_target="tpu_custom_call" | custom-call | flops 12343836672 | bytes 14000000 | tf_op jit(solution)/shard_map/attn_bwd/pallas_call | solution.py:651
  1528.0 38.7 %collective-permute-done.141.refs_5_ = bf16[256,768]{1,0:T(8,128)(2,1)} collective-permute-done((bf16[256,768]{1,0:T(8,128)(2,1)}, bf16[256,768]{1,0:T(8,128)(2,1)}, u32[]{:S(2)}, u32[]{:S(2)}) %collective-permute-start.141) | collective-permute-done | bytes 393248 | tf_op jit(solution)/shard_map/ppermute | solution.py:974
  1594.1 58.9 %collective-permute-done.155 = f32[6912]{0:T(1024)S(1)} collective-permute-done((f32[6912]{0:T(1024)S(1)}, f32[6912]{0:T(1024)S(1)}, u32[]{:S(2)}, u32[]{:S(2)}) %collective-permute-start.155) | collective-permute-done | bytes 27680 | tf_op jit(solution)/shard_map/ppermute | solution.py:963
  1699.9 25.5 %collective-permute-done.161 = bf16[4,1,96,1792]{3,2,0,1:T(8,128)(2,1)} collective-permute-done((bf16[4,1,96,1792]{3,2,0,1:T(8,128)(2,1)}, bf16[4,1,96,1792]{3,2,0,1:T(8,128)(2,1)}, u32[]{:S(2)}, u32[]{:S(2)}) %collective-permute-start.161) | collective-permute-done | bytes 1376288 | tf_op jit(solution)/shard_map/ppermute | solution.py:1218
  1731.8 28.9 %collective-permute-done.162 = bf16[2,1,96,1792]{3,2,1,0:T(8,128)(2,1)S(1)} collective-permute-done((bf16[2,1,96,1792]{3,2,1,0:T(8,128)(2,1)S(1)}, bf16[2,1,96,1792]{3,2,1,0:T(8,128)(2,1)S(1)}, u32[]{:S(2)}, u32[]{:S(2)}) %collective-permute-start.162) | collective-permute-done | bytes 688160 | tf_op jit(solution)/shard_map/ppermute | solution.py:1218
  (1380 shorter events, 840.5 us)
Async XLA Ops:
  7.2 71.5 %all-gather.5.cloned.1.call-start = ((), (), s32[]{:S(2)}) async-start(), calls=%async_computation | async-start | bytes 3981312 | tf_op jit(solution)/shard_map/all_gather | solution.py:1324
  9.9 177.1 %all-gather.7.cloned.1.call-start = ((), (), s32[]{:S(2)}) async-start(), calls=%async_computation.1 | async-start | bytes 5849088 | tf_op jit(solution)/shard_map/all_gather | solution.py:1347
  91.0 196.0 %all-gather.9.cloned.1.call-start = ((), (), s32[]{:S(2)}) async-start(), calls=%async_computation.2 | async-start | bytes 5849088 | tf_op jit(solution)/shard_map/all_gather | solution.py:1347
  185.1 190.0 %all-gather.11.cloned.1.call-start = ((), (), s32[]{:S(2)}) async-start(), calls=%async_computation.3 | async-start | bytes 5849088 | tf_op jit(solution)/shard_map/all_gather | solution.py:1347
  287.0 90.0 %collective-permute-start.28 = (bf16[2,768,1792]{2,1,0:T(8,128)(2,1)}, bf16[2,768,1792]{2,1,0:T(8,128)(2,1)}, u32[]{:S(2)}, u32[]{:S(2)}) collective-permute-start(bf16[2,768,1792]{2,1,0:T(8,128)(2,1)} %bitcast.253), channel_id=1, source_target_pairs={{0,1},{1,0},{2,3},{3,2},{4,5},{5,4},{6,7},{7,6},{8,9},{9,8},{10,11... | collective-permute-start | bytes 16515080 | tf_op jit(solution)/shard_map/ppermute | solution.py:959
  375.1 83.7 %collective-permute-start.39 = (bf16[2,768,1792]{2,1,0:T(8,128)(2,1)}, bf16[2,768,1792]{2,1,0:T(8,128)(2,1)}, u32[]{:S(2)}, u32[]{:S(2)}) collective-permute-start(bf16[2,768,1792]{2,1,0:T(8,128)(2,1)} %bitcast.265), channel_id=1, source_target_pairs={{0,1},{1,0},{2,3},{3,2},{4,5},{5,4},{6,7},{7,6},{8,9},{9,8},{10,11... | collective-permute-start | bytes 16515080 | tf_op jit(solution)/shard_map/ppermute | solution.py:959
  622.5 31.4 %collective-permute-start.60 = (bf16[288,768]{1,0:T(8,128)(2,1)}, bf16[288,768]{1,0:T(8,128)(2,1)}, u32[]{:S(2)}, u32[]{:S(2)}) collective-permute-start(bf16[288,768]{1,0:T(8,128)(2,1)} %get-tuple-element.343.refs_0_), channel_id=1, source_target_pairs={{0,1},{1,0},{2,3},{3,2},{4,5},{5,4},{6,7},{7,6},{8,9},{9,8},{10,11... | collective-permute-start | bytes 1327112 | tf_op jit(solution)/shard_map/ppermute | solution.py:959
  653.9 33.7 %collective-permute-start.75 = (bf16[288,192]{1,0:T(8,128)(2,1)S(1)}, bf16[288,192]{1,0:T(8,128)(2,1)S(1)}, u32[]{:S(2)}, u32[]{:S(2)}) collective-permute-start(bf16[288,192]{1,0:T(8,128)(2,1)S(1)} %get-tuple-element.357), channel_id=1, source_target_pairs={{0,1},{1,0},{2,3},{3,2},{4,5},{5,4},{6,7},{7,6},{8,9},{9,8},{10,11... | collective-permute-start | bytes 331784 | tf_op jit(solution)/shard_map/ppermute | solution.py:996
  1052.6 86.9 %collective-permute-start.118 = (bf16[2,768,1792]{2,1,0:T(8,128)(2,1)}, bf16[2,768,1792]{2,1,0:T(8,128)(2,1)}, u32[]{:S(2)}, u32[]{:S(2)}) collective-permute-start(bf16[2,768,1792]{2,1,0:T(8,128)(2,1)} %get-tuple-element.494), channel_id=1, source_target_pairs={{0,1},{1,0},{2,3},{3,2},{4,5},{5,4},{6,7},{7,6},{8,9},{9,8},{10,11... | collective-permute-start | bytes 16515080 | tf_op jit(solution)/shard_map/ppermute | solution.py:959
  1144.9 143.8 %collective-permute-start.131 = (bf16[768,1792]{1,0:T(8,128)(2,1)}, bf16[768,1792]{1,0:T(8,128)(2,1)}, u32[]{:S(2)}, u32[]{:S(2)}) collective-permute-start(bf16[768,1792]{1,0:T(8,128)(2,1)} %fusion.3.refs_17_), channel_id=1, source_target_pairs={{0,2},{2,0},{1,3},{3,1},{4,6},{6,4},{5,7},{7,5},{8,10},{10,8},{9,1... | collective-permute-start | bytes 8257544 | tf_op jit(solution)/shard_map/ppermute | solution.py:963
  1149.7 67.4 %collective-permute-start.117 = (bf16[256,768]{1,0:T(8,128)(2,1)}, bf16[256,768]{1,0:T(8,128)(2,1)}, u32[]{:S(2)}, u32[]{:S(2)}) collective-permute-start(bf16[256,768]{1,0:T(8,128)(2,1)} %get-tuple-element.487), channel_id=1, source_target_pairs={{0,6},{2,4},{4,2},{6,0},{1,7},{3,5},{5,3},{7,1},{8,14},{10,12},{12... | collective-permute-start | bytes 1179656 | tf_op jit(solution)/shard_map/ppermute | solution.py:974
  1151.2 73.5 %collective-permute-start.115 = (bf16[288,768]{1,0:T(8,128)(2,1)}, bf16[288,768]{1,0:T(8,128)(2,1)S(1)}, u32[]{:S(2)}, u32[]{:S(2)}) collective-permute-start(bf16[288,768]{1,0:T(8,128)(2,1)} %get-tuple-element.485), channel_id=1, source_target_pairs={{0,2},{2,0},{1,3},{3,1},{4,6},{6,4},{5,7},{7,5},{8,10},{10,8},{9,1... | collective-permute-start | bytes 1327112 | tf_op jit(solution)/shard_map/ppermute | solution.py:963
  1160.0 117.6 %collective-permute-start.152 = (bf16[2,1,96,768]{2,3,1,0:T(8,128)(2,1)}, bf16[2,1,96,768]{2,3,1,0:T(8,128)(2,1)}, u32[]{:S(2)}, u32[]{:S(2)}) collective-permute-start(bf16[2,1,96,768]{2,3,1,0:T(8,128)(2,1)} %bitcast.313), channel_id=1, source_target_pairs={{0,16},{8,24},{16,0},{24,8},{1,17},{9,25},{17,1},{25,9},{2,18},{10... | collective-permute-start | bytes 884744 | tf_op jit(solution)/shard_map/ppermute | solution.py:1218
  1271.4 97.2 %collective-permute-start.130 = (bf16[2,768,1792]{2,1,0:T(8,128)(2,1)}, bf16[2,768,1792]{2,1,0:T(8,128)(2,1)}, u32[]{:S(2)}, u32[]{:S(2)}) collective-permute-start(bf16[2,768,1792]{2,1,0:T(8,128)(2,1)} %get-tuple-element.532), channel_id=1, source_target_pairs={{0,1},{1,0},{2,3},{3,2},{4,5},{5,4},{6,7},{7,6},{8,9},{9,8},{10,11... | collective-permute-start | bytes 16515080 | tf_op jit(solution)/shard_map/ppermute | solution.py:959
  1293.2 36.0 %collective-permute-start.168 = (bf16[4,1,96,1792]{3,2,0,1:T(8,128)(2,1)S(1)}, bf16[4,1,96,1792]{3,2,0,1:T(8,128)(2,1)}, u32[]{:S(2)}, u32[]{:S(2)}) collective-permute-start(bf16[4,1,96,1792]{3,2,0,1:T(8,128)(2,1)S(1)} %dynamic-slice_bitcast_fusion), channel_id=1, source_target_pairs={{0,4},{4,0},{1,5},{5,1},{2,6},{6,2},{3,7},{7,3},{8,12},{12,8},{9,1... | collective-permute-start | bytes 4128776 | tf_op jit(solution)/shard_map/ppermute | solution.py:1218
  1331.9 34.6 %collective-permute-start.169 = (bf16[2,1,96,1792]{3,2,1,0:T(8,128)(2,1)}, bf16[2,1,96,1792]{3,2,1,0:T(8,128)(2,1)}, u32[]{:S(2)}, u32[]{:S(2)}) collective-permute-start(bf16[2,1,96,1792]{3,2,1,0:T(8,128)(2,1)} %dynamic-slice_bitcast_fusion.3), channel_id=1, source_target_pairs={{0,16},{8,24},{16,0},{24,8},{1,17},{9,25},{17,1},{25,9},{2,18},{10... | collective-permute-start | bytes 2064392 | tf_op jit(solution)/shard_map/ppermute | solution.py:1218
  1437.8 149.7 %collective-permute-start.159 = (bf16[2,768,1792]{2,1,0:T(8,128)(2,1)}, bf16[2,768,1792]{2,1,0:T(8,128)(2,1)}, u32[]{:S(2)}, u32[]{:S(2)}) collective-permute-start(bf16[2,768,1792]{2,1,0:T(8,128)(2,1)} %get-tuple-element.585), channel_id=1, source_target_pairs={{0,1},{1,0},{2,3},{3,2},{4,5},{5,4},{6,7},{7,6},{8,9},{9,8},{10,11... | collective-permute-start | bytes 16515080 | tf_op jit(solution)/shard_map/ppermute | solution.py:959
  1495.0 162.0 %collective-permute-start.164 = (bf16[768,1792]{1,0:T(8,128)(2,1)}, bf16[768,1792]{1,0:T(8,128)(2,1)}, u32[]{:S(2)}, u32[]{:S(2)}) collective-permute-start(bf16[768,1792]{1,0:T(8,128)(2,1)} %fusion.4.refs_18_), channel_id=1, source_target_pairs={{0,2},{2,0},{1,3},{3,1},{4,6},{6,4},{5,7},{7,5},{8,10},{10,8},{9,1... | collective-permute-start | bytes 8257544 | tf_op jit(solution)/shard_map/ppermute | solution.py:963
  1505.1 61.6 %collective-permute-start.141 = (bf16[256,768]{1,0:T(8,128)(2,1)}, bf16[256,768]{1,0:T(8,128)(2,1)}, u32[]{:S(2)}, u32[]{:S(2)}) collective-permute-start(bf16[256,768]{1,0:T(8,128)(2,1)} %get-tuple-element.559), channel_id=1, source_target_pairs={{0,6},{2,4},{4,2},{6,0},{1,7},{3,5},{5,3},{7,1},{8,14},{10,12},{12... | collective-permute-start | bytes 1179656 | tf_op jit(solution)/shard_map/ppermute | solution.py:974
  1517.8 56.7 %collective-permute-start.139 = (bf16[288,768]{1,0:T(8,128)(2,1)}, bf16[288,768]{1,0:T(8,128)(2,1)S(1)}, u32[]{:S(2)}, u32[]{:S(2)}) collective-permute-start(bf16[288,768]{1,0:T(8,128)(2,1)} %copy-done.197), channel_id=1, source_target_pairs={{0,2},{2,0},{1,3},{3,1},{4,6},{6,4},{5,7},{7,5},{8,10},{10,8},{9,1... | collective-permute-start | bytes 1327112 | tf_op jit(solution)/shard_map/ppermute | solution.py:963
  1526.8 56.7 %collective-permute-start.150 = (bf16[2,1,96,768]{2,3,1,0:T(8,128)(2,1)}, bf16[2,1,96,768]{2,3,1,0:T(8,128)(2,1)}, u32[]{:S(2)}, u32[]{:S(2)}) collective-permute-start(bf16[2,1,96,768]{2,3,1,0:T(8,128)(2,1)} %dynamic-slice_bitcast_fusion.9), channel_id=1, source_target_pairs={{0,16},{8,24},{16,0},{24,8},{1,17},{9,25},{17,1},{25,9},{2,18},{10... | collective-permute-start | bytes 884744 | tf_op jit(solution)/shard_map/ppermute | solution.py:1218
  1583.5 84.3 %collective-permute-start.142 = (bf16[288,192]{1,0:T(8,128)(2,1)}, bf16[288,192]{1,0:T(8,128)(2,1)S(1)}, u32[]{:S(2)}, u32[]{:S(2)}) collective-permute-start(bf16[288,192]{1,0:T(8,128)(2,1)} %copy-done.257), channel_id=1, source_target_pairs={{0,1},{1,0},{2,3},{3,2},{4,5},{5,4},{6,7},{7,6},{8,9},{9,8},{10,11... | collective-permute-start | bytes 331784 | tf_op jit(solution)/shard_map/ppermute | solution.py:996
  1585.1 84.2 %collective-permute-start.143 = (bf16[288,192]{1,0:T(8,128)(2,1)}, bf16[288,192]{1,0:T(8,128)(2,1)S(1)}, u32[]{:S(2)}, u32[]{:S(2)}) collective-permute-start(bf16[288,192]{1,0:T(8,128)(2,1)} %copy-done.256), channel_id=1, source_target_pairs={{0,2},{1,3},{2,0},{3,1},{4,6},{5,7},{6,4},{7,5},{8,10},{9,11},{10,... | collective-permute-start | bytes 331784 | tf_op jit(solution)/shard_map/ppermute | solution.py:996
  1591.0 71.5 %collective-permute-start.160 = (bf16[768,1792]{1,0:T(8,128)(2,1)S(1)}, bf16[768,1792]{1,0:T(8,128)(2,1)S(1)}, u32[]{:S(2)}, u32[]{:S(2)}) collective-permute-start(bf16[768,1792]{1,0:T(8,128)(2,1)S(1)} %fusion.5), channel_id=1, source_target_pairs={{0,2},{2,0},{1,3},{3,1},{4,6},{6,4},{5,7},{7,5},{8,10},{10,8},{9,1... | collective-permute-start | bytes 8257544 | tf_op jit(solution)/shard_map/ppermute | solution.py:963
  1592.4 60.7 %collective-permute-start.155 = (f32[6912]{0:T(1024)S(1)}, f32[6912]{0:T(1024)S(1)}, u32[]{:S(2)}, u32[]{:S(2)}) collective-permute-start(f32[6912]{0:T(1024)S(1)} %get-tuple-element.618), channel_id=1, source_target_pairs={{0,2},{2,0},{1,3},{3,1},{4,6},{6,4},{5,7},{7,5},{8,10},{10,8},{9,1... | collective-permute-start | bytes 82952 | tf_op jit(solution)/shard_map/ppermute | solution.py:963
  1662.6 33.4 %collective-permute-start.165 = (bf16[4,1,96,1792]{3,2,0,1:T(8,128)(2,1)}, bf16[4,1,96,1792]{3,2,0,1:T(8,128)(2,1)}, u32[]{:S(2)}, u32[]{:S(2)}) collective-permute-start(bf16[4,1,96,1792]{3,2,0,1:T(8,128)(2,1)} %dynamic-slice_bitcast_fusion.1), channel_id=1, source_target_pairs={{0,4},{4,0},{1,5},{5,1},{2,6},{6,2},{3,7},{7,3},{8,12},{12,8},{9,1... | collective-permute-start | bytes 4128776 | tf_op jit(solution)/shard_map/ppermute | solution.py:1218
  1671.3 54.1 %collective-permute-start.161 = (bf16[4,1,96,1792]{3,2,0,1:T(8,128)(2,1)}, bf16[4,1,96,1792]{3,2,0,1:T(8,128)(2,1)}, u32[]{:S(2)}, u32[]{:S(2)}) collective-permute-start(bf16[4,1,96,1792]{3,2,0,1:T(8,128)(2,1)} %dynamic-slice_bitcast_fusion.2), channel_id=1, source_target_pairs={{0,4},{4,0},{1,5},{5,1},{2,6},{6,2},{3,7},{7,3},{8,12},{12,8},{9,1... | collective-permute-start | bytes 4128776 | tf_op jit(solution)/shard_map/ppermute | solution.py:1218
  1675.7 91.5 %collective-permute-start.170 = (bf16[1,1,96,1792]{3,2,1,0:T(8,128)(2,1)}, bf16[1,1,96,1792]{3,2,1,0:T(8,128)(2,1)}, u32[]{:S(2)}, u32[]{:S(2)}) collective-permute-start(bf16[1,1,96,1792]{3,2,1,0:T(8,128)(2,1)} %constant_dynamic-slice_fusion), channel_id=1, source_target_pairs={{0,8},{8,0},{16,24},{24,16},{1,9},{9,1},{17,25},{25,17},{2,10},{10... | collective-permute-start | bytes 1032200 | tf_op jit(solution)/shard_map/ppermute | solution.py:1218
  1680.0 85.2 %collective-permute-start.145 = (bf16[512,192]{1,0:T(8,128)(2,1)S(1)}, bf16[512,192]{1,0:T(8,128)(2,1)}, u32[]{:S(2)}, u32[]{:S(2)}) collective-permute-start(bf16[512,192]{1,0:T(8,128)(2,1)S(1)} %get-tuple-element.565), channel_id=1, source_target_pairs={{4,0},{0,4},{5,1},{1,5},{6,2},{2,6},{7,3},{3,7},{12,8},{8,12},{13,... | collective-permute-start | bytes 589832 | tf_op jit(solution)/shard_map/ppermute | solution.py:1158
  1698.1 33.5 %collective-permute-start.166 = (bf16[2,1,96,1792]{3,2,1,0:T(8,128)(2,1)S(1)}, bf16[2,1,96,1792]{3,2,1,0:T(8,128)(2,1)S(1)}, u32[]{:S(2)}, u32[]{:S(2)}) collective-permute-start(bf16[2,1,96,1792]{3,2,1,0:T(8,128)(2,1)S(1)} %dynamic-slice_bitcast_fusion.4), channel_id=1, source_target_pairs={{0,16},{8,24},{16,0},{24,8},{1,17},{9,25},{17,1},{25,9},{2,18},{10... | collective-permute-start | bytes 2064392 | tf_op jit(solution)/shard_map/ppermute | solution.py:1218
  1727.2 33.5 %collective-permute-start.162 = (bf16[2,1,96,1792]{3,2,1,0:T(8,128)(2,1)S(1)}, bf16[2,1,96,1792]{3,2,1,0:T(8,128)(2,1)S(1)}, u32[]{:S(2)}, u32[]{:S(2)}) collective-permute-start(bf16[2,1,96,1792]{3,2,1,0:T(8,128)(2,1)S(1)} %dynamic-slice_bitcast_fusion.5), channel_id=1, source_target_pairs={{0,16},{8,24},{16,0},{24,8},{1,17},{9,25},{17,1},{25,9},{2,18},{10... | collective-permute-start | bytes 2064392 | tf_op jit(solution)/shard_map/ppermute | solution.py:1218
  1731.7 35.5 %collective-permute-start.167 = (bf16[1,1,96,1792]{3,2,1,0:T(8,128)(2,1)S(1)}, bf16[1,1,96,1792]{3,2,1,0:T(8,128)(2,1)}, u32[]{:S(2)}, u32[]{:S(2)}) collective-permute-start(bf16[1,1,96,1792]{3,2,1,0:T(8,128)(2,1)S(1)} %constant_dynamic-slice_fusion.1), channel_id=1, source_target_pairs={{0,8},{8,0},{16,24},{24,16},{1,9},{9,1},{17,25},{25,17},{2,10},{10... | collective-permute-start | bytes 1032200 | tf_op jit(solution)/shard_map/ppermute | solution.py:1218
  (526 other events, 11070.6 us)
Sparse Core Ops, SparseCore 0:
  10.8 67.8 all-gather.4
  91.1 95.8 all-gather.6
  190.3 95.9 all-gather.8
  289.4 85.6 all-gather.10

commit v2 on v1

--- a/solution.py
+++ b/solution.py
@@ -80,75 +80,68 @@
     return pl.CostEstimate(flops=int(flops), bytes_accessed=int(nbytes), transcendentals=int(trans))
 
 
-def weight_copies(mine, other, my_x, wout, wud, sems):
-    copies = []
-    for s in range(4):
-        src = (mine if s % 2 == 0 else other).at[my_x ^ (s // 2)]
-        copies.append(
-            (
-                pltpu.make_async_copy(src.at[:, pl.ds(1536, 256)], wout.at[s], sems.at[0, s]),
-                pltpu.make_async_copy(src.at[:, pl.ds(0, 1536)], wud.at[s], sems.at[1, s]),
-            )
-        )
-    return copies
-
-
-def start_weights(sc, packs, wout, wud, sems, out_first):
-    def go(pair):
-        copies = weight_copies(pair[0], pair[1], sc[4], wout, wud, sems)
-        order = (0, 1) if out_first else (1, 0)
+class Weights:
+
+    def __init__(self, sc, packs, wout, wud, sems):
+        self.sc, self.packs, self.sems = sc, packs, sems
+        self.dst = ((wout, 1536, 256), (wud, 0, 1536))
+        self.parts, self.size = packs[0].shape[1], packs[0].shape[2]
+
+    def start(self, order):
+        if len(self.packs) == 1:
+            self.start_from(self.packs[0], order)
+        else:
+            for k, src in enumerate(self.packs):
+                pl.when(self.sc[1] == k)(functools.partial(self.start_from, src, order))
+
+    def start_from(self, src, order):
         for kind in order:
+            dst, lo, size = self.dst[kind]
             for s in range(4):
-                copies[s][kind].start()
-
-    if len(packs) == 1:
-        go(packs[0])
-    else:
-        for k, pair in enumerate(packs):
-            pl.when(sc[1] == k)(functools.partial(go, pair))
+                for j in range(self.parts):
+                    rows = pl.ds(j * self.size, self.size)
+                    pltpu.make_async_copy(
+                        src.at[self.sc[3] ^ s, j, :, pl.ds(lo, size)],
+                        dst.at[s, rows],
+                        self.sems.at[kind, s],
+                    ).start()
+
+    def wait(self, kind, s):
+        dst = self.dst[kind][0].at[s]
+        pltpu.make_async_copy(dst, dst, self.sems.at[kind, s]).wait()
 
 
 def mlp_fwd_kernel(ranks, last, prompt, sc, *refs):
     h_ref, o0, o1, o2, o3, vec_ref, bup_ref, nvec_ref = refs[:8]
-    packs = [(refs[8 + 2 * k], refs[9 + 2 * k]) for k in range(ranks)]
-    outs = refs[8 + 2 * ranks :]
-    h1_ref, u_hbm, m_hbm, h_out = outs[:4]
-    wout, wud, sems, u_ref, m_ref, osem = outs[-6:]
-    start_weights(sc, packs, wout, wud, sems, True)
-    waits = weight_copies(packs[0][0], packs[0][1], sc[4], wout, wud, sems)
+    outs = refs[8 + ranks :]
+    h1_ref, u_ref, h_out = outs[:3]
+    wout, wud, sems = outs[-3:]
+    weights = Weights(sc, refs[8 : 8 + ranks], wout, wud, sems)
+    weights.start((0, 1))
     total = h_ref[...] + vec_ref[0, 0:1, :]
     for s, o_ref in enumerate((o0, o1, o2, o3)):
-        waits[s][0].wait()
+        weights.wait(0, s)
         total = total + nt(o_ref[...], wout[s])
     h1_ref[...] = total
     centered, _ = stats(total)
     a2 = (centered * vec_ref[0, 2:3, :] + vec_ref[0, 3:4, :]).astype(BF16)
     h_out[...] = total + vec_ref[0, 1:2, :]
-    stores = []
     for s in range(4):
-        waits[s][1].wait()
+        weights.wait(1, s)
         bias = bup_ref[0, pl.ds(sc[3] ^ s, 1), 0, :]
         up = nn(a2, wud[s, :, 0:768]) + bias
         u_ref[s] = up.astype(BF16)
         act = 0.5 * up * (1.0 + jnp.tanh(GELU_COEF * (up + 0.044715 * up * up * up)))
-        act = act.astype(BF16)
-        m_ref[s] = act
-        stores.append(pltpu.make_async_copy(u_ref.at[s], u_hbm.at[s], osem.at[0, s]))
-        stores.append(pltpu.make_async_copy(m_ref.at[s], m_hbm.at[s], osem.at[1, s]))
-        stores[-2].start()
-        stores[-1].start()
-        h_out[...] += nt(act, wud[s, :, 768:1536])
+        h_out[...] += nt(act.astype(BF16), wud[s, :, 768:1536])
     if last:
-        y_refs = outs[4:8]
+        y_refs = outs[3:7]
         send_features(sc, h_out, y_refs)
     else:
-        a_ref, ap_ref = outs[4:6]
+        a_ref, ap_ref = outs[3:5]
         centered, _ = stats(h_out[...])
         nxt = (centered * nvec_ref[0, 4:5, :] + nvec_ref[0, 5:6, :]).astype(BF16)
         a_ref[...] = nxt
         ap_ref[...] = nxt[:prompt]
-    for copy in stores:
-        copy.wait()
 
 
 def send_features(sc, value, refs):
@@ -181,14 +174,12 @@
     pltpu.SemaphoreType.DMA((2, 4)),
 ]
 ANY = pl.BlockSpec(memory_space=pl.ANY)
-HBM = pl.BlockSpec(memory_space=pltpu.HBM)
 
 
 def mlp_fwd(layer, sc, hidden, o_parts, vecs, bup, packs, prompt, last, width, deps=()):
     tok = hidden.shape[0]
     shapes = [
         jax.ShapeDtypeStruct((tok, D), F32),
-        jax.ShapeDtypeStruct((4, tok, D), BF16),
         jax.ShapeDtypeStruct((4, tok, D), BF16),
         jax.ShapeDtypeStruct((tok, D), F32),
     ]
@@ -197,8 +188,7 @@
     else:
         shapes += [jax.ShapeDtypeStruct((tok, D), BF16), jax.ShapeDtypeStruct((prompt, D), BF16)]
     out_specs = [whole_spec(v.shape) for v in shapes]
-    out_specs[1] = out_specs[2] = HBM
-    ins = [hidden, *o_parts, vecs, bup, vecs, *[w for pair in packs for w in pair]]
+    ins = [hidden, *o_parts, vecs, bup, vecs, *packs]
     kernel = functools.partial(mlp_fwd_kernel, len(packs), last, prompt)
     return pl.pallas_call(
         strip(kernel, layer, len(ins), len(deps)),
@@ -208,14 +198,9 @@
             in_specs=[whole_spec((tok, D))]
             + [whole_spec((tok, 256))] * 4
             + vec_specs(layer)
-            + [ANY] * (2 * len(packs) + len(deps)),
+            + [ANY] * (len(packs) + len(deps)),
             out_specs=out_specs,
-            scratch_shapes=WSCR
-            + [
-                pltpu.VMEM((4, tok, D), BF16),
-                pltpu.VMEM((4, tok, D), BF16),
-                pltpu.SemaphoreType.DMA((2, 4)),
-            ],
+            scratch_shapes=WSCR,
         ),
         out_shape=shapes,
         compiler_params=params(44),
@@ -233,15 +218,14 @@
         rest = refs[4:nin]
         refs = refs[nin:]
     h1_ref, u_hbm, vec_ref, nvec_ref = refs[:4]
-    packs = [(refs[4 + 2 * k], refs[5 + 2 * k]) for k in range(ranks)]
-    outs = refs[4 + 2 * ranks :]
-    gm_ref, du_ref, a2_ref, g1_ref, go_ref, d0, d1, d2, d3, small_ref = outs[:10]
-    wout, wud, sems, u_ref, usem = outs[10:]
+    outs = refs[4 + ranks :]
+    tok_ref, mine_ref, theirs_ref, g1_ref, d0, d1, d2, d3, small_ref = outs[:9]
+    wout, wud, sems, u_ref, usem = outs[9:]
     loads = [pltpu.make_async_copy(u_hbm.at[s], u_ref.at[s], usem.at[s]) for s in range(4)]
-    start_weights(sc, packs, wout, wud, sems, False)
+    weights = Weights(sc, refs[4 : 4 + ranks], wout, wud, sems)
+    weights.start((1, 0))
     for copy in loads:
         copy.start()
-    waits = weight_copies(packs[0][0], packs[0][1], sc[4], wout, wud, sems)
     small_ref[...] = jnp.zeros_like(small_ref)
     if first:
         grad = g_ref[...]
@@ -255,10 +239,10 @@
         small_ref[9:10, :] = colsum(da1)
         grad = g_ref[...] + norm_back(da1, nvec_ref[0, 4:5, :], centered, inverse)
     gm = grad.astype(BF16)
-    gm_ref[...] = gm
+    tok_ref[1] = gm
     small_ref[4:5, :] = colsum(gm.astype(F32))
     for s in range(4):
-        waits[s][1].wait()
+        weights.wait(1, s)
         dm = nn(gm, wud[s, :, 768:1536])
         loads[s].wait()
         up = u_ref[s].astype(F32)
@@ -268,7 +252,9 @@
             GELU_COEF * (1.0 + 3.0 * 0.044715 * square)
         )
         du = (dm * slope).astype(BF16)
-        du_ref[s] = du
+        side = mine_ref if s % 2 == 0 else theirs_ref
+        side[s // 2] = du
+        side[2 + s // 2] = (0.5 * up * (1.0 + tanh)).astype(BF16)
         small_ref[s : s + 1, :] = colsum(du.astype(F32))
         term = nt(du, wud[s, :, 0:768])
         if s == 0:
@@ -278,16 +264,16 @@
     da2 = g1_ref[...]
     centered, inverse = stats(h1_ref[...])
     gain = vec_ref[0, 2:3, :]
-    a2_ref[...] = (centered * gain + vec_ref[0, 3:4, :]).astype(BF16)
+    tok_ref[0] = (centered * gain + vec_ref[0, 3:4, :]).astype(BF16)
     small_ref[6:7, :] = colsum(da2 * centered)
     small_ref[7:8, :] = colsum(da2)
     grad = grad + norm_back(da2, gain, centered, inverse)
     g1_ref[...] = grad
     go = grad.astype(BF16)
-    go_ref[...] = go
+    tok_ref[2] = go
     small_ref[5:6, :] = colsum(go.astype(F32))
     for s, ref in enumerate((d0, d1, d2, d3)):
-        waits[s][0].wait()
+        weights.wait(0, s)
         ref[...] = nn(go, wout[s]).astype(BF16)
 
 
@@ -295,19 +281,17 @@
     tok = grad.shape[0]
     first = back is None
     others = 0 if first else len(back[3])
-    small = jax.ShapeDtypeStruct((tok, D), BF16)
     shapes = [
-        small,
+        jax.ShapeDtypeStruct((3, tok, D), BF16),
         jax.ShapeDtypeStruct((4, tok, D), BF16),
-        small,
+        jax.ShapeDtypeStruct((4, tok, D), BF16),
         jax.ShapeDtypeStruct((tok, D), F32),
-        small,
     ]
     shapes += [jax.ShapeDtypeStruct((tok, 256), BF16)] * 4
     shapes += [jax.ShapeDtypeStruct((16, D), F32)]
     extra = [] if first else [back[0], back[1], back[2], *back[3]]
     specs = vec_specs(layer)
-    ins = [grad, *extra, h1, up, vecs, vecs, *[w for pair in packs for w in pair]]
+    ins = [grad, *extra, h1, up, vecs, vecs, *packs]
     kernel = functools.partial(mlp_bwd_kernel, len(packs), others // 2, first, prompt)
     return pl.pallas_call(
         strip(kernel, layer, len(ins), len(deps)),
@@ -315,8 +299,8 @@
             num_scalar_prefetch=1,
             grid=(1,),
             in_specs=[whole_spec(v.shape) for v in [grad, *extra, h1]]
-            + [HBM, specs[0], specs[2]]
-            + [ANY] * (2 * len(packs) + len(deps)),
+            + [ANY, specs[0], specs[2]]
+            + [ANY] * (len(packs) + len(deps)),
             out_specs=[whole_spec(s.shape) for s in shapes],
             scratch_shapes=WSCR + [pltpu.VMEM((4, tok, D), BF16), pltpu.SemaphoreType.DMA((4,))],
         ),
@@ -358,7 +342,7 @@
             kv_ref[0, base_b + at : base_b + at + piece, :] = low_kv[piece : 2 * piece]
     lanes = lax.broadcasted_iota(jnp.int32, (1, 128), 1)
     upper = lanes >= 64
-    sub = min(128, chunk)
+    sub = min(256, chunk)
 
     def begin(query, keys, mask):
         scores = nt(query, keys)
@@ -450,6 +434,7 @@
 
 
 def attn_fwd(layer, sc, own, oth, w_all, b_all, pos, dims, deps=()):
+    single = w_all.shape[0] == 1
     rows, piece, cpiece, chunk, cont = dims
     tok = own[0].shape[0]
     nq, nk = 2 * chunk + cont, 2 * chunk * rows + cont
@@ -474,7 +459,7 @@
             grid=(3,),
             in_specs=[whole_spec(v.shape) for v in [*own, *oth]]
             + [
-                pl.BlockSpec((1, D, 256), lambda i, sc: (sc[at], 0, i)),
+                pl.BlockSpec((1, D, 256), lambda i, sc: (0 if single else sc[at + 1], 0, i)),
                 pl.BlockSpec((1, 1, 256), lambda i, sc: (sc[at], 0, i)),
             ]
             + attn_inputs(pos)
@@ -500,9 +485,9 @@
     prow, pcol, crow, ccol, srow, scol = refs[13:19]
     outs = refs[19:]
     npc = 4 * rows
-    own_out, oth_out = outs[:4], outs[4:npc]
-    dq_out, dkv_out, bias_out = outs[npc : npc + 3]
-    do_s, drow, drowc, dq_s, dkv_s, da_s = outs[npc + 3 :]
+    mine_out, theirs_out = outs[:2]
+    dq_out, dkv_out, bias_out = outs[2:5]
+    do_s, drow, drowc, dq_s, dkv_s, da_s = outs[5:]
     head = pl.program_id(0)
     base_b = chunk * rows
     base_c = 2 * chunk * rows
@@ -549,7 +534,7 @@
         dkv_s[k_at, :] += nn(prob.astype(BF16), dout) + nn(dscore, query)
         dq_s[q_at, :] += tn(dscore, keys)
 
-    kb = min(256, chunk)
+    kb = min(512, chunk)
     at_a, at_b = pl.ds(0, chunk), pl.ds(chunk, chunk)
     lse_a, lse_b, dot_a, dot_b = lse_ref[0, 0], lse_ref[0, 1], drow[0], drow[1]
     for j in range(chunk // kb):
@@ -582,7 +567,7 @@
     def gather3(value, where):
         return jnp.concatenate([value[a : a + n] for a, n in where], axis=0)
 
-    def emit(slot, count, ref, term):
+    def emit(slot, count, ref, row, term):
         at = pl.ds(slot, count)
 
         def set_first():
@@ -592,7 +577,7 @@
             da_s[at, :] += term
 
         def finish():
-            ref[...] = (da_s[at, :] + term).astype(BF16)
+            ref[row : row + count, :] = (da_s[at, :] + term).astype(BF16)
 
         pl.when(head == 0)(set_first)
         pl.when(head == 1)(add_next)
@@ -614,7 +599,8 @@
         kv_sum = kv_sum + colsum(dkv.astype(F32))
         both = jnp.concatenate([dq, dkv], axis=1)
         dq_out[s, 0] = both
-        emit(s * tok, tok, own_out[s], nt(both, weight))
+        side = mine_out if s % 2 == 0 else theirs_out
+        emit(s * tok, tok, side, (s // 2) * tok, nt(both, weight))
     for t in range(1, rows):
         for s in range(4):
             at = t * chunk + s * piece
@@ -624,7 +610,9 @@
             kv_sum = kv_sum + colsum(dkv.astype(F32))
             k = (t - 1) * 4 + s
             dkv_out[k, 0] = dkv
-            emit(4 * tok + k * 2 * piece, 2 * piece, oth_out[k], nt(dkv, weight[:, 128:256]))
+            side = mine_out if s % 2 == 0 else theirs_out
+            row = 2 * tok + (k // 2) * 2 * piece
+            emit(4 * tok + k * 2 * piece, 2 * piece, side, row, nt(dkv, weight[:, 128:256]))
     bias_out[0] = jnp.broadcast_to(jnp.concatenate([q_sum, kv_sum], axis=1), (8, 256))
 
 
@@ -634,15 +622,14 @@
     nq, nk = 2 * chunk + cont, 2 * chunk * rows + cont
     noth = 4 * (rows - 1)
     shapes = (
-        [jax.ShapeDtypeStruct((tok, D), BF16)] * 4
-        + [jax.ShapeDtypeStruct((2 * piece, D), BF16)] * noth
+        [jax.ShapeDtypeStruct((2 * tok + noth * piece, D), BF16)] * 2
         + [
             jax.ShapeDtypeStruct((4, 3, tok, 256), BF16),
             jax.ShapeDtypeStruct((noth, 3, 2 * piece, 128), BF16),
             jax.ShapeDtypeStruct((3, 8, 256), F32),
         ]
     )
-    out_specs = [whole_spec(s.shape) for s in shapes[: 4 + noth]] + [
+    out_specs = [whole_spec(s.shape) for s in shapes[:2]] + [
         pl.BlockSpec((4, 1, tok, 256), lambda i, sc: (0, i, 0, 0)),
         pl.BlockSpec((noth, 1, 2 * piece, 128), lambda i, sc: (0, i, 0, 0)),
         pl.BlockSpec((1, 8, 256), lambda i, sc: (i, 0, 0)),
@@ -659,7 +646,7 @@
                 pl.BlockSpec((1, nk, 128), lambda i, sc: (i, 0, 0)),
                 pl.BlockSpec((1, 2, 1, chunk), lambda i, sc: (i, 0, 0, 0)),
                 pl.BlockSpec((1, 1, cont), lambda i, sc: (i, 0, 0)),
-                pl.BlockSpec((1, D, 256), lambda i, sc: (sc[at], 0, i)),
+                pl.BlockSpec((1, D, 256), lambda i, sc: (sc[at + 1], 0, i)),
             ]
             + attn_inputs(pos)
             + [ANY] * len(deps),
@@ -733,7 +720,7 @@
         grid_spec=pltpu.PrefetchScalarGridSpec(
             num_scalar_prefetch=1,
             grid=(3,),
-            in_specs=[HBM] * len(ins) + [ANY] * len(deps),
+            in_specs=[ANY] * len(ins) + [ANY] * len(deps),
             out_specs=[pl.BlockSpec((D, 256), lambda i, sc: (0, i)), whole_spec((8, 128))],
             scratch_shapes=[
                 pltpu.VMEM((4, tok, D), BF16),
@@ -748,120 +735,106 @@
             jax.ShapeDtypeStruct((D, D), BF16),
             jax.ShapeDtypeStruct((8, 128), F32),
         ],
-        compiler_params=params(40),
+        compiler_params=params(56),
         cost_estimate=cost(2 * 3 * D * (4 * tok * 256 + noth * two * 128), 10e6),
         name="dw_qkv",
     )(sc, *ins, *deps)
 
 
-def dw_terms(refs, scratch, act, sems, tile, first):
-    a2_h, gm_h, go_h, du_ref, act_h, o0, o1, o2, o3 = refs
-    a2, gm, go = scratch
-
-    def load(k, src, dst):
-        return pltpu.make_async_copy(src, dst, sems.at[k])
-
-    loads = [load(0, a2_h, a2), load(1, gm_h, gm), load(2, go_h, go)]
-
-    def tile_load(s):
-        return load(3 + s, act_h.at[s], act.at[s])
-
-    def begin():
-        for copy in loads:
-            copy.start()
-        for s in range(4):
-            tile_load(s).start()
-        for copy in loads:
-            copy.wait()
-
-    pl.when(first)(begin)
-    pl.when(tile == 0)(lambda: tile_load(0).wait())
-    for s in range(1, 4):
-        pl.when(tile == s)(lambda s=s: tile_load(s).wait())
-
-    def run(put):
-        for j in range(3):
-            put(j * 256, tn(a2[...], du_ref[0, :, j * 256 : (j + 1) * 256]))
-            put(768 + j * 256, tn(gm[...], act[tile, :, j * 256 : (j + 1) * 256]))
-        for s, ref in enumerate((o0, o1, o2, o3)):
-            pl.when(tile == s)(lambda ref=ref: put(1536, tn(go[...], ref[...])))
-
-    return run
+def dw_loads(refs, tok, side, outp, sems):
+    tok_m, tok_r, mine, got, o0, o2, r1, r3 = refs
+    size = tok_m.shape[1]
+    low, high = pl.ds(0, size), pl.ds(size, size)
+    pairs = [(tok_m, tok.at[:, low]), (tok_r, tok.at[:, high])]
+    pairs += [(mine, side.at[:, low]), (got, side.at[:, high])]
+    pairs += [(o0, outp.at[0, low]), (r1, outp.at[0, high])]
+    pairs += [(o2, outp.at[1, low]), (r3, outp.at[1, high])]
+    return [pltpu.make_async_copy(a, b, sems.at[k]) for k, (a, b) in enumerate(pairs)]
+
+
+def dw_products(tile, tok, side, outp, put):
+    for j in range(3):
+        cols = slice(j * 256, (j + 1) * 256)
+        put(j * 256, tn(tok[0], side[tile, :, cols]))
+        put(768 + j * 256, tn(tok[1], side[2 + tile, :, cols]))
+    put(1536, tn(tok[2], outp[tile]))
 
 
 def dw_mlp_kernel(sc, *refs):
-    old_ref, new_ref, token = refs[9:12]
-    a2, gm, go, act, sems = refs[12:]
+    old_ref, new_ref, token = refs[8:11]
+    tok, side, outp, sems = refs[11:]
     token[...] = jnp.zeros_like(token)
     tile = pl.program_id(0)
     keep = sc[6] == 0
-    run = dw_terms(refs[:9], (a2, gm, go), act, sems, tile, tile == 0)
+
+    def begin():
+        loads = dw_loads(refs[:8], tok, side, outp, sems)
+        for copy in loads:
+            copy.start()
+        for copy in loads:
+            copy.wait()
+
+    pl.when(tile == 0)(begin)
 
     def put(lo, value):
         size = value.shape[1]
         old = old_ref[0, 0, :, lo : lo + size].astype(F32)
         new_ref[0, 0, :, lo : lo + size] = (value + jnp.where(keep, old, 0.0)).astype(BF16)
 
-    run(put)
-
-
-def dw_specs(tok):
-    return (
-        [HBM] * 3
-        + [pl.BlockSpec((1, tok, D), lambda i, sc: (i, 0, 0)), HBM]
-        + [whole_spec((tok, 256))] * 4
-    )
+    dw_products(tile, tok, side, outp, put)
 
 
 def dw_scratch(tok):
-    return [pltpu.VMEM((tok, D), BF16)] * 3 + [
-        pltpu.VMEM((4, tok, D), BF16),
-        pltpu.SemaphoreType.DMA((7,)),
+    return [
+        pltpu.VMEM((3, 2 * tok, D), BF16),
+        pltpu.VMEM((4, 2 * tok, D), BF16),
+        pltpu.VMEM((2, 2 * tok, 256), BF16),
+        pltpu.SemaphoreType.DMA((8,)),
     ]
 
 
-def dw_mlp(layer, sc, a2, gm, go, du, act, o_parts, acc, deps=()):
-    tok = a2.shape[0]
+def dw_mlp(layer, sc, ins, acc, deps=()):
+    tok = ins[0].shape[1]
     at = layer * 8
     acc_spec = pl.BlockSpec((1, 1, D, PACK), lambda i, sc: (sc[at + 1], i, 0, 0))
-    ins = [a2, gm, go, du, act, *o_parts, acc]
     return pl.pallas_call(
-        strip(dw_mlp_kernel, layer, len(ins), len(deps)),
+        strip(dw_mlp_kernel, layer, 9, len(deps)),
         grid_spec=pltpu.PrefetchScalarGridSpec(
             num_scalar_prefetch=1,
-            grid=(4,),
-            in_specs=dw_specs(tok) + [acc_spec] + [ANY] * len(deps),
+            grid=(2,),
+            in_specs=[ANY] * 8 + [acc_spec] + [ANY] * len(deps),
             out_specs=[acc_spec, whole_spec((8, 128))],
             scratch_shapes=dw_scratch(tok),
         ),
         out_shape=[jax.ShapeDtypeStruct(acc.shape, acc.dtype), jax.ShapeDtypeStruct((8, 128), F32)],
-        input_output_aliases={len(ins): 0},
-        compiler_params=params(40),
-        cost_estimate=cost(2 * tok * D * 4 * PACK, 30e6),
+        input_output_aliases={9: 0},
+        compiler_params=params(56),
+        cost_estimate=cost(2 * tok * D * 4 * PACK, 20e6),
         name="dw_mlp",
-    )(sc, *ins, *deps)
-
-
-def dw_last_kernel(rank, sc, *refs):
-    send_ref, keep_ref, acc, token = refs[10:14]
-    a2, gm, go, act, sems, done, other, dsem, osem = refs[14:]
+    )(sc, *ins, acc, *deps)
+
+
+def dw_last_kernel(rank, groups, slot, sc, *refs):
+    keep_a, give_a, keep_b, give_b, acc, token = refs[9:15]
+    tok, side, outp, sems, done, other, dsem, osem, out_ref = refs[15:]
     token[...] = jnp.zeros_like(token)
-    step = pl.program_id(0)
-    tile = last_tile(step)
+    tile = pl.program_id(0)
     same = sc[1] == rank
     keep = sc[6] == 0
     used = jnp.logical_or(jnp.logical_not(same), keep)
 
-    def load(i):
-        return pltpu.make_async_copy(acc.at[rank, last_tile(i)], done.at[i % 2], dsem.at[i % 2])
-
-    def start_two():
-        load(0).start()
-        load(1).start()
-
-    pl.when(step == 0)(start_two)
-    run = dw_terms(refs[:9], (a2, gm, go), act, sems, tile, step == 0)
-    load(step).wait()
+    def load(t):
+        return pltpu.make_async_copy(acc.at[rank, t], done.at[t], dsem.at[t])
+
+    def begin():
+        loads = dw_loads(refs[:8], tok, side, outp, sems)
+        for copy in [*loads, load(0), load(1)]:
+            copy.start()
+        for copy in loads:
+            copy.wait()
+
+    pl.when(tile == 0)(begin)
+    load(tile).wait()
 
     def fetch_other():
         copy = pltpu.make_async_copy(acc.at[sc[1], tile], other, osem)
@@ -873,17 +846,8 @@
     def put(lo, value):
         size = value.shape[1]
         cols = slice(lo, lo + size)
-        old = jnp.where(used, done[step % 2, :, cols].astype(F32), 0.0)
-        total = (old + jnp.where(same, value, 0.0)).astype(BF16)
-
-        def to_send():
-            send_ref[0, :, cols] = total
-
-        def to_keep():
-            keep_ref[0, :, cols] = total
-
-        pl.when(step < 2)(to_send)
-        pl.when(step >= 2)(to_keep)
+        old = jnp.where(used, done[tile, :, cols].astype(F32), 0.0)
+        out_ref[:, cols] = (old + jnp.where(same, value, 0.0)).astype(BF16)
 
         def add_other():
             before = jnp.where(keep, other[:, cols].astype(F32), 0.0)
@@ -891,7 +855,7 @@
 
         pl.when(jnp.logical_not(same))(add_other)
 
-    run(put)
+    dw_products(tile, tok, side, outp, put)
 
     def store_other():
         copy = pltpu.make_async_copy(other, acc.at[sc[1], tile], osem)
@@ -899,45 +863,72 @@
         copy.wait()
 
     pl.when(jnp.logical_not(same))(store_other)
-    pl.when(step < 2)(lambda: load(step + 2).start())
-
-
-def last_tile(step):
-    return jnp.where(step < 2, 2 * step + 1, 2 * step - 4)
-
-
-def dw_last(layer, sc, a2, gm, go, du, act, o_parts, acc, deps=()):
-    tok = a2.shape[0]
-    ins = [a2, gm, go, du, act, *o_parts, acc]
-    specs = dw_specs(tok)
-    specs[3] = pl.BlockSpec((1, tok, D), lambda i, sc: (last_tile(i), 0, 0))
-    two = jax.ShapeDtypeStruct((2, D, PACK), BF16)
+    half = PACK // 2
+
+    def first_half(ref):
+        ref[...] = out_ref[:, 0:half]
+
+    pl.when(tile == 0)(functools.partial(first_half, keep_a))
+    pl.when(tile == 1)(functools.partial(first_half, give_a))
+    size = D // (2 * groups)
+    bit = sc[slot]
+    for g in range(groups):
+        for ref, part in ((keep_b, bit), (give_b, 1 - bit)):
+            src = pl.ds(pl.multiple_of((2 * g + part) * size, size), size)
+            dst = pl.ds(pl.multiple_of((tile * groups + g) * size, size), size)
+            ref[dst, :] = out_ref[src, half:]
+
+
+def dw_last(layer, sc, ins, acc, groups, deps=()):
+    tok = ins[0].shape[1]
+    slot = LAYERS * 8 + 1 + len(bits_of("dp")) - layer * 8
+    half = jax.ShapeDtypeStruct((D, PACK // 2), BF16)
     return pl.pallas_call(
-        strip(functools.partial(dw_last_kernel, layer), layer, len(ins), len(deps)),
+        strip(functools.partial(dw_last_kernel, layer, groups, slot), layer, 9, len(deps)),
         grid_spec=pltpu.PrefetchScalarGridSpec(
             num_scalar_prefetch=1,
-            grid=(4,),
-            in_specs=specs + [HBM] + [ANY] * len(deps),
-            out_specs=[
-                pl.BlockSpec((1, D, PACK), lambda i, sc: (jnp.minimum(i, 1), 0, 0)),
-                pl.BlockSpec((1, D, PACK), lambda i, sc: (jnp.maximum(i - 2, 0), 0, 0)),
-                HBM,
-                whole_spec((8, 128)),
-            ],
+            grid=(2,),
+            in_specs=[ANY] * 9 + [ANY] * len(deps),
+            out_specs=[whole_spec(half.shape)] * 4 + [ANY, whole_spec((8, 128))],
             scratch_shapes=dw_scratch(tok)
             + [
                 pltpu.VMEM((2, D, PACK), BF16),
                 pltpu.VMEM((D, PACK), BF16),
                 pltpu.SemaphoreType.DMA((2,)),
                 pltpu.SemaphoreType.DMA(()),
+                pltpu.VMEM((D, PACK), BF16),
             ],
         ),
-        out_shape=[two, two, jax.ShapeDtypeStruct(acc.shape, acc.dtype), jax.ShapeDtypeStruct((8, 128), F32)],
-        input_output_aliases={len(ins): 2},
-        compiler_params=params(52),
-        cost_estimate=cost(2 * tok * D * 4 * PACK, 30e6),
+        out_shape=[half] * 4
+        + [
+            jax.ShapeDtypeStruct(acc.shape, acc.dtype),
+            jax.ShapeDtypeStruct((8, 128), F32),
+        ],
+        input_output_aliases={9: 4},
+        compiler_params=params(56),
+        cost_estimate=cost(2 * tok * D * 4 * PACK, 20e6),
         name="dw_last",
-    )(sc, *ins, *deps)
+    )(sc, *ins, acc, *deps)
+
+
+def qkv_total(sc, rank, parts, groups, deps):
+    size = D // (2 * groups)
+    slot = LAYERS * 8 + 1 + len(bits_of("dp"))
+
+    def add(sc, *refs):
+        keep, give = refs[-2:]
+        bit = sc[slot]
+        for g in range(groups):
+            for out, side in ((keep, bit), (give, 1 - bit)):
+                at = pl.ds(pl.multiple_of((2 * g + side) * size, size), size)
+                total = jnp.zeros((size, D), F32)
+                for k, ref in enumerate(refs[:-2]):
+                    used = sc[(rank + k) * 8 + 1] == rank
+                    total = total + jnp.where(used, ref[at, :].astype(F32), 0.0)
+                out[g * size : (g + 1) * size, :] = total.astype(BF16)
+
+    shape = jax.ShapeDtypeStruct((D // 2, D), BF16)
+    return simple_call(add, sc, parts, [shape] * 2, name="qkv_total", deps=deps)
 
 
 def blank(shape, dtype):
@@ -1001,28 +992,27 @@
     return (a.astype(F32) + b.astype(F32)).astype(BF16)
 
 
-def add_kernel(refs_in, refs_out):
-    for k, out in enumerate(refs_out):
-        out[...] = add_low(refs_in[2 * k][...], refs_in[2 * k + 1][...])
-
-
-def add_pairs(pairs):
-    flat = [v for pair in pairs for v in pair]
-    count = len(flat)
-    return pl.pallas_call(
-        lambda *refs: add_kernel(refs[:count], refs[count:]),
-        out_shape=[jax.ShapeDtypeStruct(a.shape, a.dtype) for a, _ in pairs],
+def sum_kernel(sizes, a, b, *outs):
+    at = 0
+    for size, out in zip(sizes, outs):
+        out[...] = add_low(a[at : at + size, :], b[at : at + size, :])
+        at += size
+
+
+def collect(mine, theirs, tok, prompt, deps=()):
+    rows = lax.axis_size("row")
+    sizes = [tok, tok] + [prompt] * (2 * (rows - 1))
+    vmem = pl.BlockSpec(memory_space=pltpu.VMEM)
+    count = len(deps)
+    sums = pl.pallas_call(
+        lambda a, b, *refs: sum_kernel(sizes, a, b, *refs[count:]),
+        in_specs=[vmem] * 2 + [ANY] * count,
+        out_specs=[vmem] * len(sizes),
+        out_shape=[jax.ShapeDtypeStruct((n, D), BF16) for n in sizes],
         compiler_params=params(24),
         cost_estimate=cost(1e6, 4e6),
-        name="add_pairs",
-    )(*flat)
-
-
-def collect(own, oth):
-    rows = lax.axis_size("row")
-    pieces = [*own, *oth]
-    pairs = [(pieces[k], swap_core(pieces[k + 1])) for k in range(0, len(pieces), 2)]
-    sums = add_pairs(pairs)
+        name="sum_cores",
+    )(mine, swap_core(theirs), *deps)
     got = swap_x(sums[1])
     rest = []
     for t in range(1, rows):
@@ -1030,26 +1020,60 @@
     return sums[0], got, rest
 
 
-def pick_kernel(sc_at, sc, src, *rest):
-    out, sem = rest[-2:]
-    copy = pltpu.make_async_copy(src.at[sc[sc_at]], out, sem)
-    copy.start()
-    copy.wait()
-
-
-def pick(src, sc, at, deps=()):
+def behind(values, deps):
+    if not deps:
+        return list(values)
+    count = len(values)
+
+    def body(*refs):
+        del refs
+
     return pl.pallas_call(
-        functools.partial(pick_kernel, at),
-        grid_spec=pltpu.PrefetchScalarGridSpec(
-            num_scalar_prefetch=1,
-            grid=(1,),
-            in_specs=[ANY] * (1 + len(deps)),
-            out_specs=ANY,
-            scratch_shapes=[pltpu.SemaphoreType.DMA(())],
-        ),
-        out_shape=jax.ShapeDtypeStruct(src.shape[1:], src.dtype),
-        name="pick",
-    )(sc, src, *deps)
+        body,
+        in_specs=[ANY] * (count + len(deps)),
+        out_specs=[ANY] * count,
+        out_shape=[jax.ShapeDtypeStruct(v.shape, v.dtype) for v in values],
+        input_output_aliases={k: k for k in range(count)},
+        name="behind",
+    )(*values, *deps)
+
+
+def held(value, deps):
+    def body(src, *rest):
+        rest[-1][...] = src[...]
+
+    vmem = pl.BlockSpec(memory_space=pltpu.VMEM)
+    return pl.pallas_call(
+        body,
+        in_specs=[vmem] + [ANY] * len(deps),
+        out_specs=vmem,
+        out_shape=jax.ShapeDtypeStruct(value.shape, value.dtype),
+        name="held",
+    )(value, *deps)
+
+
+def gather_begin(value, names):
+    total = 1
+    for a in names:
+        total *= lax.axis_size(a)
+    return [lax.ppermute(value, names, [(i, i ^ t) for i in range(total)]) for t in range(1, total)]
+
+
+def gather_end(sc, pieces, index, ahead=(), deps=()):
+    lead, n, width = pieces[0].shape
+    count = len(pieces)
+
+    def place(sc, *refs):
+        out = refs[-1]
+        for block in refs[count:-1]:
+            out[0:1] = block[...]
+        base = len(ahead)
+        for t in range(count):
+            at = pl.ds(pl.multiple_of((sc[index] ^ t) * n, n), n)
+            out[base : base + lead, at, :] = refs[t][...]
+
+    shape = jax.ShapeDtypeStruct((lead + len(ahead), count * n, width), BF16)
+    return simple_call(place, sc, [*pieces, *ahead], [shape], name="place", deps=deps)[0]
 
 
 def zig(j, rows):
@@ -1102,23 +1126,28 @@
         ap_ref[...] = low[:prompt]
 
 
-def simple_call(kernel, sc, ins, shapes, specs=None, name="small"):
+def simple_call(kernel, sc, ins, shapes, specs=None, name="small", deps=()):
     return pl.pallas_call(
-        lambda sc_ref, *refs: kernel(Row(sc_ref, 0), *refs),
+        strip(kernel, 0, len(ins), len(deps)),
         grid_spec=pltpu.PrefetchScalarGridSpec(
             num_scalar_prefetch=1,
             grid=(1,),
-            in_specs=specs or [whole_spec(v.shape) for v in ins],
+            in_specs=(specs or [whole_spec(v.shape) for v in ins]) + [ANY] * len(deps),
             out_specs=[whole_spec(v.shape) for v in shapes],
         ),
         out_shape=shapes,
         compiler_params=params(24),
         cost_estimate=cost(1e6, 3e6),
         name=name,
-    )(sc, *ins)
+    )(sc, *ins, *deps)
 
 
 def enter(prompt, cont, sc, vecs, normed):
+    parts = enter_begin(prompt, cont, sc)
+    return parts, enter_end(exchange_heads(parts), sc, vecs, normed, prompt.shape[0] // 4)
+
+
+def enter_begin(prompt, cont, sc, deps=()):
     rows = lax.axis_size("row")
     half, width = prompt.shape[0] // 2, prompt.shape[1]
     piece, cpiece = half // 4, cont.shape[0] // 4
@@ -1130,33 +1159,51 @@
     odd = lax.ppermute(odd, "row", [(i, zig(2 * i + 1, rows)) for i in range(rows)])
     part = jax.ShapeDtypeStruct((tok, width), BF16)
     parts = simple_call(
-        functools.partial(split_kernel, piece, cpiece), sc, [even, odd, cont], [part] * 4, name="split"
+        functools.partial(split_kernel, piece, cpiece), sc, [even, odd, cont], [part] * 4, name="split", deps=deps
     )
-    parts = exchange_heads(parts)
+    return parts
+
+
+def enter_end(parts, sc, vecs, normed, prompt, deps=()):
+    tok, width = parts[0].shape
     shapes = [jax.ShapeDtypeStruct((tok, D), F32)]
     if normed:
-        shapes += [jax.ShapeDtypeStruct((tok, D), BF16), jax.ShapeDtypeStruct((2 * piece, D), BF16)]
+        shapes += [jax.ShapeDtypeStruct((tok, D), BF16), jax.ShapeDtypeStruct((prompt, D), BF16)]
     specs = [whole_spec((tok, width))] * 4 + [pl.BlockSpec((1, 8, D), lambda i, sc: (sc[0], 0, 0))]
     return simple_call(
-        functools.partial(join_kernel, 2 * piece, normed), sc, [*parts, vecs], shapes, specs, "join"
+        functools.partial(join_kernel, prompt, normed), sc, [*parts, vecs], shapes, specs, "join", deps
     )
 
 
 def leave(parts, sc, prompt_rows):
-    rows = lax.axis_size("row")
-    parts = exchange_heads(parts)
+    return leave_end(sc, *leave_begin(exchange_heads(parts), sc, prompt_rows))
+
+
+def leave_begin(parts, sc, prompt_rows, deps=()):
     width = parts[0].shape[1]
     half = prompt_rows // 2
     piece = half // 4
     cpiece = parts[0].shape[0] - 2 * piece
     shapes = [jax.ShapeDtypeStruct((n, width), BF16) for n in (half, half, 4 * cpiece)]
     even, odd, cont = simple_call(
-        functools.partial(merge_kernel, piece, cpiece), sc, parts, shapes, name="merge"
+        functools.partial(merge_kernel, piece, cpiece), sc, parts, shapes, name="merge", deps=deps
     )
+    return even, odd, cont
+
+
+def leave_end(sc, even, odd, cont, deps=()):
+    rows = lax.axis_size("row")
     if rows > 2:
         even = lax.ppermute(even, "row", [(zig(2 * i, rows), i) for i in range(rows)])
     odd = lax.ppermute(odd, "row", [(zig(2 * i + 1, rows), i) for i in range(rows)])
-    return jnp.concatenate([even, odd], axis=0)[None], cont[None]
+    half, width = even.shape
+
+    def stack(sc, first, second, out):
+        out[0, 0:half, :] = first[...]
+        out[0, half:, :] = second[...]
+
+    shape = jax.ShapeDtypeStruct((1, 2 * half, width), BF16)
+    return simple_call(stack, sc, [even, odd], [shape], name="rows", deps=deps)[0], cont[None]
 
 
 def final_kernel(prompt, others, sc, *refs):
@@ -1175,7 +1222,7 @@
     send_features(sc, out_ref, outs)
 
 
-def final_norm(sc, grad, back, vecs, prompt, width):
+def final_norm(sc, grad, back, vecs, prompt, width, deps):
     tok = grad.shape[0]
     h_in, base, got, rest = back
     ins = [grad, h_in, base, got, *rest, vecs]
@@ -1188,55 +1235,76 @@
         pl.BlockSpec((1, 8, D), lambda i, sc: (sc[0], 0, 0))
     ]
     return simple_call(
-        functools.partial(final_kernel, prompt, len(rest)), sc, ins, shapes, specs, "final_norm"
+        functools.partial(final_kernel, prompt, len(rest)), sc, ins, shapes, specs, "final_norm", deps
     )
 
 
 class Reduce:
 
-    def __init__(self, value, plan, out):
-        self.value, self.plan, self.out = value, list(plan), out
-        self.pending = None
-        self.send()
-
-    def halves(self, axis, bit):
-        where = {"dp": 0, "row": 1}[axis]
-        size = self.value.shape[where]
-        step = size // 2
-        shape = self.value.shape
-        split = self.value.reshape(shape[:where] + (2, step) + shape[where + 1 :])
-        mine = (lax.axis_index(axis) // bit) % 2
-        take = functools.partial(lax.dynamic_index_in_dim, split, axis=where, keepdims=False)
-        return take(mine), take(1 - mine)
-
-    def send(self):
+    def __init__(self, sc, keep, give, name, names, plan):
+        self.sc, self.keep, self.give = sc, keep, give
+        self.names, self.plan = list(names), list(plan)
+        self.ready, self.waiting = 0, None
+        self.send(name)
+
+    def send(self, name):
+        axis, bit = name
+        count = lax.axis_size(axis)
+        self.got = lax.ppermute(self.give, axis, [(i, i ^ bit) for i in range(count)])
+
+    def step(self, deps=(), hold=False):
+        rows, width = self.keep.shape
         if not self.plan:
-            return
-        axis, bit = self.plan.pop(0)
-        count = lax.axis_size(axis)
-        keep, send = self.halves(axis, bit)
-        got = lax.ppermute(send, axis, [(i, i ^ bit) for i in range(count)])
-        self.pending = (keep, got)
-
-    def step(self):
-        if self.pending is None:
-            return self.value
-        keep, got = self.pending
-        self.pending = None
-        total = keep.astype(F32) + got.astype(F32)
-        self.value = total if not self.plan else total.astype(BF16)
-        self.send()
-        return self.value
+            return []
+        name = self.plan.pop(0)
+        where = self.names.index(name)
+        self.names.pop(where)
+        before, size = 2**where, rows // 2 ** (where + 1)
+        if name[0] == "x":
+            slot = None
+        else:
+            slot = LAYERS * 8 + 1 + (bits_of("dp") + bits_of("row")).index(name)
+
+        def add(sc, keep, got, new_keep, new_give):
+            bit = 0 if slot is None else sc[slot]
+            for a in range(before):
+                for out, side in ((new_keep, bit), (new_give, 1 - bit)):
+                    lo = (2 * a + side) * size
+                    at = pl.ds(lo if slot is None else pl.multiple_of(lo, size), size)
+                    out[a * size : (a + 1) * size, :] = add_low(keep[at, :], got[at, :])
+
+        if size % 16:
+            total = add_low(self.keep, self.got).reshape(before, 2, size, width)
+            bit = 0 if slot is None else self.sc[slot]
+            self.keep, self.give = (
+                lax.dynamic_index_in_dim(total, side, 1, keepdims=False).reshape(rows // 2, width)
+                for side in (bit, 1 - bit)
+            )
+        else:
+            shape = jax.ShapeDtypeStruct((rows // 2, width), BF16)
+            self.keep, self.give = simple_call(
+                add, self.sc, [self.keep, self.got], [shape] * 2, name="add", deps=deps
+            )
+        if hold and name[0] != "dp":
+            self.waiting = name
+        else:
+            self.send(name)
+        return [self.give]
+
+    def release(self, deps):
+        if self.waiting is not None:
+            self.give = behind([self.give], deps)[0]
+            self.send(self.waiting)
+            self.waiting = None
 
     def finish(self):
-        while self.pending is not None:
+        while self.plan:
             self.step()
-        return self.value[0, 0].astype(F32)
+        return [self.keep, self.got]
 
 
 def bits_of(axis):
-    count = lax.axis_size(axis)
-    bits, bit = [], count // 2
+    bits, bit = [], lax.axis_size(axis) // 2
     while bit:
         bits.append((axis, bit))
         bit //= 2
@@ -1251,21 +1319,109 @@
     return value.reshape(shape)
 
 
+def narrow_kernel(width, sc, *refs):
+    smalls, qkvs, last_ref, out = refs[:LAYERS], refs[LAYERS : 2 * LAYERS], refs[2 * LAYERS], refs[-1]
+    out[...] = jnp.zeros_like(out)
+    for b in range(NB):
+        total = jnp.zeros((16, D), F32)
+        qkv = jnp.zeros((HEADS_COL, 256), F32)
+        for i in range(LAYERS):
+            mine = sc[i * 8] == b
+            total = total + jnp.where(mine, smalls[i][...], 0.0)
+            qkv = qkv + jnp.where(mine, qkvs[i][:, 0, :], 0.0)
+        gain = jnp.where(sc[0] == b, last_ref[0:2, :], 0.0)
+        for i in range(1, LAYERS):
+            gain = gain + jnp.where(sc[i * 8] == b, smalls[i - 1][8:10, :], 0.0)
+        rows = jnp.concatenate([total[5:6], total[4:5], total[6:8], gain], axis=0)
+        for s in range(4):
+            out[s, b, 0:1, :] = total[s : s + 1]
+            for c in range(4):
+
+                def put(s=s, b=b, c=c, rows=rows):
+                    out[s, b, 1:7, 0:width] = rows[:, c * width : (c + 1) * width]
+
+                pl.when((sc[3] ^ s) == c)(put)
+        for h in range(HEADS_COL):
+            out[0, b, 7:8, h * 256 : (h + 1) * 256] = qkv[h : h + 1]
+
+
+def end_slot():
+    return LAYERS * 8 + 1 + len(bits_of("dp")) + len(bits_of("row"))
+
+
+def pack_end(sc, parts, width):
+    slot = end_slot()
+    share = parts[0].shape[0]
+
+    def end(sc, *refs):
+        up, down, out = refs[-3:]
+        for k in range(NB):
+            ka, ga, kb, gb = refs[4 * k : 4 * k + 4]
+            left = ka[...].astype(F32) + ga[...].astype(F32)
+            right = kb[...].astype(F32) + gb[...].astype(F32)
+            for b in range(NB):
+
+                def put(b=b, left=left, right=right):
+                    up[b] = left[:, 0:D]
+                    down[b, :, 0 : 896 - D] = left[:, D:]
+                    down[b, :, 896 - D :] = right[:, 0 : 2 * D - 896]
+                    out[b] = right[:, 2 * D - 896 : 2 * D - 896 + width]
+
+                pl.when(sc[slot + b] == k)(put)
+
+    shapes = [jax.ShapeDtypeStruct((NB, share, n), F32) for n in (D, D, width)]
+    return simple_call(end, sc, parts, shapes, name="pack_end")
+
+
+def qkv_end(sc, parts, width):
+    slot = end_slot()
+    share = parts[0].shape[0]
+
+    def end(sc, *refs):
+        out = refs[-1]
+        for k in range(NB):
+            total = refs[2 * k][...].astype(F32) + refs[2 * k + 1][...].astype(F32)
+            for b in range(NB):
+
+                def put(b=b, total=total):
+                    for h in range(HEADS_COL):
+                        for j, lane in enumerate((0, 128, 192)):
+                            at = h * 256 + lane
+                            out[b, j, :, h * HD : (h + 1) * HD] = total[:, at : at + HD]
+
+                pl.when(sc[slot + b] == k)(put)
+
+    shape = jax.ShapeDtypeStruct((NB, 3, share, width), F32)
+    return simple_call(end, sc, parts, [shape], name="qkv_end")[0].transpose(0, 2, 1, 3)
+
+
+def narrow_end(sc, value, got, width):
+    def end(sc, value, got, bup, qv, *vecs):
+        for b in range(NB):
+            total = value[b] + got[b]
+            bup[b : b + 1, :] = total[0:1]
+            for k, out in enumerate(vecs):
+                out[b : b + 1, :] = total[1 + k : 2 + k, 0:width]
+            for h in range(HEADS_COL):
+                for j, lane in enumerate((0, 192)):
+                    at = h * 256 + lane
+                    qv[b, j : j + 1, h * HD : (h + 1) * HD] = total[7:8, at : at + HD]
+
+    shapes = [jax.ShapeDtypeStruct((NB, D), F32), jax.ShapeDtypeStruct((NB, 2, width), F32)]
+    shapes += [jax.ShapeDtypeStruct((NB, width), F32)] * 6
+    return simple_call(end, sc, [value, got], shapes, name="narrow_end")
+
+
 def sum_small(value):
-    rows, dps = lax.axis_size("row"), lax.axis_size("dp")
-    x, core = lax.axis_index("x"), lax.axis_index("core")
-    value = value.reshape(2, 2, -1)
-    take = lax.dynamic_index_in_dim
-    send = take(value, 1 - core, 1, keepdims=False)
-    value = take(value, core, 1, keepdims=False) + swap_core(send)
-    send = take(value, 1 - x, 0, keepdims=False)
-    value = take(value, x, 0, keepdims=False) + swap_x(send)
-    for axis, count in (("row", rows), ("dp", dps)):
-        bit = 1
-        while bit < count:
-            value = value + lax.ppermute(value, axis, [(i, i ^ bit) for i in range(count)])
-            bit *= 2
-    return value
+    got = swap_core(jnp.stack([value[1], value[3]]))
+    near, far = value[0] + got[0], value[2] + got[1]
+    value = near + swap_x(far)
+    steps = bits_of("row") + bits_of("dp")
+    for k, (axis, bit) in enumerate(steps):
+        got = lax.ppermute(value, axis, [(i, i ^ bit) for i in range(lax.axis_size(axis))])
+        if k + 1 < len(steps):
+            value = value + got
+    return value, got
 
 
 def per_device(
@@ -1300,28 +1456,39 @@
 
     layer_map = layer_map.astype(jnp.int32)
     places = jnp.arange(LAYERS, dtype=jnp.int32)
-    first_use = [jnp.min(jnp.where(layer_map == b, places, 99)) for b in range(NB)]
-    rank_of = [sum((first_use[o] < first_use[b]).astype(jnp.int32) for o in range(NB) if o != b) for b in range(NB)]
-    block_at = [sum(b * (rank_of[b] == k).astype(jnp.int32) for b in range(NB)) for k in range(NB)]
-    block_of = [layer_map[i] for i in range(LAYERS)]
-    rank_layer = [
-        sum(rank_of[b] * (block_of[i] == b).astype(jnp.int32) for b in range(NB)) for i in range(LAYERS)
-    ]
-
-    def scalars(layer):
-        fresh = jnp.int32(1)
-        for later in range(layer + 1, LAYERS):
-            fresh = fresh * (rank_layer[later] != rank_layer[layer]).astype(jnp.int32)
-        after = min(layer + 1, LAYERS - 1)
-        return [block_of[layer], rank_layer[layer], block_of[after], my_col, my_x, my_row, fresh, my_row % 2]
-
-    sc = jnp.stack([v for i in range(LAYERS) for v in scalars(i)] + block_at).astype(jnp.int32)
+    blocks = jnp.arange(NB, dtype=jnp.int32)
+    first_use = jnp.min(jnp.where(layer_map[None] == blocks[:, None], places[None], 99), axis=1)
+    rank_of = jnp.sum((first_use[None] < first_use[:, None]).astype(jnp.int32), axis=1)
+    rank_layer = jnp.sum(jnp.where(layer_map[:, None] == blocks[None], rank_of[None], 0), axis=1)
+    later = (rank_layer[None] == rank_layer[:, None]) & (places[None] > places[:, None])
+    fresh = 1 - jnp.max(later.astype(jnp.int32), axis=1)
+    after = jnp.concatenate([layer_map[1:], layer_map[-1:]])
+
+    def fill(value):
+        return jnp.broadcast_to(value, (LAYERS,)).astype(jnp.int32)
+
+    sc = jnp.stack(
+        [layer_map, rank_layer, after, fill(my_col), fill(my_x), fill(my_row), fresh, fill(my_row % 2)],
+        axis=1,
+    ).reshape(-1)
+    my_dp = lax.axis_index("dp")
+    extra = [my_dp * rows + my_row]
+    ends = [rank_of[b] for b in range(NB)]
+    extra += [(lax.axis_index(a) // b) % 2 for a, b in bits_of("dp") + bits_of("row")]
+    sc = jnp.concatenate([sc, jnp.stack(extra + ends).astype(jnp.int32)])
 
     heads = w_qkv.reshape(NB, -1, 3, HEADS_COL, HD)
     zero = jnp.zeros_like(heads[:, :, 0])
     packed = jnp.stack([heads[:, :, 0], zero, heads[:, :, 1], heads[:, :, 2]], axis=3)
     packed = packed.reshape(NB, -1, D)
-    wqkv_all = lax.all_gather(packed, ("dp", "row"), axis=1, tiled=True)
+
+    def by_block(stacked):
+        nothing = jnp.zeros((), stacked.dtype)
+        return [
+            sum(jnp.where(rank_of[b] == k, stacked[b], nothing) for b in range(NB)) for k in range(NB)
+        ]
+
+    packed = by_block(packed)
     pair = bias_qv.astype(F32).reshape(NB, 2, HEADS_COL, HD)
     none = jnp.zeros((NB, HEADS_COL, 2, HD), F32)
     bqkv = jnp.concatenate([pair[:, 0][:, :, None], none, pair[:, 1][:, :, None]], axis=2).reshape(NB, 1, D)
@@ -1341,11 +1508,14 @@
     pack_local = jnp.concatenate(
         [w_up, w_down, w_out, jnp.zeros(w_out.shape[:2] + (64,), BF16)], axis=2
     )
-
-    def gather_pack(k, deps):
-        local = pick(pack_local, sc, LAYERS * 8 + k, deps)
-        mine = lax.all_gather(local, ("x", "dp", "row"), axis=0, tiled=True).reshape(2, D, PACK)
-        return mine, swap_core(mine)
+    share = D // (dps * rows)
+    packs = []
+    for local in by_block(pack_local):
+        pack = lax.all_gather(local, ("x", "core", "dp", "row"), axis=0)
+        if share % 16:
+            packs.append(pack.reshape(4, 1, D, PACK))
+        else:
+            packs.append(pack.reshape(4, dps * rows, share, PACK))
 
     def places_of(size):
         index = jnp.arange(4 * size, dtype=jnp.int32)
@@ -1355,27 +1525,47 @@
     seg = reorder(seg_ids[0].astype(jnp.int32).reshape(4, cpiece)).reshape(cont)
     pos = [ppos[None], ppos[:, None], cpos[None], cpos[:, None], seg[None], seg[:, None]]
 
-    hidden, low, low_prompt = enter(x_prompt[0], x_cont[0], sc, vecs, True)
-    packs = [gather_pack(0, [wqkv_all])]
+    tok = prompt + cpiece
+    direct = dps * rows <= 8
+    parts, (hidden, low, low_prompt) = enter(x_prompt[0], x_cont[0], sc, vecs, True)
+    if direct:
+        first = held(packed[0][None], [parts[0]])
+        first = [first] + gather_begin(first, ("dp", "row"))
+        wqkv_first = gather_end(sc, first, LAYERS * 8, deps=[low])
+    else:
+        wqkv_all = lax.all_gather(jnp.stack(packed), ("dp", "row"), axis=1, tiled=True)
+        wqkv_first = wqkv_all
     saved = []
     for i in range(LAYERS):
         last = i == LAYERS - 1
         own, oth = spread(low, low_prompt)
-        res = attn_fwd(i, sc, own, oth, wqkv_all, bqkv, pos, dims)
+        if i == 1 and direct:
+            wqkv_all = gather_end(sc, rest, LAYERS * 8, [wqkv_first], deps=[low])
+        weight = wqkv_first if i == 0 else wqkv_all
+        res = attn_fwd(i, sc, own, oth, weight, bqkv, pos, dims)
         o_send, (q, kv, lse, lsec) = res[:4], res[4:]
-        if i + 1 < NB:
-            packs.append(gather_pack(i + 1, [lsec]))
+        if i == 0 and direct:
+            rest = held(jnp.stack(packed[1:]), [lsec])
+            rest = [rest] + gather_begin(rest, ("dp", "row"))
+        deps = []
+        if i == 2:
+            cot_parts = enter_begin(cot_prompt[0], cot_cont[0], sc, [lsec])
+            deps = [cot_parts[0]]
+        if i == 3:
+            grad = enter_end(cot_got, sc, vecs, False, prompt, [lsec])[0]
+            deps = [grad]
         o_got = exchange_heads(o_send)
         avail = packs[: min(i, NB - 1) + 1]
-        res = mlp_fwd(i, sc, hidden, o_got, vecs, bup, avail, prompt, last, width)
-        saved.append((hidden, own, oth, o_send, q, kv, lse, lsec, o_got, res[0], res[1], res[2]))
-        hidden = res[3]
+        res = mlp_fwd(i, sc, hidden, o_got, vecs, bup, avail, prompt, last, width, deps)
+        if i == 2:
+            cot_got = exchange_heads(cot_parts)
+        saved.append((hidden, own, oth, o_send, q, kv, lse, lsec, o_got, res[0], res[1]))
+        hidden = res[2]
         if not last:
-            low, low_prompt = res[4], res[5]
-    y_prompt, y_cont = leave(res[4:8], sc, prompt_row)
-
-    grad = enter(cot_prompt[0], cot_cont[0], sc, vecs, False)[0]
-    acc_pack = blank((NB, 4, D, PACK), BF16)
+            low, low_prompt = res[3], res[4]
+    y_send = exchange_heads(res[3:7])
+
+    acc_pack = blank((NB, 2, D, PACK), BF16)
     back = None
     small = [None] * LAYERS
     small_qkv = [None] * LAYERS
@@ -1383,92 +1573,94 @@
     done_pack = [None] * NB
     done_qkv = [None] * NB
     dws = [None] * LAYERS
-    steps = bits_of("row") + bits_of("dp")
+    dp_bits, row_bits = bits_of("dp"), bits_of("row")
+    bits = dp_bits + row_bits
+    top, x_bit = row_bits[0], ("x", 1)
     fence = []
-    sent = None
     for i in reversed(range(LAYERS)):
-        h_in, own, oth, o_send, q, kv, lse, lsec, o_got, h1, up, act = saved[i]
+        h_in, own, oth, o_send, q, kv, lse, lsec, o_got, h1, up = saved[i]
         res = mlp_bwd(i, sc, grad, back, h1, up, vecs, packs, prompt, fence)
-        gm, du, a2, grad, go = res[:5]
-        do_send, small[i] = res[5:9], res[9]
+        tokens, mine, theirs, grad = res[:4]
+        do_send, small[i] = res[4:8], res[8]
+        fence = []
+        for part in sums:
+            if part.ready <= 2 * (LAYERS - i):
+                fence += part.step([small[i]])
+        if i == LAYERS - 1:
+            y_parts = leave_begin(y_send, sc, prompt_row, [small[i]])
+            fence.append(y_parts[0])
+        *do_send, tokens, theirs = behind([*do_send, tokens, theirs], fence)
         do_got = exchange_heads(do_send)
+        ins = [tokens, swap_core(tokens), mine, swap_core(theirs)]
+        ins += [o_got[0], o_got[2], swap_core(o_got[1]), swap_core(o_got[3])]
         if i < NB:
-            send, keep, acc_pack, token = dw_last(i, sc, a2, gm, go, du, act, o_got, acc_pack)
-            sent = (keep, swap_core(send))
+            res = dw_last(i, sc, ins, acc_pack, dps, do_got[1:])
+            keep_a, give_a, keep_b, give_b, acc_pack, token = res
+            left = [n for n in bits if n != top]
+            done_pack[i] = [
+                Reduce(sc, keep_a, give_a, x_bit, bits, row_bits + dp_bits[::-1]),
+                Reduce(sc, keep_b, give_b, top, [x_bit] + left, [x_bit] + row_bits[1:] + dp_bits[::-1]),
+            ]
+            sums += done_pack[i]
+            fence = [token]
+            if i + 1 < NB:
+                fence += done_qkv[i + 1].step([token])
         else:
-            acc_pack, token = dw_mlp(i, sc, a2, gm, go, du, act, o_got, acc_pack)
-        res = attn_bwd(i, sc, do_got, o_send, q, kv, lse, lsec, wqkv_all, pos, dims, [token])
-        da_own, da_oth = res[:4], res[4 : 4 * rows]
-        dq, dkv, small_qkv[i] = res[4 * rows :]
-        base, got, rest = collect(da_own, da_oth)
-        dws[i], token = dw_qkv(i, sc, own, oth, dq, dkv)
+            fence = []
+        fence += [part.give for part in sums]
+        res = attn_bwd(i, sc, do_got, o_send, q, kv, lse, lsec, wqkv_all, pos, dims, fence)
+        da_mine, da_theirs, dq, dkv, small_qkv[i] = res
+        fence = []
+        for part in sums:
+            if part.ready <= 2 * (LAYERS - i) + 1:
+                fence += part.step([small_qkv[i]], i > 0)
+        if i == LAYERS - 1:
+            y_prompt, y_cont = leave_end(sc, *y_parts, deps=[small_qkv[i]])
+            fence.append(y_prompt)
+        if i > 0:
+            base, got, rest = collect(da_mine, behind([da_theirs], fence)[0], tok, prompt)
+            dws[i], token = dw_qkv(i, sc, own, oth, dq, dkv)
+        else:
+            dws[i], token = dw_qkv(i, sc, own, oth, dq, dkv, fence)
+            fence = []
+            for part in done_pack[0]:
+                fence += part.step([token])
+            base, got, rest = collect(da_mine, behind([da_theirs], fence)[0], tok, prompt)
         fence = [token]
+        if i >= NB:
+            acc_pack, token = dw_mlp(i, sc, ins, acc_pack, [base])
+            fence.append(token)
         for part in sums:
-            fence.append(part.step())
+            part.release([got, *rest])
         if i < NB:
-            keep, recv = sent
-            far = add_low(keep[1], recv[1])
-            near = (keep[0], recv[0], swap_x(far))
-            fence.append(far)
-            value = sum(
-                jnp.where(rank_layer[l] == i, dws[l].astype(F32), 0.0) for l in range(i, LAYERS)
-            )
-            shape = (dps, rows, D // (dps * rows), D)
-            done_qkv[i] = Reduce(value.astype(BF16).reshape(shape), steps, None)
+            keep, give = qkv_total(sc, i, dws[i:], dps, [got])
+            done_qkv[i] = Reduce(sc, keep, give, top, left, row_bits[1:] + dp_bits[::-1])
+            done_qkv[i].ready = 2 * (LAYERS - i) + 3
             sums.append(done_qkv[i])
-            done_pack[i] = near
+            fence.append(give)
         back = (h_in, base, got, rest)
-        if i + 1 < NB:
-            near = done_pack[i + 1]
-            value = (near[0].astype(F32) + near[1].astype(F32) + near[2].astype(F32)).astype(BF16)
-            shape = (dps, rows, D // (dps * rows), PACK)
-            done_pack[i + 1] = Reduce(value.reshape(shape), steps, None)
-            sums.append(done_pack[i + 1])
-            fence.append(value)
-
-    res = final_norm(sc, grad, back, vecs, prompt, width)
-    dx_prompt, dx_cont = leave(res[:4], sc, prompt_row)
-    last_gain, last_shift = res[4][0:1], res[4][1:2]
-    near = done_pack[0]
-    value = (near[0].astype(F32) + near[1].astype(F32) + near[2].astype(F32)).astype(BF16)
-    done_pack[0] = Reduce(value.reshape(dps, rows, D // (dps * rows), PACK), steps, None)
-    done_pack = [part.finish() for part in done_pack]
-    done_qkv = [part.finish() for part in done_qkv]
-
-    pieces = []
-    for i in range(LAYERS):
-        ups = reorder(small[i][0:4])
-        nxt = small[i - 1] if i > 0 else None
-        gain1 = last_gain if i == 0 else nxt[8:9]
-        shift1 = last_shift if i == 0 else nxt[9:10]
-        vec6 = jnp.concatenate([small[i][5:6], small[i][4:5], small[i][6:8], gain1, shift1], axis=0)
-        vec6 = vec6.reshape(6, 4, width).transpose(1, 0, 2).reshape(4, 6 * width)
-        sums = small_qkv[i][:, 0, :].reshape(HEADS_COL, 4, HD)
-        mine = jnp.concatenate([sums[:, 0].reshape(-1), sums[:, 3].reshape(-1)])
-        spot = (jnp.arange(4) == my_col)[:, None]
-        qv = jnp.where(spot, mine[None], 0.0)
-        pieces.append(jnp.concatenate([vec6, ups, qv], axis=1))
-    stacked = jnp.stack(pieces)
-    by_block = jnp.stack(
-        [
-            sum(jnp.where(block_of[i] == b, stacked[i], 0.0) for i in range(LAYERS))
-            for b in range(NB)
-        ],
-        axis=1,
-    )
-    mine = sum_small(by_block).reshape(NB, -1)
-    g_vec = mine[:, : 6 * width].reshape(NB, 6, width)
-    g_bup = mine[:, 6 * width : 6 * width + D]
-    g_qv = mine[:, 6 * width + D :].reshape(NB, 2, width)
-
-    def by_rank(parts):
-        return jnp.stack(
-            [sum(jnp.where(rank_of[b] == k, parts[k], 0.0) for k in range(NB)) for b in range(NB)]
-        )
-
-    g_pack = by_rank(done_pack)
-    g_heads = by_rank(done_qkv).reshape(NB, -1, HEADS_COL, 4, HD)
-    g_qkv = jnp.stack([g_heads[:, :, :, j].reshape(NB, -1, width) for j in (0, 2, 3)], axis=2)
+        sums = [part for part in sums if part.plan]
+
+    for part in sums:
+        if part.ready <= 2 * LAYERS + 2:
+            fence += part.step([got])
+    res = final_norm(sc, grad, back, vecs, prompt, width, fence)
+    dx_parts = leave_begin(exchange_heads(res[:4]), sc, prompt_row)
+    for part in sums:
+        part.step([dx_parts[0]])
+    dx_prompt, dx_cont = leave_end(sc, *dx_parts)
+    for part in sums:
+        part.step([dx_prompt])
+    for part in sums:
+        part.step()
+    g_up, g_down, g_out = pack_end(sc, [v for parts in done_pack for p in parts for v in p.finish()], width)
+    g_qkv = qkv_end(sc, [v for part in done_qkv for v in part.finish()], width)
+
+    shape = jax.ShapeDtypeStruct((4, NB, 8, D), F32)
+    narrow = simple_call(
+        functools.partial(narrow_kernel, width), sc, [*small, *small_qkv, res[4]], [shape], name="narrow"
+    )[0]
+    g_bup, g_qv, *g_vec = narrow_end(sc, *sum_small(narrow), width)
     return (
         y_prompt,
         y_cont,
@@ -1476,16 +1668,16 @@
         dx_cont,
         g_qkv,
         g_qv,
-        g_pack[:, :, 1536 : 1536 + width],
-        g_vec[:, 0],
-        g_pack[:, :, 0:768],
+        g_out,
+        g_vec[0],
+        g_up,
         g_bup,
-        g_pack[:, :, 768:1536],
-        g_vec[:, 1],
-        g_vec[:, 4],
-        g_vec[:, 5],
-        g_vec[:, 2],
-        g_vec[:, 3],
+        g_down,
+        g_vec[1],
+        g_vec[4],
+        g_vec[5],
+        g_vec[2],
+        g_vec[3],
     )
 
 

time: 1800 us -> 1390 us (0.77)
  waiting for transfers between devices: 660 us -> 401 us
  local copies, waits for them, and re-layouts: 190 us -> 121 us
  Pallas kernels: 717 us -> 650 us
  starting transfers between devices: 117 us -> 175 us
  other arithmetic: 61.4 us -> 7.35 us
    ppermute x12, waiting for transfers between devices: 181 us -> 51.4 us  [shift_row_x(): return lax.ppermute(value, ('row', 'x'), pairs)]
    all_gather x4 -> x3, waiting for transfers between devices: 127 us -> 12.6 us  [per_device(): pack = lax.all_gather(local, ('x', 'core', 'dp', 'row'), axis=0)]
    ppermute x16 -> x13, waiting for transfers between devices: 137 us -> 55 us  [swap_x(): return lax.ppermute(value, 'x', SWAP)]
    ppermute x25 -> x54, starting transfers between devices: 27.9 us -> 82.7 us  [the longest x14 36 us: gather_begin(): lax.ppermute(value, names, [(i, i ^ t) for i in range(total)])]
    convert_element_type x20 -> x0, other arithmetic: 44.6 us -> none  [the longest x12 16.2 us: step(): self.value = total if not self.plan else total.astype(BF16)]
    ppermute x25 -> x54, waiting for transfers between devices: 113 us -> 154 us  [the longest x14 100 us: gather_begin(): lax.ppermute(value, names, [(i, i ^ t) for i in range(total)])]
    pallas_call x6, Pallas kernels: 66.6 us -> 43.6 us  [mlp_fwd(): pl.pallas_call(strip(kernel, layer, len(ins), len(deps)), grid_spec=pltpu...]
    pallas_call x22 -> x67, Pallas kernels: 171 us -> 151 us  [the longest x3 54.1 us: dw_last(): pl.pallas_call(strip(functools.partial(dw_last_kernel, layer, groups, slo...]
  transfers between devices with their start and end apart: 175 -> 200, of which waited for: 86 -> 73; matrix products, arithmetic and copies ran while one was open for 8% -> 2% of each run, Pallas kernels for 23% -> 32%
where the time goes in v2:
time: 1390 us; the launch traced here: 1380 us
  Pallas kernels  650 us (47%)
  waiting for transfers between devices  401 us (29%)
  starting transfers between devices  175 us (13%)
  local copies, waits for them, and re-layouts  121 us (9%)
  between operations  24 us (2%)
    pallas_call x6, Pallas kernels, attn_bwd(): pl.pallas_call(strip(functools.partial(attn_bwd_kernel, dims), layer, 13...  181 us
    pallas_call x6, Pallas kernels, attn_fwd(): pl.pallas_call(strip(functools.partial(attn_fwd_kernel, dims), layer, cou...  132 us
    unnamed x808, local copies, waits for them, and re-layouts  109 us
    ppermute x14, waiting for transfers between devices, gather_begin(): lax.ppermute(value, names, [(i, i ^ t) for i in range(total)])  100 us
    pallas_call x6, Pallas kernels, mlp_bwd(): pl.pallas_call(strip(kernel, layer, len(ins), len(deps)), grid_spec=pltpu...  89.7 us
    ppermute x51, waiting for transfers between devices, exchange_heads(): out.append(lax.ppermute(parts[s], ('x', 'core'), pairs))  75.7 us
    ppermute x13, waiting for transfers between devices, swap_x(): return lax.ppermute(value, 'x', SWAP)  55 us
    pallas_call x3, Pallas kernels, dw_last(): pl.pallas_call(strip(functools.partial(dw_last_kernel, layer, groups, slo...  54.1 us
  transfers between devices with their start and end apart: 200, of which 73 were waited for; matrix products, arithmetic and copies ran while one was open for 2% of the time, Pallas kernels for 32%

profile of v2, /device:TPU:0, one launch (start us, length us, event | category | flops | bytes accessed | tf_op | source)
XLA Modules:
  0.0 1379.2 jit_solution(12318677715825764192)
XLA Ops:
  52.3 11.7 collective-permute-start.17
  104.4 21.8 %attn_fwd.6 = (bf16[288,256]{1,0:T(8,128)(2,1)S(1)}, bf16[288,256]{1,0:T(8,128)(2,1)S(1)}, bf16[288,256]{1,0:T(8,128)(2,1)S(1)}, bf16[288,256]{1,0:T(8,128)(2,1)...) custom-call(s32[55]{0:T(128)S(1)} %concatenate.19.sc, ...), custom_call_target="tpu_custom_call" | custom-call | flops 6568280064 | bytes 12000000 | tf_op jit(solution)/shard_map/attn_fwd/pallas_call | solution.py:455
  155.7 37.6 %collective-permute-done.35.refs_5_ = bf16[2,96,768]{2,1,0:T(8,128)(2,1)} collective-permute-done((bf16[2,96,768]{2,1,0:T(8,128)(2,1)}, bf16[2,96,768]{2,1,0:T(8,128)(2,1)}, u32[]{:S(2)}, u32[]{:S(2)}) %collective-permute-start.35) | collective-permute-done | bytes 294944 | tf_op jit(solution)/shard_map/ppermute | solution.py:1059
  195.9 11.6 collective-permute-done.34.refs_4_
  222.1 14.9 %collective-permute-done.31.refs_1_ = bf16[2,96,768]{2,1,0:T(8,128)(2,1)S(1)} collective-permute-done((bf16[2,96,768]{2,1,0:T(8,128)(2,1)S(1)}, bf16[2,96,768]{2,1,0:T(8,128)(2,1)S(1)}, u32[]{:S(2)}, u32[]{:S(2)}) %collective-permute-start.31) | collective-permute-done | bytes 294944 | tf_op jit(solution)/shard_map/ppermute | solution.py:1059
  242.6 22.0 %attn_fwd.7 = (bf16[288,256]{1,0:T(8,128)(2,1)S(1)}, bf16[288,256]{1,0:T(8,128)(2,1)S(1)}, bf16[288,256]{1,0:T(8,128)(2,1)S(1)}, bf16[288,256]{1,0:T(8,128)(2,1)...) custom-call(s32[55]{0:T(128)S(1)} %concatenate.19.sc, ...), custom_call_target="tpu_custom_call" | custom-call | flops 6568280064 | bytes 12000000 | tf_op jit(solution)/shard_map/attn_fwd/pallas_call | solution.py:455
  292.9 19.1 %collective-permute-done.42.refs_2_ = bf16[288,768]{1,0:T(8,128)(2,1)} collective-permute-done((bf16[288,768]{1,0:T(8,128)(2,1)}, bf16[288,768]{1,0:T(8,128)(2,1)}, u32[]{:S(2)}, u32[]{:S(2)}) %collective-permute-start.42) | collective-permute-done | bytes 442400 | tf_op jit(solution)/shard_map/ppermute | solution.py:954
  324.2 22.7 %attn_fwd.8 = (bf16[288,256]{1,0:T(8,128)(2,1)S(1)}, bf16[288,256]{1,0:T(8,128)(2,1)S(1)}, bf16[288,256]{1,0:T(8,128)(2,1)}, bf16[288,256]{1,0:T(8,128)(2,1)}, b...) custom-call(s32[55]{0:T(128)S(1)} %concatenate.19.sc, ...), custom_call_target="tpu_custom_call" | custom-call | flops 6568280064 | bytes 12000000 | tf_op jit(solution)/shard_map/attn_fwd/pallas_call | solution.py:455
  352.1 12.6 all-gather.8.cloned.1.call-done
  398.0 21.8 %attn_fwd.9 = (bf16[288,256]{1,0:T(8,128)(2,1)S(1)}, bf16[288,256]{1,0:T(8,128)(2,1)S(1)}, bf16[288,256]{1,0:T(8,128)(2,1)S(1)}, bf16[288,256]{1,0:T(8,128)(2,1)...) custom-call(s32[55]{0:T(128)S(1)} %concatenate.19.sc, ...), custom_call_target="tpu_custom_call" | custom-call | flops 6568280064 | bytes 12000000 | tf_op jit(solution)/shard_map/attn_fwd/pallas_call | solution.py:455
  469.9 22.0 %attn_fwd.10 = (bf16[288,256]{1,0:T(8,128)(2,1)S(1)}, bf16[288,256]{1,0:T(8,128)(2,1)S(1)}, bf16[288,256]{1,0:T(8,128)(2,1)S(1)}, bf16[288,256]{1,0:T(8,128)(2,1...) custom-call(s32[55]{0:T(128)S(1)} %concatenate.19.sc, ...), custom_call_target="tpu_custom_call" | custom-call | flops 6568280064 | bytes 12000000 | tf_op jit(solution)/shard_map/attn_fwd/pallas_call | solution.py:455
  534.1 21.8 %attn_fwd.11 = (bf16[288,256]{1,0:T(8,128)(2,1)S(1)}, bf16[288,256]{1,0:T(8,128)(2,1)S(1)}, bf16[288,256]{1,0:T(8,128)(2,1)S(1)}, bf16[288,256]{1,0:T(8,128)(2,1...) custom-call(s32[55]{0:T(128)S(1)} %concatenate.19.sc, ...), custom_call_target="tpu_custom_call" | custom-call | flops 6568280064 | bytes 12000000 | tf_op jit(solution)/shard_map/attn_fwd/pallas_call | solution.py:455
  577.9 14.1 %mlp_bwd.6 = (bf16[3,288,768]{2,1,0:T(8,128)(2,1)S(1)}, bf16[4,288,768]{2,1,0:T(8,128)(2,1)}, bf16[4,288,768]{2,1,0:T(8,128)(2,1)}, f32[288,768]{1,0:T(8,128)S(1...) custom-call(s32[55]{0:T(128)S(1)} %concatenate.19.sc, ...), custom_call_target="tpu_custom_call" | custom-call | flops 3057647616 | bytes 16000000 | tf_op jit(solution)/shard_map/mlp_bwd/pallas_call | solution.py:296
  605.6 30.0 %attn_bwd.6 = (bf16[1088,768]{1,0:T(8,128)(2,1)}, bf16[1088,768]{1,0:T(8,128)(2,1)}, bf16[4,3,288,256]{3,2,1,0:T(8,128)(2,1)}, bf16[4,3,256,128]{3,2,1,0:T(8,128)(2,1)}, f32[3,8,256]{2,1,0:T(8,128)}) custom-call(s32[55]{0:T(128)} %copy-done.39, bf16[288,256]{1,0:T(8,128)(2,1)} %get-tuple-element.411.refs_0_, bf16[288,256]{1,0:T(8,128)(2,1)} %copy-done.388, ...), custom_call_target="tpu_custom_call" | custom-call | flops 12343836672 | bytes 14000000 | tf_op jit(solution)/shard_map/attn_bwd/pallas_call | solution.py:638
  658.6 12.2 dw_mlp.3
  671.6 14.7 %mlp_bwd.7 = (bf16[3,288,768]{2,1,0:T(8,128)(2,1)}, bf16[4,288,768]{2,1,0:T(8,128)(2,1)}, bf16[4,288,768]{2,1,0:T(8,128)(2,1)}, f32[288,768]{1,0:T(8,128)S(1)}, ...) custom-call(s32[55]{0:T(128)S(1)} %copy-done.41, ...), custom_call_target="tpu_custom_call" | custom-call | flops 3057647616 | bytes 16000000 | tf_op jit(solution)/shard_map/mlp_bwd/pallas_call | solution.py:296
  696.7 30.2 %attn_bwd.7 = (bf16[1088,768]{1,0:T(8,128)(2,1)}, bf16[1088,768]{1,0:T(8,128)(2,1)}, bf16[4,3,288,256]{3,2,1,0:T(8,128)(2,1)}, bf16[4,3,256,128]{3,2,1,0:T(8,128)(2,1)}, f32[3,8,256]{2,1,0:T(8,128)}) custom-call(s32[55]{0:T(128)} %copy-done.39, bf16[288,256]{1,0:T(8,128)(2,1)} %copy-done.312, bf16[288,256]{1,0:T(8,128)(2,1)} %copy-done.390, ...), custom_call_target="tpu_custom_call" | custom-call | flops 12343836672 | bytes 14000000 | tf_op jit(solution)/shard_map/attn_bwd/pallas_call | solution.py:638
  746.6 12.5 dw_mlp.4
  759.9 14.6 %mlp_bwd.8 = (bf16[3,288,768]{2,1,0:T(8,128)(2,1)}, bf16[4,288,768]{2,1,0:T(8,128)(2,1)}, bf16[4,288,768]{2,1,0:T(8,128)(2,1)}, f32[288,768]{1,0:T(8,128)S(1)}, ...) custom-call(s32[55]{0:T(128)S(1)} %copy-done.42, ...), custom_call_target="tpu_custom_call" | custom-call | flops 3057647616 | bytes 16000000 | tf_op jit(solution)/shard_map/mlp_bwd/pallas_call | solution.py:296
  785.5 30.2 %attn_bwd.8 = (bf16[1088,768]{1,0:T(8,128)(2,1)}, bf16[1088,768]{1,0:T(8,128)(2,1)}, bf16[4,3,288,256]{3,2,1,0:T(8,128)(2,1)}, bf16[4,3,256,128]{3,2,1,0:T(8,128)(2,1)}, f32[3,8,256]{2,1,0:T(8,128)}) custom-call(s32[55]{0:T(128)} %copy-done.39, bf16[288,256]{1,0:T(8,128)(2,1)} %copy-done.313, bf16[288,256]{1,0:T(8,128)(2,1)} %copy-done.391, ...), custom_call_target="tpu_custom_call" | custom-call | flops 12343836672 | bytes 14000000 | tf_op jit(solution)/shard_map/attn_bwd/pallas_call | solution.py:638
  835.5 12.5 dw_mlp.5
  848.8 14.6 %mlp_bwd.9 = (bf16[3,288,768]{2,1,0:T(8,128)(2,1)}, bf16[4,288,768]{2,1,0:T(8,128)(2,1)}, bf16[4,288,768]{2,1,0:T(8,128)(2,1)}, f32[288,768]{1,0:T(8,128)S(1)}, ...) custom-call(s32[55]{0:T(128)S(1)} %copy-done.43, ...), custom_call_target="tpu_custom_call" | custom-call | flops 3057647616 | bytes 16000000 | tf_op jit(solution)/shard_map/mlp_bwd/pallas_call | solution.py:296
  879.1 18.0 %dw_last.3 = (bf16[768,896]{1,0:T(8,128)(2,1)}, bf16[768,896]{1,0:T(8,128)(2,1)}, bf16[768,896]{1,0:T(8,128)(2,1)}, bf16[768,896]{1,0:T(8,128)(2,1)}, bf16[3,2,7...) custom-call(s32[55]{0:T(128)} %copy-done.39, ...), custom_call_target="tpu_custom_call", output_to_operand_aliasing={{4}: (9, {})} | custom-call | flops 3170893824 | bytes 20000000 | tf_op jit(solution)/shard_map/dw_last/pallas_call | solution.py:886
  900.5 30.2 %attn_bwd.9 = (bf16[1088,768]{1,0:T(8,128)(2,1)}, bf16[1088,768]{1,0:T(8,128)(2,1)}, bf16[4,3,288,256]{3,2,1,0:T(8,128)(2,1)}, bf16[4,3,256,128]{3,2,1,0:T(8,128)(2,1)}, f32[3,8,256]{2,1,0:T(8,128)}) custom-call(s32[55]{0:T(128)} %copy-done.39, bf16[288,256]{1,0:T(8,128)(2,1)} %copy-done.309, bf16[288,256]{1,0:T(8,128)(2,1)} %copy-done.344, ...), custom_call_target="tpu_custom_call" | custom-call | flops 12343836672 | bytes 14000000 | tf_op jit(solution)/shard_map/attn_bwd/pallas_call | solution.py:638
  978.3 15.7 %mlp_bwd.10 = (bf16[3,288,768]{2,1,0:T(8,128)(2,1)}, bf16[4,288,768]{2,1,0:T(8,128)(2,1)}, bf16[4,288,768]{2,1,0:T(8,128)(2,1)}, f32[288,768]{1,0:T(8,128)S(1)},...) custom-call(s32[55]{0:T(128)S(1)} %copy-done.45, ...), custom_call_target="tpu_custom_call" | custom-call | flops 3057647616 | bytes 16000000 | tf_op jit(solution)/shard_map/mlp_bwd/pallas_call | solution.py:296
  1014.9 18.1 %dw_last.4 = (bf16[768,896]{1,0:T(8,128)(2,1)}, bf16[768,896]{1,0:T(8,128)(2,1)}, bf16[768,896]{1,0:T(8,128)(2,1)}, bf16[768,896]{1,0:T(8,128)(2,1)}, bf16[3,2,7...) custom-call(s32[55]{0:T(128)} %copy-done.39, ...), custom_call_target="tpu_custom_call", output_to_operand_aliasing={{4}: (9, {})} | custom-call | flops 3170893824 | bytes 20000000 | tf_op jit(solution)/shard_map/dw_last/pallas_call | solution.py:886
  1043.1 30.2 %attn_bwd.10 = (bf16[1088,768]{1,0:T(8,128)(2,1)}, bf16[1088,768]{1,0:T(8,128)(2,1)}, bf16[4,3,288,256]{3,2,1,0:T(8,128)(2,1)}, bf16[4,3,256,128]{3,2,1,0:T(8,128)(2,1)}, f32[3,8,256]{2,1,0:T(8,128)}) custom-call(s32[55]{0:T(128)} %copy-done.39, bf16[288,256]{1,0:T(8,128)(2,1)} %get-tuple-element.534.refs_0_, bf16[288,256]{1,0:T(8,128)(2,1)} %copy-done.338, ...), custom_call_target="tpu_custom_call" | custom-call | flops 12343836672 | bytes 14000000 | tf_op jit(solution)/shard_map/attn_bwd/pallas_call | solution.py:638
  1124.4 15.9 %mlp_bwd.11 = (bf16[3,288,768]{2,1,0:T(8,128)(2,1)}, bf16[4,288,768]{2,1,0:T(8,128)(2,1)}, bf16[4,288,768]{2,1,0:T(8,128)(2,1)}, f32[288,768]{1,0:T(8,128)S(1)},...) custom-call(s32[55]{0:T(128)S(1)} %copy-done.48, ...), custom_call_target="tpu_custom_call" | custom-call | flops 3057647616 | bytes 16000000 | tf_op jit(solution)/shard_map/mlp_bwd/pallas_call | solution.py:296
  1164.0 18.1 %dw_last.5 = (bf16[768,896]{1,0:T(8,128)(2,1)}, bf16[768,896]{1,0:T(8,128)(2,1)}, bf16[768,896]{1,0:T(8,128)(2,1)}, bf16[768,896]{1,0:T(8,128)(2,1)}, bf16[3,2,7...) custom-call(s32[55]{0:T(128)} %copy-done.39, ...), custom_call_target="tpu_custom_call", output_to_operand_aliasing={{4}: (9, {})} | custom-call | flops 3170893824 | bytes 20000000 | tf_op jit(solution)/shard_map/dw_last/pallas_call | solution.py:886
  1186.9 30.1 %attn_bwd.11 = (bf16[1088,768]{1,0:T(8,128)(2,1)}, bf16[1088,768]{1,0:T(8,128)(2,1)}, bf16[4,3,288,256]{3,2,1,0:T(8,128)(2,1)}, bf16[4,3,256,128]{3,2,1,0:T(8,128)(2,1)}, f32[3,8,256]{2,1,0:T(8,128)}) custom-call(s32[55]{0:T(128)} %copy-done.39, bf16[288,256]{1,0:T(8,128)(2,1)} %get-tuple-element.587.refs_0_, bf16[288,256]{1,0:T(8,128)(2,1)} %copy-done.339, ...), custom_call_target="tpu_custom_call" | custom-call | flops 12343836672 | bytes 14000000 | tf_op jit(solution)/shard_map/attn_bwd/pallas_call | solution.py:638
  1318.0 15.2 %collective-permute-done.182.refs_1_ = bf16[192,768]{1,0:T(8,128)(2,1)S(1)} collective-permute-done((bf16[192,768]{1,0:T(8,128)(2,1)S(1)}, bf16[192,768]{1,0:T(8,128)(2,1)S(1)}, u32[]{:S(2)}, u32[]{:S(2)}) %collective-permute-start.182) | collective-permute-done | bytes 294944 | tf_op jit(solution)/shard_map/ppermute | solution.py:1253
  1339.3 10.9 collective-permute-done.189
  (1345 shorter events, 727.6 us)
Async XLA Ops:
  7.2 133.9 %all-gather.4.cloned.1.call-start = ((), (), s32[]{:S(2)}) async-start(), calls=%async_computation | async-start | bytes 11354112 | tf_op jit(solution)/shard_map/all_gather | solution.py:1514
  18.0 251.8 %all-gather.6.cloned.1.call-start = ((), (), s32[]{:S(2)}) async-start(), calls=%async_computation.1 | async-start | bytes 11354112 | tf_op jit(solution)/shard_map/all_gather | solution.py:1514
  18.7 345.9 %all-gather.8.cloned.1.call-start = ((), (), s32[]{:S(2)}) async-start(), calls=%async_computation.2 | async-start | bytes 11354112 | tf_op jit(solution)/shard_map/all_gather | solution.py:1514
  45.8 39.0 %collective-permute-start.12 = (bf16[256,768]{1,0:T(8,128)(2,1)S(1)}, bf16[256,768]{1,0:T(8,128)(2,1)}, u32[]{:S(2)}, u32[]{:S(2)}) collective-permute-start(bf16[256,768]{1,0:T(8,128)(2,1)S(1)} %get-tuple-element.349), channel_id=1, source_target_pairs={{0,6},{2,4},{4,2},{6,0},{1,7},{3,5},{5,3},{7,1},{8,14},{10,12},{12... | collective-permute-start | bytes 1179656 | tf_op jit(solution)/shard_map/ppermute | solution.py:965
  48.6 36.6 %collective-permute-start.10 = (bf16[256,768]{1,0:T(8,128)(2,1)S(1)}, bf16[256,768]{1,0:T(8,128)(2,1)S(1)}, u32[]{:S(2)}, u32[]{:S(2)}) collective-permute-start(bf16[256,768]{1,0:T(8,128)(2,1)S(1)} %get-tuple-element.349), channel_id=1, source_target_pairs={{0,4},{4,0},{1,5},{5,1},{2,6},{6,2},{3,7},{7,3},{8,12},{12,8},{9,1... | collective-permute-start | bytes 1179656 | tf_op jit(solution)/shard_map/ppermute | solution.py:959
  48.8 36.5 %collective-permute-start.8 = (bf16[288,768]{1,0:T(8,128)(2,1)S(1)}, bf16[288,768]{1,0:T(8,128)(2,1)}, u32[]{:S(2)}, u32[]{:S(2)}) collective-permute-start(bf16[288,768]{1,0:T(8,128)(2,1)S(1)} %get-tuple-element.348.refs_8_.refs_0_), channel_id=1, source_target_pairs={{0,2},{2,0},{1,3},{3,1},{4,6},{6,4},{5,7},{7,5},{8,10},{10,8},{9,1... | collective-permute-start | bytes 1327112 | tf_op jit(solution)/shard_map/ppermute | solution.py:954
  136.1 57.2 %collective-permute-start.35 = (bf16[2,96,768]{2,1,0:T(8,128)(2,1)}, bf16[2,96,768]{2,1,0:T(8,128)(2,1)}, u32[]{:S(2)}, u32[]{:S(2)}) collective-permute-start(bf16[2,96,768]{2,1,0:T(8,128)(2,1)} %held.3.refs_0_), channel_id=1, source_target_pairs={{0,20},{4,16},{8,28},{12,24},{16,4},{20,0},{24,12},{28,8},{1,21},{... | collective-permute-start | bytes 884744 | tf_op jit(solution)/shard_map/ppermute | solution.py:1059
  137.0 70.4 %collective-permute-start.34 = (bf16[2,96,768]{2,1,0:T(8,128)(2,1)}, bf16[2,96,768]{2,1,0:T(8,128)(2,1)}, u32[]{:S(2)}, u32[]{:S(2)}) collective-permute-start(bf16[2,96,768]{2,1,0:T(8,128)(2,1)} %held.3.refs_0_), channel_id=1, source_target_pairs={{0,16},{4,20},{8,24},{12,28},{16,0},{20,4},{24,8},{28,12},{1,17},{... | collective-permute-start | bytes 884744 | tf_op jit(solution)/shard_map/ppermute | solution.py:1059
  152.2 62.5 %collective-permute-start.25 = (bf16[288,768]{1,0:T(8,128)(2,1)S(1)}, bf16[288,768]{1,0:T(8,128)(2,1)S(1)}, u32[]{:S(2)}, u32[]{:S(2)}) collective-permute-start(bf16[288,768]{1,0:T(8,128)(2,1)S(1)} %get-tuple-element.355.refs_9_.refs_0_), channel_id=1, source_target_pairs={{0,2},{2,0},{1,3},{3,1},{4,6},{6,4},{5,7},{7,5},{8,10},{10,8},{9,1... | collective-permute-start | bytes 1327112 | tf_op jit(solution)/shard_map/ppermute | solution.py:954
  153.9 61.2 %collective-permute-start.29 = (bf16[256,768]{1,0:T(8,128)(2,1)S(1)}, bf16[256,768]{1,0:T(8,128)(2,1)S(1)}, u32[]{:S(2)}, u32[]{:S(2)}) collective-permute-start(bf16[256,768]{1,0:T(8,128)(2,1)S(1)} %get-tuple-element.356), channel_id=1, source_target_pairs={{0,6},{2,4},{4,2},{6,0},{1,7},{3,5},{5,3},{7,1},{8,14},{10,12},{12... | collective-permute-start | bytes 1179656 | tf_op jit(solution)/shard_map/ppermute | solution.py:965
  153.9 61.3 %collective-permute-start.27 = (bf16[256,768]{1,0:T(8,128)(2,1)S(1)}, bf16[256,768]{1,0:T(8,128)(2,1)S(1)}, u32[]{:S(2)}, u32[]{:S(2)}) collective-permute-start(bf16[256,768]{1,0:T(8,128)(2,1)S(1)} %get-tuple-element.356), channel_id=1, source_target_pairs={{0,4},{4,0},{1,5},{5,1},{2,6},{6,2},{3,7},{7,3},{8,12},{12,8},{9,1... | collective-permute-start | bytes 1179656 | tf_op jit(solution)/shard_map/ppermute | solution.py:959
  292.9 31.2 %collective-permute-start.41 = (bf16[288,768]{1,0:T(8,128)(2,1)}, bf16[288,768]{1,0:T(8,128)(2,1)}, u32[]{:S(2)}, u32[]{:S(2)}) collective-permute-start(bf16[288,768]{1,0:T(8,128)(2,1)} %get-tuple-element.363.refs_0_), channel_id=1, source_target_pairs={{0,1},{1,0},{2,3},{3,2},{4,5},{5,4},{6,7},{7,6},{8,9},{9,8},{10,11... | collective-permute-start | bytes 1327112 | tf_op jit(solution)/shard_map/ppermute | solution.py:950
  598.1 37.5 %collective-permute-start.88 = (bf16[512,192]{1,0:T(8,128)(2,1)S(1)}, bf16[512,192]{1,0:T(8,128)(2,1)S(1)}, u32[]{:S(2)}, u32[]{:S(2)}) collective-permute-start(bf16[512,192]{1,0:T(8,128)(2,1)S(1)} %get-tuple-element.404), channel_id=1, source_target_pairs={{4,0},{0,4},{5,1},{1,5},{6,2},{2,6},{7,3},{3,7},{12,8},{8,12},{13,... | collective-permute-start | bytes 589832 | tf_op jit(solution)/shard_map/ppermute | solution.py:1198
  897.1 33.7 %collective-permute-start.130 = (bf16[768,896]{1,0:T(8,128)(2,1)}, bf16[768,896]{1,0:T(8,128)(2,1)S(1)}, u32[]{:S(2)}, u32[]{:S(2)}) collective-permute-start(bf16[768,896]{1,0:T(8,128)(2,1)} %get-tuple-element.500.refs_21_), channel_id=1, source_target_pairs={{0,4},{4,0},{1,5},{5,1},{2,6},{6,2},{3,7},{7,3},{8,12},{12,8},{9,1... | collective-permute-start | bytes 4128776 | tf_op jit(solution)/shard_map/ppermute | solution.py:1253
  898.9 34.4 %collective-permute-start.129 = (bf16[768,896]{1,0:T(8,128)(2,1)}, bf16[768,896]{1,0:T(8,128)(2,1)S(1)}, u32[]{:S(2)}, u32[]{:S(2)}) collective-permute-start(bf16[768,896]{1,0:T(8,128)(2,1)} %get-tuple-element.499.refs_20_), channel_id=1, source_target_pairs={{0,2},{2,0},{1,3},{3,1},{4,6},{6,4},{5,7},{7,5},{8,10},{10,8},{9,1... | collective-permute-start | bytes 4128776 | tf_op jit(solution)/shard_map/ppermute | solution.py:1253
  962.6 32.1 %collective-permute-start.136 = (bf16[384,896]{1,0:T(8,128)(2,1)}, bf16[384,896]{1,0:T(8,128)(2,1)}, u32[]{:S(2)}, u32[]{:S(2)}) collective-permute-start(bf16[384,896]{1,0:T(8,128)(2,1)} %behind.15), channel_id=1, source_target_pairs={{0,2},{2,0},{1,3},{3,1},{4,6},{6,4},{5,7},{7,5},{8,10},{10,8},{9,1... | collective-permute-start | bytes 2064392 | tf_op jit(solution)/shard_map/ppermute | solution.py:1253
  964.2 33.1 %collective-permute-start.135 = (bf16[384,896]{1,0:T(8,128)(2,1)}, bf16[384,896]{1,0:T(8,128)(2,1)}, u32[]{:S(2)}, u32[]{:S(2)}) collective-permute-start(bf16[384,896]{1,0:T(8,128)(2,1)} %behind.14), channel_id=1, source_target_pairs={{0,4},{4,0},{1,5},{5,1},{2,6},{6,2},{3,7},{7,3},{8,12},{12,8},{9,1... | collective-permute-start | bytes 2064392 | tf_op jit(solution)/shard_map/ppermute | solution.py:1253
  1007.1 31.3 %collective-permute-start.144 = (bf16[384,768]{1,0:T(8,128)(2,1)}, bf16[384,768]{1,0:T(8,128)(2,1)S(1)}, u32[]{:S(2)}, u32[]{:S(2)}) collective-permute-start(bf16[384,768]{1,0:T(8,128)(2,1)} %get-tuple-element.521.refs_14_), channel_id=1, source_target_pairs={{0,4},{4,0},{1,5},{5,1},{2,6},{6,2},{3,7},{7,3},{8,12},{12,8},{9,1... | collective-permute-start | bytes 1769480 | tf_op jit(solution)/shard_map/ppermute | solution.py:1253
  1033.0 43.2 %collective-permute-start.149 = (bf16[768,896]{1,0:T(8,128)(2,1)}, bf16[768,896]{1,0:T(8,128)(2,1)S(1)}, u32[]{:S(2)}, u32[]{:S(2)}) collective-permute-start(bf16[768,896]{1,0:T(8,128)(2,1)} %get-tuple-element.550.refs_25_), channel_id=1, source_target_pairs={{0,4},{4,0},{1,5},{5,1},{2,6},{6,2},{3,7},{7,3},{8,12},{12,8},{9,1... | collective-permute-start | bytes 4128776 | tf_op jit(solution)/shard_map/ppermute | solution.py:1253
  1034.8 44.1 %collective-permute-start.148 = (bf16[768,896]{1,0:T(8,128)(2,1)}, bf16[768,896]{1,0:T(8,128)(2,1)S(1)}, u32[]{:S(2)}, u32[]{:S(2)}) collective-permute-start(bf16[768,896]{1,0:T(8,128)(2,1)} %get-tuple-element.549.refs_24_), channel_id=1, source_target_pairs={{0,2},{2,0},{1,3},{3,1},{4,6},{6,4},{5,7},{7,5},{8,10},{10,8},{9,1... | collective-permute-start | bytes 4128776 | tf_op jit(solution)/shard_map/ppermute | solution.py:1253
  1035.3 38.0 %collective-permute-start.146 = (bf16[192,896]{1,0:T(8,128)(2,1)S(1)}, bf16[192,896]{1,0:T(8,128)(2,1)S(1)}, u32[]{:S(2)}, u32[]{:S(2)}) collective-permute-start(bf16[192,896]{1,0:T(8,128)(2,1)S(1)} %copy-done.151), channel_id=1, source_target_pairs={{0,8},{8,0},{16,24},{24,16},{1,9},{9,1},{17,25},{25,17},{2,10},{10... | collective-permute-start | bytes 1032200 | tf_op jit(solution)/shard_map/ppermute | solution.py:1253
  1038.3 36.5 %collective-permute-start.145 = (bf16[192,896]{1,0:T(8,128)(2,1)S(1)}, bf16[192,896]{1,0:T(8,128)(2,1)S(1)}, u32[]{:S(2)}, u32[]{:S(2)}) collective-permute-start(bf16[192,896]{1,0:T(8,128)(2,1)S(1)} %copy-done.153), channel_id=1, source_target_pairs={{0,8},{8,0},{16,24},{24,16},{1,9},{9,1},{17,25},{25,17},{2,10},{10... | collective-permute-start | bytes 1032200 | tf_op jit(solution)/shard_map/ppermute | solution.py:1253
  1041.2 34.3 %collective-permute-start.147 = (bf16[192,768]{1,0:T(8,128)(2,1)}, bf16[192,768]{1,0:T(8,128)(2,1)S(1)}, u32[]{:S(2)}, u32[]{:S(2)}) collective-permute-start(bf16[192,768]{1,0:T(8,128)(2,1)} %get-tuple-element.548.refs_20_.refs_23_), channel_id=1, source_target_pairs={{0,8},{8,0},{16,24},{24,16},{1,9},{9,1},{17,25},{25,17},{2,10},{10... | collective-permute-start | bytes 884744 | tf_op jit(solution)/shard_map/ppermute | solution.py:1253
  1109.3 31.0 %collective-permute-start.155 = (bf16[384,896]{1,0:T(8,128)(2,1)}, bf16[384,896]{1,0:T(8,128)(2,1)}, u32[]{:S(2)}, u32[]{:S(2)}) collective-permute-start(bf16[384,896]{1,0:T(8,128)(2,1)} %behind.19), channel_id=1, source_target_pairs={{0,2},{2,0},{1,3},{3,1},{4,6},{6,4},{5,7},{7,5},{8,10},{10,8},{9,1... | collective-permute-start | bytes 2064392 | tf_op jit(solution)/shard_map/ppermute | solution.py:1253
  1110.3 33.3 %collective-permute-start.154 = (bf16[384,896]{1,0:T(8,128)(2,1)}, bf16[384,896]{1,0:T(8,128)(2,1)}, u32[]{:S(2)}, u32[]{:S(2)}) collective-permute-start(bf16[384,896]{1,0:T(8,128)(2,1)} %behind.18), channel_id=1, source_target_pairs={{0,4},{4,0},{1,5},{5,1},{2,6},{6,2},{3,7},{7,3},{8,12},{12,8},{9,1... | collective-permute-start | bytes 2064392 | tf_op jit(solution)/shard_map/ppermute | solution.py:1253
  1182.1 34.9 %collective-permute-start.164 = (bf16[768,896]{1,0:T(8,128)(2,1)}, bf16[768,896]{1,0:T(8,128)(2,1)S(1)}, u32[]{:S(2)}, u32[]{:S(2)}) collective-permute-start(bf16[768,896]{1,0:T(8,128)(2,1)} %get-tuple-element.601.refs_24_), channel_id=1, source_target_pairs={{0,2},{2,0},{1,3},{3,1},{4,6},{6,4},{5,7},{7,5},{8,10},{10,8},{9,1... | collective-permute-start | bytes 4128776 | tf_op jit(solution)/shard_map/ppermute | solution.py:1253
  1183.5 37.5 %collective-permute-start.169 = (bf16[768,896]{1,0:T(8,128)(2,1)}, bf16[768,896]{1,0:T(8,128)(2,1)S(1)}, u32[]{:S(2)}, u32[]{:S(2)}) collective-permute-start(bf16[768,896]{1,0:T(8,128)(2,1)} %get-tuple-element.602.refs_25_), channel_id=1, source_target_pairs={{0,4},{4,0},{1,5},{5,1},{2,6},{6,2},{3,7},{7,3},{8,12},{12,8},{9,1... | collective-permute-start | bytes 4128776 | tf_op jit(solution)/shard_map/ppermute | solution.py:1253
  1219.5 38.0 %collective-permute-start.165 = (bf16[384,896]{1,0:T(8,128)(2,1)}, bf16[384,896]{1,0:T(8,128)(2,1)S(1)}, u32[]{:S(2)}, u32[]{:S(2)}) collective-permute-start(bf16[384,896]{1,0:T(8,128)(2,1)} %get-tuple-element.608.refs_13_), channel_id=1, source_target_pairs={{0,4},{4,0},{1,5},{5,1},{2,6},{6,2},{3,7},{7,3},{8,12},{12,8},{9,1... | collective-permute-start | bytes 2064392 | tf_op jit(solution)/shard_map/ppermute | solution.py:1253
  1222.7 36.2 %collective-permute-start.170 = (bf16[384,896]{1,0:T(8,128)(2,1)}, bf16[384,896]{1,0:T(8,128)(2,1)S(1)}, u32[]{:S(2)}, u32[]{:S(2)}) collective-permute-start(bf16[384,896]{1,0:T(8,128)(2,1)} %get-tuple-element.618.refs_14_), channel_id=1, source_target_pairs={{0,2},{2,0},{1,3},{3,1},{4,6},{6,4},{5,7},{7,5},{8,10},{10,8},{9,1... | collective-permute-start | bytes 2064392 | tf_op jit(solution)/shard_map/ppermute | solution.py:1253
  1314.8 35.4 %collective-permute-start.192 = (bf16[96,896]{1,0:T(8,128)(2,1)S(1)}, bf16[96,896]{1,0:T(8,128)(2,1)S(1)}, u32[]{:S(2)}, u32[]{:S(2)}) collective-permute-start(bf16[96,896]{1,0:T(8,128)(2,1)S(1)} %get-tuple-element.632.refs_10_), channel_id=1, source_target_pairs={{0,16},{8,24},{16,0},{24,8},{1,17},{9,25},{17,1},{25,9},{2,18},{10... | collective-permute-start | bytes 516104 | tf_op jit(solution)/shard_map/ppermute | solution.py:1253
  1317.8 32.4 %collective-permute-start.189 = (f32[3,8,768]{2,1,0:T(8,128)S(1)}, f32[3,8,768]{2,1,0:T(8,128)S(1)}, u32[]{:S(2)}, u32[]{:S(2)}) collective-permute-start(f32[3,8,768]{2,1,0:T(8,128)S(1)} %add.308), channel_id=1, source_target_pairs={{0,16},{8,24},{16,0},{24,8},{1,17},{9,25},{17,1},{25,9},{2,18},{10... | collective-permute-start | bytes 221192 | tf_op jit(solution)/shard_map/ppermute | solution.py:1421
  1335.6 31.0 %collective-permute-start.185 = (bf16[96,768]{1,0:T(8,128)(2,1)S(1)}, bf16[96,768]{1,0:T(8,128)(2,1)}, u32[]{:S(2)}, u32[]{:S(2)}) collective-permute-start(bf16[96,768]{1,0:T(8,128)(2,1)S(1)} %copy-done.217), channel_id=1, source_target_pairs={{0,16},{8,24},{16,0},{24,8},{1,17},{9,25},{17,1},{25,9},{2,18},{10... | collective-permute-start | bytes 442376 | tf_op jit(solution)/shard_map/ppermute | solution.py:1253
  (566 other events, 7557.6 us)
Sparse Core Ops, SparseCore 0:
  18.1 115.9 all-gather.3
  137.6 123.4 all-gather.5
  264.0 100.5 all-gather.7

commit v3 on v2

--- a/solution.py
+++ b/solution.py
@@ -222,10 +222,10 @@
     tok_ref, mine_ref, theirs_ref, g1_ref, d0, d1, d2, d3, small_ref = outs[:9]
     wout, wud, sems, u_ref, usem = outs[9:]
     loads = [pltpu.make_async_copy(u_hbm.at[s], u_ref.at[s], usem.at[s]) for s in range(4)]
+    for copy in loads:
+        copy.start()
     weights = Weights(sc, refs[4 : 4 + ranks], wout, wud, sems)
     weights.start((1, 0))
-    for copy in loads:
-        copy.start()
     small_ref[...] = jnp.zeros_like(small_ref)
     if first:
         grad = g_ref[...]
@@ -741,22 +741,55 @@
     )(sc, *ins, *deps)
 
 
-def dw_loads(refs, tok, side, outp, sems):
-    tok_m, tok_r, mine, got, o0, o2, r1, r3 = refs
-    size = tok_m.shape[1]
-    low, high = pl.ds(0, size), pl.ds(size, size)
-    pairs = [(tok_m, tok.at[:, low]), (tok_r, tok.at[:, high])]
-    pairs += [(mine, side.at[:, low]), (got, side.at[:, high])]
-    pairs += [(o0, outp.at[0, low]), (r1, outp.at[0, high])]
-    pairs += [(o2, outp.at[1, low]), (r3, outp.at[1, high])]
-    return [pltpu.make_async_copy(a, b, sems.at[k]) for k, (a, b) in enumerate(pairs)]
-
-
-def dw_products(tile, tok, side, outp, put):
+class Loads:
+
+    def __init__(self, refs, tok, side, outp, sems):
+        tok_m, tok_r, mine, got, o0, o2, r1, r3 = refs
+        size = tok_m.shape[1]
+        low, high = pl.ds(0, size), pl.ds(size, size)
+        pairs = {}
+        for k in range(3):
+            pairs["tok", k] = [(tok_m.at[k], tok.at[k, low]), (tok_r.at[k], tok.at[k, high])]
+        for k in range(4):
+            pairs["side", k] = [(mine.at[k], side.at[k, low]), (got.at[k], side.at[k, high])]
+        pairs["outp", 0] = [(o0, outp.at[0, low]), (r1, outp.at[0, high])]
+        pairs["outp", 1] = [(o2, outp.at[1, low]), (r3, outp.at[1, high])]
+        self.copies, n = {}, 0
+        for key, both in pairs.items():
+            self.copies[key] = []
+            for a, b in both:
+                self.copies[key].append(pltpu.make_async_copy(a, b, sems.at[n]))
+                n += 1
+
+    def start(self):
+        first = [("tok", 0), ("side", 0), ("tok", 1), ("side", 2), ("tok", 2), ("outp", 0)]
+        for key in [*first, ("side", 1), ("side", 3), ("outp", 1)]:
+            for copy in self.copies[key]:
+                copy.start()
+
+    def wait(self, *key):
+        for copy in self.copies[key]:
+            copy.wait()
+
+    def wait_tile(self, tile, name, index):
+        tokens = {"up": 0, "down": 1, "out": 2}[index]
+
+        def first():
+            self.wait("tok", tokens)
+            self.wait(name, 2 if index == "down" else 0)
+
+        pl.when(tile == 0)(first)
+        pl.when(tile == 1)(lambda: self.wait(name, 3 if index == "down" else 1))
+
+
+def dw_products(tile, loads, tok, side, outp, put):
+    loads.wait_tile(tile, "side", "up")
     for j in range(3):
-        cols = slice(j * 256, (j + 1) * 256)
-        put(j * 256, tn(tok[0], side[tile, :, cols]))
-        put(768 + j * 256, tn(tok[1], side[2 + tile, :, cols]))
+        put(j * 256, tn(tok[0], side[tile, :, j * 256 : (j + 1) * 256]))
+    loads.wait_tile(tile, "side", "down")
+    for j in range(3):
+        put(768 + j * 256, tn(tok[1], side[2 + tile, :, j * 256 : (j + 1) * 256]))
+    loads.wait_tile(tile, "outp", "out")
     put(1536, tn(tok[2], outp[tile]))
 
 
@@ -767,21 +800,15 @@
     tile = pl.program_id(0)
     keep = sc[6] == 0
 
-    def begin():
-        loads = dw_loads(refs[:8], tok, side, outp, sems)
-        for copy in loads:
-            copy.start()
-        for copy in loads:
-            copy.wait()
-
-    pl.when(tile == 0)(begin)
+    loads = Loads(refs[:8], tok, side, outp, sems)
+    pl.when(tile == 0)(loads.start)
 
     def put(lo, value):
         size = value.shape[1]
         old = old_ref[0, 0, :, lo : lo + size].astype(F32)
         new_ref[0, 0, :, lo : lo + size] = (value + jnp.where(keep, old, 0.0)).astype(BF16)
 
-    dw_products(tile, tok, side, outp, put)
+    dw_products(tile, loads, tok, side, outp, put)
 
 
 def dw_scratch(tok):
@@ -789,7 +816,7 @@
         pltpu.VMEM((3, 2 * tok, D), BF16),
         pltpu.VMEM((4, 2 * tok, D), BF16),
         pltpu.VMEM((2, 2 * tok, 256), BF16),
-        pltpu.SemaphoreType.DMA((8,)),
+        pltpu.SemaphoreType.DMA((18,)),
     ]
 
 
@@ -816,7 +843,7 @@
 
 def dw_last_kernel(rank, groups, slot, sc, *refs):
     keep_a, give_a, keep_b, give_b, acc, token = refs[9:15]
-    tok, side, outp, sems, done, other, dsem, osem, out_ref = refs[15:]
+    tok, side, outp, sems, done, other, dsem, osem, out_a, out_b, asem, bsem = refs[15:]
     token[...] = jnp.zeros_like(token)
     tile = pl.program_id(0)
     same = sc[1] == rank
@@ -826,12 +853,12 @@
     def load(t):
         return pltpu.make_async_copy(acc.at[rank, t], done.at[t], dsem.at[t])
 
+    loads = Loads(refs[:8], tok, side, outp, sems)
+
     def begin():
-        loads = dw_loads(refs[:8], tok, side, outp, sems)
-        for copy in [*loads, load(0), load(1)]:
-            copy.start()
-        for copy in loads:
-            copy.wait()
+        loads.start()
+        load(0).start()
+        load(1).start()
 
     pl.when(tile == 0)(begin)
     load(tile).wait()
@@ -847,7 +874,11 @@
         size = value.shape[1]
         cols = slice(lo, lo + size)
         old = jnp.where(used, done[tile, :, cols].astype(F32), 0.0)
-        out_ref[:, cols] = (old + jnp.where(same, value, 0.0)).astype(BF16)
+        total = (old + jnp.where(same, value, 0.0)).astype(BF16)
+        if lo < D:
+            out_a[tile, :, cols] = total
+        else:
+            out_b[tile, :, lo - D : lo - D + size] = total
 
         def add_other():
             before = jnp.where(keep, other[:, cols].astype(F32), 0.0)
@@ -855,7 +886,7 @@
 
         pl.when(jnp.logical_not(same))(add_other)
 
-    dw_products(tile, tok, side, outp, put)
+    dw_products(tile, loads, tok, side, outp, put)
 
     def store_other():
         copy = pltpu.make_async_copy(other, acc.at[sc[1], tile], osem)
@@ -863,43 +894,57 @@
         copy.wait()
 
     pl.when(jnp.logical_not(same))(store_other)
-    half = PACK // 2
-
-    def first_half(ref):
-        ref[...] = out_ref[:, 0:half]
-
-    pl.when(tile == 0)(functools.partial(first_half, keep_a))
-    pl.when(tile == 1)(functools.partial(first_half, give_a))
     size = D // (2 * groups)
     bit = sc[slot]
-    for g in range(groups):
-        for ref, part in ((keep_b, bit), (give_b, 1 - bit)):
-            src = pl.ds(pl.multiple_of((2 * g + part) * size, size), size)
-            dst = pl.ds(pl.multiple_of((tile * groups + g) * size, size), size)
-            ref[dst, :] = out_ref[src, half:]
+
+    def copies(t):
+        both = [pltpu.make_async_copy(out_a.at[t], (keep_a, give_a)[t], asem.at[t])]
+        for g in range(groups):
+            for k, (ref, part) in enumerate(((keep_b, bit), (give_b, 1 - bit))):
+                src = pl.ds(pl.multiple_of((2 * g + part) * size, size), size)
+                dst = pl.ds((t * groups + g) * size, size)
+                both.append(pltpu.make_async_copy(out_b.at[t, src], ref.at[dst], bsem.at[t, 2 * g + k]))
+        return both
+
+    def leave(t):
+        for copy in copies(t):
+            copy.start()
+
+    pl.when(tile == 0)(functools.partial(leave, 0))
+
+    def finish():
+        leave(1)
+        for t in range(2):
+            for copy in copies(t):
+                copy.wait()
+
+    pl.when(tile == 1)(finish)
 
 
 def dw_last(layer, sc, ins, acc, groups, deps=()):
     tok = ins[0].shape[1]
     slot = LAYERS * 8 + 1 + len(bits_of("dp")) - layer * 8
-    half = jax.ShapeDtypeStruct((D, PACK // 2), BF16)
+    halves = [jax.ShapeDtypeStruct((D, n), BF16) for n in (D, D, PACK - D, PACK - D)]
     return pl.pallas_call(
         strip(functools.partial(dw_last_kernel, layer, groups, slot), layer, 9, len(deps)),
         grid_spec=pltpu.PrefetchScalarGridSpec(
             num_scalar_prefetch=1,
             grid=(2,),
             in_specs=[ANY] * 9 + [ANY] * len(deps),
-            out_specs=[whole_spec(half.shape)] * 4 + [ANY, whole_spec((8, 128))],
+            out_specs=[ANY] * 4 + [ANY, whole_spec((8, 128))],
             scratch_shapes=dw_scratch(tok)
             + [
                 pltpu.VMEM((2, D, PACK), BF16),
                 pltpu.VMEM((D, PACK), BF16),
                 pltpu.SemaphoreType.DMA((2,)),
                 pltpu.SemaphoreType.DMA(()),
-                pltpu.VMEM((D, PACK), BF16),
+                pltpu.VMEM((2, D, D), BF16),
+                pltpu.VMEM((2, D, PACK - D), BF16),
+                pltpu.SemaphoreType.DMA((2,)),
+                pltpu.SemaphoreType.DMA((2, 2 * groups)),
             ],
         ),
-        out_shape=[half] * 4
+        out_shape=halves
         + [
             jax.ShapeDtypeStruct(acc.shape, acc.dtype),
             jax.ShapeDtypeStruct((8, 128), F32),
@@ -1362,10 +1407,9 @@
             for b in range(NB):
 
                 def put(b=b, left=left, right=right):
-                    up[b] = left[:, 0:D]
-                    down[b, :, 0 : 896 - D] = left[:, D:]
-                    down[b, :, 896 - D :] = right[:, 0 : 2 * D - 896]
-                    out[b] = right[:, 2 * D - 896 : 2 * D - 896 + width]
+                    up[b] = left
+                    down[b] = right[:, 0:D]
+                    out[b] = right[:, D : D + width]
 
                 pl.when(sc[slot + b] == k)(put)
 
@@ -1594,8 +1638,9 @@
         ins = [tokens, swap_core(tokens), mine, swap_core(theirs)]
         ins += [o_got[0], o_got[2], swap_core(o_got[1]), swap_core(o_got[3])]
         if i < NB:
-            res = dw_last(i, sc, ins, acc_pack, dps, do_got[1:])
+            res = dw_last(i, sc, ins, acc_pack, dps)
             keep_a, give_a, keep_b, give_b, acc_pack, token = res
+            give_a, give_b = behind([give_a, give_b], do_got[1:])
             left = [n for n in bits if n != top]
             done_pack[i] = [
                 Reduce(sc, keep_a, give_a, x_bit, bits, row_bits + dp_bits[::-1]),
@@ -1611,7 +1656,7 @@
         res = attn_bwd(i, sc, do_got, o_send, q, kv, lse, lsec, wqkv_all, pos, dims, fence)
         da_mine, da_theirs, dq, dkv, small_qkv[i] = res
         fence = []
-        for part in sums:
+        for part in sums if i > 0 else done_pack[0]:
             if part.ready <= 2 * (LAYERS - i) + 1:
                 fence += part.step([small_qkv[i]], i > 0)
         if i == LAYERS - 1:
@@ -1631,7 +1676,7 @@
             acc_pack, token = dw_mlp(i, sc, ins, acc_pack, [base])
             fence.append(token)
         for part in sums:
-            part.release([got, *rest])
+            part.release([got, *rest, token])
         if i < NB:
             keep, give = qkv_total(sc, i, dws[i:], dps, [got])
             done_qkv[i] = Reduce(sc, keep, give, top, left, row_bits[1:] + dp_bits[::-1])
@@ -1643,7 +1688,10 @@
 
     for part in sums:
         if part.ready <= 2 * LAYERS + 2:
-            fence += part.step([got])
+            step = part.step([got])
+            if part not in done_pack[0]:
+                continue
+            fence += step
     res = final_norm(sc, grad, back, vecs, prompt, width, fence)
     dx_parts = leave_begin(exchange_heads(res[:4]), sc, prompt_row)
     for part in sums:

time: 1390 us -> 1340 us (0.964)
  waiting for transfers between devices: 401 us -> 365 us
  Pallas kernels: 650 us -> 636 us
    ppermute x51, waiting for transfers between devices: 75.7 us -> 60.7 us  [exchange_heads(): out.append(lax.ppermute(parts[s], ('x', 'core'), pairs))]
    unnamed x808 -> x792, local copies, waits for them, and re-layouts: 109 us -> 109 us
  transfers between devices with their start and end apart: 200 -> 200, of which waited for: 73 -> 75; matrix products, arithmetic and copies ran while one was open for 2% -> 2% of each run, Pallas kernels for 32% -> 34%
where the time goes in v3:
time: 1340 us; the launch traced here: 1330 us
  Pallas kernels  636 us (47%)
  waiting for transfers between devices  365 us (27%)
  starting transfers between devices  174 us (13%)
  local copies, waits for them, and re-layouts  122 us (9%)
  between operations  24 us (2%)
    pallas_call x6, Pallas kernels, attn_bwd(): pl.pallas_call(strip(functools.partial(attn_bwd_kernel, dims), layer, 13...  181 us
    pallas_call x6, Pallas kernels, attn_fwd(): pl.pallas_call(strip(functools.partial(attn_fwd_kernel, dims), layer, cou...  132 us
    unnamed x792, local copies, waits for them, and re-layouts  109 us
    ppermute x14, waiting for transfers between devices, gather_begin(): lax.ppermute(value, names, [(i, i ^ t) for i in range(total)])  100 us
    pallas_call x6, Pallas kernels, mlp_bwd(): pl.pallas_call(strip(kernel, layer, len(ins), len(deps)), grid_spec=pltpu...  79.6 us
    ppermute x51, waiting for transfers between devices, exchange_heads(): out.append(lax.ppermute(parts[s], ('x', 'core'), pairs))  60.7 us
    ppermute x13, waiting for transfers between devices, swap_x(): return lax.ppermute(value, 'x', SWAP)  55.1 us
    pallas_call x3, Pallas kernels, dw_last(): pl.pallas_call(strip(functools.partial(dw_last_kernel, layer, groups, slo...  52.7 us
  transfers between devices with their start and end apart: 200, of which 75 were waited for; matrix products, arithmetic and copies ran while one was open for 2% of the time, Pallas kernels for 34%

profile of v3, /device:TPU:0, one launch (start us, length us, event | category | flops | bytes accessed | tf_op | source)
XLA Modules:
  0.0 1328.9 jit_solution(8932267268484121511)
XLA Ops:
  52.2 11.7 collective-permute-start.17
  104.4 21.9 %attn_fwd.6 = (bf16[288,256]{1,0:T(8,128)(2,1)S(1)}, bf16[288,256]{1,0:T(8,128)(2,1)S(1)}, bf16[288,256]{1,0:T(8,128)(2,1)S(1)}, bf16[288,256]{1,0:T(8,128)(2,1)...) custom-call(s32[55]{0:T(128)S(1)} %concatenate.19.sc, ...), custom_call_target="tpu_custom_call" | custom-call | flops 6568280064 | bytes 12000000 | tf_op jit(solution)/shard_map/attn_fwd/pallas_call | solution.py:455
  155.7 37.6 %collective-permute-done.35.refs_5_ = bf16[2,96,768]{2,1,0:T(8,128)(2,1)} collective-permute-done((bf16[2,96,768]{2,1,0:T(8,128)(2,1)}, bf16[2,96,768]{2,1,0:T(8,128)(2,1)}, u32[]{:S(2)}, u32[]{:S(2)}) %collective-permute-start.35) | collective-permute-done | bytes 294944 | tf_op jit(solution)/shard_map/ppermute | solution.py:1104
  195.9 11.6 collective-permute-done.34.refs_4_
  222.2 14.9 %collective-permute-done.31.refs_1_ = bf16[2,96,768]{2,1,0:T(8,128)(2,1)S(1)} collective-permute-done((bf16[2,96,768]{2,1,0:T(8,128)(2,1)S(1)}, bf16[2,96,768]{2,1,0:T(8,128)(2,1)S(1)}, u32[]{:S(2)}, u32[]{:S(2)}) %collective-permute-start.31) | collective-permute-done | bytes 294944 | tf_op jit(solution)/shard_map/ppermute | solution.py:1104
  242.6 22.0 %attn_fwd.7 = (bf16[288,256]{1,0:T(8,128)(2,1)S(1)}, bf16[288,256]{1,0:T(8,128)(2,1)S(1)}, bf16[288,256]{1,0:T(8,128)(2,1)S(1)}, bf16[288,256]{1,0:T(8,128)(2,1)...) custom-call(s32[55]{0:T(128)S(1)} %concatenate.19.sc, ...), custom_call_target="tpu_custom_call" | custom-call | flops 6568280064 | bytes 12000000 | tf_op jit(solution)/shard_map/attn_fwd/pallas_call | solution.py:455
  293.0 19.2 %collective-permute-done.42.refs_2_ = bf16[288,768]{1,0:T(8,128)(2,1)} collective-permute-done((bf16[288,768]{1,0:T(8,128)(2,1)}, bf16[288,768]{1,0:T(8,128)(2,1)}, u32[]{:S(2)}, u32[]{:S(2)}) %collective-permute-start.42) | collective-permute-done | bytes 442400 | tf_op jit(solution)/shard_map/ppermute | solution.py:999
  324.2 22.7 %attn_fwd.8 = (bf16[288,256]{1,0:T(8,128)(2,1)S(1)}, bf16[288,256]{1,0:T(8,128)(2,1)S(1)}, bf16[288,256]{1,0:T(8,128)(2,1)}, bf16[288,256]{1,0:T(8,128)(2,1)}, b...) custom-call(s32[55]{0:T(128)S(1)} %concatenate.19.sc, ...), custom_call_target="tpu_custom_call" | custom-call | flops 6568280064 | bytes 12000000 | tf_op jit(solution)/shard_map/attn_fwd/pallas_call | solution.py:455
  352.0 12.6 all-gather.8.cloned.1.call-done
  398.0 21.9 %attn_fwd.9 = (bf16[288,256]{1,0:T(8,128)(2,1)S(1)}, bf16[288,256]{1,0:T(8,128)(2,1)S(1)}, bf16[288,256]{1,0:T(8,128)(2,1)S(1)}, bf16[288,256]{1,0:T(8,128)(2,1)...) custom-call(s32[55]{0:T(128)S(1)} %concatenate.19.sc, ...), custom_call_target="tpu_custom_call" | custom-call | flops 6568280064 | bytes 12000000 | tf_op jit(solution)/shard_map/attn_fwd/pallas_call | solution.py:455
  448.1 9.5 collective-permute-done.66.refs_2_
  469.9 22.0 %attn_fwd.10 = (bf16[288,256]{1,0:T(8,128)(2,1)S(1)}, bf16[288,256]{1,0:T(8,128)(2,1)S(1)}, bf16[288,256]{1,0:T(8,128)(2,1)S(1)}, bf16[288,256]{1,0:T(8,128)(2,1...) custom-call(s32[55]{0:T(128)S(1)} %concatenate.19.sc, ...), custom_call_target="tpu_custom_call" | custom-call | flops 6568280064 | bytes 12000000 | tf_op jit(solution)/shard_map/attn_fwd/pallas_call | solution.py:455
  534.1 21.8 %attn_fwd.11 = (bf16[288,256]{1,0:T(8,128)(2,1)S(1)}, bf16[288,256]{1,0:T(8,128)(2,1)S(1)}, bf16[288,256]{1,0:T(8,128)(2,1)S(1)}, bf16[288,256]{1,0:T(8,128)(2,1...) custom-call(s32[55]{0:T(128)S(1)} %concatenate.19.sc, ...), custom_call_target="tpu_custom_call" | custom-call | flops 6568280064 | bytes 12000000 | tf_op jit(solution)/shard_map/attn_fwd/pallas_call | solution.py:455
  577.9 12.5 mlp_bwd.6
  604.4 29.9 %attn_bwd.6 = (bf16[1088,768]{1,0:T(8,128)(2,1)}, bf16[1088,768]{1,0:T(8,128)(2,1)}, bf16[4,3,288,256]{3,2,1,0:T(8,128)(2,1)}, bf16[4,3,256,128]{3,2,1,0:T(8,128)(2,1)}, f32[3,8,256]{2,1,0:T(8,128)}) custom-call(s32[55]{0:T(128)} %copy-done.42, bf16[288,256]{1,0:T(8,128)(2,1)} %get-tuple-element.417.refs_0_, bf16[288,256]{1,0:T(8,128)(2,1)} %copy-done.380, ...), custom_call_target="tpu_custom_call" | custom-call | flops 12343836672 | bytes 14000000 | tf_op jit(solution)/shard_map/attn_bwd/pallas_call | solution.py:638
  657.4 12.9 dw_mlp.3
  671.1 13.0 mlp_bwd.7
  695.1 30.2 %attn_bwd.7 = (bf16[1088,768]{1,0:T(8,128)(2,1)}, bf16[1088,768]{1,0:T(8,128)(2,1)}, bf16[4,3,288,256]{3,2,1,0:T(8,128)(2,1)}, bf16[4,3,256,128]{3,2,1,0:T(8,128)(2,1)}, f32[3,8,256]{2,1,0:T(8,128)}) custom-call(s32[55]{0:T(128)} %copy-done.42, bf16[288,256]{1,0:T(8,128)(2,1)} %copy-done.308, bf16[288,256]{1,0:T(8,128)(2,1)} %copy-done.382, ...), custom_call_target="tpu_custom_call" | custom-call | flops 12343836672 | bytes 14000000 | tf_op jit(solution)/shard_map/attn_bwd/pallas_call | solution.py:638
  745.1 13.1 dw_mlp.4
  759.0 12.9 mlp_bwd.8
  782.9 30.3 %attn_bwd.8 = (bf16[1088,768]{1,0:T(8,128)(2,1)}, bf16[1088,768]{1,0:T(8,128)(2,1)}, bf16[4,3,288,256]{3,2,1,0:T(8,128)(2,1)}, bf16[4,3,256,128]{3,2,1,0:T(8,128)(2,1)}, f32[3,8,256]{2,1,0:T(8,128)}) custom-call(s32[55]{0:T(128)} %copy-done.42, bf16[288,256]{1,0:T(8,128)(2,1)} %copy-done.309, bf16[288,256]{1,0:T(8,128)(2,1)} %copy-done.383, ...), custom_call_target="tpu_custom_call" | custom-call | flops 12343836672 | bytes 14000000 | tf_op jit(solution)/shard_map/attn_bwd/pallas_call | solution.py:638
  833.0 13.1 dw_mlp.5
  846.9 13.0 mlp_bwd.9
  870.3 17.6 %dw_last.3 = (bf16[768,768]{1,0:T(8,128)(2,1)}, bf16[768,768]{1,0:T(8,128)(2,1)}, bf16[768,1024]{1,0:T(8,128)(2,1)}, bf16[768,1024]{1,0:T(8,128)(2,1)}, bf16[3,2...) custom-call(s32[55]{0:T(128)} %copy-done.42, ...), custom_call_target="tpu_custom_call", output_to_operand_aliasing={{4}: (9, {})} | custom-call | flops 3170893824 | bytes 20000000 | tf_op jit(solution)/shard_map/dw_last/pallas_call | solution.py:928
  892.1 30.1 %attn_bwd.9 = (bf16[1088,768]{1,0:T(8,128)(2,1)}, bf16[1088,768]{1,0:T(8,128)(2,1)}, bf16[4,3,288,256]{3,2,1,0:T(8,128)(2,1)}, bf16[4,3,256,128]{3,2,1,0:T(8,128)(2,1)}, f32[3,8,256]{2,1,0:T(8,128)}) custom-call(s32[55]{0:T(128)} %copy-done.42, bf16[288,256]{1,0:T(8,128)(2,1)} %copy-done.303, bf16[288,256]{1,0:T(8,128)(2,1)} %copy-done.342, ...), custom_call_target="tpu_custom_call" | custom-call | flops 12343836672 | bytes 14000000 | tf_op jit(solution)/shard_map/attn_bwd/pallas_call | solution.py:638
  962.6 14.0 %mlp_bwd.10 = (bf16[3,288,768]{2,1,0:T(8,128)(2,1)}, bf16[4,288,768]{2,1,0:T(8,128)(2,1)}, bf16[4,288,768]{2,1,0:T(8,128)(2,1)}, f32[288,768]{1,0:T(8,128)S(1)},...) custom-call(s32[55]{0:T(128)S(1)} %copy-done.48, ...), custom_call_target="tpu_custom_call" | custom-call | flops 3057647616 | bytes 16000000 | tf_op jit(solution)/shard_map/mlp_bwd/pallas_call | solution.py:296
  990.7 17.6 %dw_last.4 = (bf16[768,768]{1,0:T(8,128)(2,1)}, bf16[768,768]{1,0:T(8,128)(2,1)}, bf16[768,1024]{1,0:T(8,128)(2,1)}, bf16[768,1024]{1,0:T(8,128)(2,1)}, bf16[3,2...) custom-call(s32[55]{0:T(128)} %copy-done.42, ...), custom_call_target="tpu_custom_call", output_to_operand_aliasing={{4}: (9, {})} | custom-call | flops 3170893824 | bytes 20000000 | tf_op jit(solution)/shard_map/dw_last/pallas_call | solution.py:928
  1017.4 30.1 %attn_bwd.10 = (bf16[1088,768]{1,0:T(8,128)(2,1)}, bf16[1088,768]{1,0:T(8,128)(2,1)}, bf16[4,3,288,256]{3,2,1,0:T(8,128)(2,1)}, bf16[4,3,256,128]{3,2,1,0:T(8,128)(2,1)}, f32[3,8,256]{2,1,0:T(8,128)}) custom-call(s32[55]{0:T(128)} %copy-done.42, bf16[288,256]{1,0:T(8,128)(2,1)} %get-tuple-element.542.refs_0_, bf16[288,256]{1,0:T(8,128)(2,1)} %copy-done.340, ...), custom_call_target="tpu_custom_call" | custom-call | flops 12343836672 | bytes 14000000 | tf_op jit(solution)/shard_map/attn_bwd/pallas_call | solution.py:638
  1092.6 14.0 %mlp_bwd.11 = (bf16[3,288,768]{2,1,0:T(8,128)(2,1)}, bf16[4,288,768]{2,1,0:T(8,128)(2,1)}, bf16[4,288,768]{2,1,0:T(8,128)(2,1)}, f32[288,768]{1,0:T(8,128)S(1)},...) custom-call(s32[55]{0:T(128)S(1)} %copy-done.51, ...), custom_call_target="tpu_custom_call" | custom-call | flops 3057647616 | bytes 16000000 | tf_op jit(solution)/shard_map/mlp_bwd/pallas_call | solution.py:296
  1122.1 17.6 %dw_last.5 = (bf16[768,768]{1,0:T(8,128)(2,1)}, bf16[768,768]{1,0:T(8,128)(2,1)}, bf16[768,1024]{1,0:T(8,128)(2,1)}, bf16[768,1024]{1,0:T(8,128)(2,1)}, bf16[3,2...) custom-call(s32[55]{0:T(128)} %copy-done.42, ...), custom_call_target="tpu_custom_call", output_to_operand_aliasing={{4}: (9, {})} | custom-call | flops 3170893824 | bytes 20000000 | tf_op jit(solution)/shard_map/dw_last/pallas_call | solution.py:928
  1145.5 30.1 %attn_bwd.11 = (bf16[1088,768]{1,0:T(8,128)(2,1)}, bf16[1088,768]{1,0:T(8,128)(2,1)}, bf16[4,3,288,256]{3,2,1,0:T(8,128)(2,1)}, bf16[4,3,256,128]{3,2,1,0:T(8,128)(2,1)}, f32[3,8,256]{2,1,0:T(8,128)}) custom-call(s32[55]{0:T(128)} %copy-done.42, bf16[288,256]{1,0:T(8,128)(2,1)} %get-tuple-element.597.refs_0_, ...), custom_call_target="tpu_custom_call" | custom-call | flops 12343836672 | bytes 14000000 | tf_op jit(solution)/shard_map/attn_bwd/pallas_call | solution.py:638
  1279.5 11.9 collective-permute-done.189.refs_1_
  (1332 shorter events, 691.4 us)
Async XLA Ops:
  7.2 134.0 %all-gather.4.cloned.1.call-start = ((), (), s32[]{:S(2)}) async-start(), calls=%async_computation | async-start | bytes 11354112 | tf_op jit(solution)/shard_map/all_gather | solution.py:1558
  18.0 251.8 %all-gather.6.cloned.1.call-start = ((), (), s32[]{:S(2)}) async-start(), calls=%async_computation.1 | async-start | bytes 11354112 | tf_op jit(solution)/shard_map/all_gather | solution.py:1558
  18.7 345.9 %all-gather.8.cloned.1.call-start = ((), (), s32[]{:S(2)}) async-start(), calls=%async_computation.2 | async-start | bytes 11354112 | tf_op jit(solution)/shard_map/all_gather | solution.py:1558
  43.6 28.9 %collective-permute-start.18 = (bf16[1,96,768]{2,1,0:T(8,128)(2,1)}, bf16[1,96,768]{2,1,0:T(8,128)(2,1)S(1)}, u32[]{:S(2)}, u32[]{:S(2)}) collective-permute-start(bf16[1,96,768]{2,1,0:T(8,128)(2,1)} %held.2.refs_0_), channel_id=1, source_target_pairs={{0,20},{4,16},{8,28},{12,24},{16,4},{20,0},{24,12},{28,8},{1,21},{... | collective-permute-start | bytes 442376 | tf_op jit(solution)/shard_map/ppermute | solution.py:1104
  45.7 39.0 %collective-permute-start.12 = (bf16[256,768]{1,0:T(8,128)(2,1)S(1)}, bf16[256,768]{1,0:T(8,128)(2,1)}, u32[]{:S(2)}, u32[]{:S(2)}) collective-permute-start(bf16[256,768]{1,0:T(8,128)(2,1)S(1)} %get-tuple-element.355), channel_id=1, source_target_pairs={{0,6},{2,4},{4,2},{6,0},{1,7},{3,5},{5,3},{7,1},{8,14},{10,12},{12... | collective-permute-start | bytes 1179656 | tf_op jit(solution)/shard_map/ppermute | solution.py:1010
  48.6 36.6 %collective-permute-start.10 = (bf16[256,768]{1,0:T(8,128)(2,1)S(1)}, bf16[256,768]{1,0:T(8,128)(2,1)S(1)}, u32[]{:S(2)}, u32[]{:S(2)}) collective-permute-start(bf16[256,768]{1,0:T(8,128)(2,1)S(1)} %get-tuple-element.355), channel_id=1, source_target_pairs={{0,4},{4,0},{1,5},{5,1},{2,6},{6,2},{3,7},{7,3},{8,12},{12,8},{9,1... | collective-permute-start | bytes 1179656 | tf_op jit(solution)/shard_map/ppermute | solution.py:1004
  48.7 36.5 %collective-permute-start.8 = (bf16[288,768]{1,0:T(8,128)(2,1)S(1)}, bf16[288,768]{1,0:T(8,128)(2,1)}, u32[]{:S(2)}, u32[]{:S(2)}) collective-permute-start(bf16[288,768]{1,0:T(8,128)(2,1)S(1)} %get-tuple-element.354.refs_8_.refs_0_), channel_id=1, source_target_pairs={{0,2},{2,0},{1,3},{3,1},{4,6},{6,4},{5,7},{7,5},{8,10},{10,8},{9,1... | collective-permute-start | bytes 1327112 | tf_op jit(solution)/shard_map/ppermute | solution.py:999
  136.1 57.3 %collective-permute-start.35 = (bf16[2,96,768]{2,1,0:T(8,128)(2,1)}, bf16[2,96,768]{2,1,0:T(8,128)(2,1)}, u32[]{:S(2)}, u32[]{:S(2)}) collective-permute-start(bf16[2,96,768]{2,1,0:T(8,128)(2,1)} %held.3.refs_0_), channel_id=1, source_target_pairs={{0,20},{4,16},{8,28},{12,24},{16,4},{20,0},{24,12},{28,8},{1,21},{... | collective-permute-start | bytes 884744 | tf_op jit(solution)/shard_map/ppermute | solution.py:1104
  137.1 70.4 %collective-permute-start.34 = (bf16[2,96,768]{2,1,0:T(8,128)(2,1)}, bf16[2,96,768]{2,1,0:T(8,128)(2,1)}, u32[]{:S(2)}, u32[]{:S(2)}) collective-permute-start(bf16[2,96,768]{2,1,0:T(8,128)(2,1)} %held.3.refs_0_), channel_id=1, source_target_pairs={{0,16},{4,20},{8,24},{12,28},{16,0},{20,4},{24,8},{28,12},{1,17},{... | collective-permute-start | bytes 884744 | tf_op jit(solution)/shard_map/ppermute | solution.py:1104
  152.2 62.4 %collective-permute-start.25 = (bf16[288,768]{1,0:T(8,128)(2,1)S(1)}, bf16[288,768]{1,0:T(8,128)(2,1)S(1)}, u32[]{:S(2)}, u32[]{:S(2)}) collective-permute-start(bf16[288,768]{1,0:T(8,128)(2,1)S(1)} %get-tuple-element.361.refs_9_.refs_0_), channel_id=1, source_target_pairs={{0,2},{2,0},{1,3},{3,1},{4,6},{6,4},{5,7},{7,5},{8,10},{10,8},{9,1... | collective-permute-start | bytes 1327112 | tf_op jit(solution)/shard_map/ppermute | solution.py:999
  154.0 61.2 %collective-permute-start.29 = (bf16[256,768]{1,0:T(8,128)(2,1)S(1)}, bf16[256,768]{1,0:T(8,128)(2,1)S(1)}, u32[]{:S(2)}, u32[]{:S(2)}) collective-permute-start(bf16[256,768]{1,0:T(8,128)(2,1)S(1)} %get-tuple-element.362), channel_id=1, source_target_pairs={{0,6},{2,4},{4,2},{6,0},{1,7},{3,5},{5,3},{7,1},{8,14},{10,12},{12... | collective-permute-start | bytes 1179656 | tf_op jit(solution)/shard_map/ppermute | solution.py:1010
  154.0 61.2 %collective-permute-start.27 = (bf16[256,768]{1,0:T(8,128)(2,1)S(1)}, bf16[256,768]{1,0:T(8,128)(2,1)S(1)}, u32[]{:S(2)}, u32[]{:S(2)}) collective-permute-start(bf16[256,768]{1,0:T(8,128)(2,1)S(1)} %get-tuple-element.362), channel_id=1, source_target_pairs={{0,4},{4,0},{1,5},{5,1},{2,6},{6,2},{3,7},{7,3},{8,12},{12,8},{9,1... | collective-permute-start | bytes 1179656 | tf_op jit(solution)/shard_map/ppermute | solution.py:1004
  291.0 29.5 %collective-permute-start.46 = (bf16[256,768]{1,0:T(8,128)(2,1)S(1)}, bf16[256,768]{1,0:T(8,128)(2,1)}, u32[]{:S(2)}, u32[]{:S(2)}) collective-permute-start(bf16[256,768]{1,0:T(8,128)(2,1)S(1)} %get-tuple-element.370), channel_id=1, source_target_pairs={{0,6},{2,4},{4,2},{6,0},{1,7},{3,5},{5,3},{7,1},{8,14},{10,12},{12... | collective-permute-start | bytes 1179656 | tf_op jit(solution)/shard_map/ppermute | solution.py:1010
  291.4 29.1 %collective-permute-start.44 = (bf16[256,768]{1,0:T(8,128)(2,1)S(1)}, bf16[256,768]{1,0:T(8,128)(2,1)S(1)}, u32[]{:S(2)}, u32[]{:S(2)}) collective-permute-start(bf16[256,768]{1,0:T(8,128)(2,1)S(1)} %get-tuple-element.370), channel_id=1, source_target_pairs={{0,4},{4,0},{1,5},{5,1},{2,6},{6,2},{3,7},{7,3},{8,12},{12,8},{9,1... | collective-permute-start | bytes 1179656 | tf_op jit(solution)/shard_map/ppermute | solution.py:1004
  293.0 31.1 %collective-permute-start.41 = (bf16[288,768]{1,0:T(8,128)(2,1)}, bf16[288,768]{1,0:T(8,128)(2,1)}, u32[]{:S(2)}, u32[]{:S(2)}) collective-permute-start(bf16[288,768]{1,0:T(8,128)(2,1)} %get-tuple-element.369.refs_0_), channel_id=1, source_target_pairs={{0,1},{1,0},{2,3},{3,2},{4,5},{5,4},{6,7},{7,6},{8,9},{9,8},{10,11... | collective-permute-start | bytes 1327112 | tf_op jit(solution)/shard_map/ppermute | solution.py:995
  322.6 27.5 %collective-permute-start.51 = (bf16[512,192]{1,0:T(8,128)(2,1)}, bf16[512,192]{1,0:T(8,128)(2,1)S(1)}, u32[]{:S(2)}, u32[]{:S(2)}) collective-permute-start(bf16[512,192]{1,0:T(8,128)(2,1)} %bitcast.40), channel_id=1, source_target_pairs={{0,4},{4,0},{1,5},{5,1},{2,6},{6,2},{3,7},{7,3},{8,12},{12,8},{9,1... | collective-permute-start | bytes 589832 | tf_op jit(solution)/shard_map/ppermute | solution.py:1204
  395.4 28.0 %collective-permute-start.62 = (bf16[288,192]{1,0:T(8,128)(2,1)S(1)}, bf16[288,192]{1,0:T(8,128)(2,1)S(1)}, u32[]{:S(2)}, u32[]{:S(2)}) collective-permute-start(bf16[288,192]{1,0:T(8,128)(2,1)S(1)} %copy-done.307), channel_id=1, source_target_pairs={{0,1},{1,0},{2,3},{3,2},{4,5},{5,4},{6,7},{7,6},{8,9},{9,8},{10,11... | collective-permute-start | bytes 331784 | tf_op jit(solution)/shard_map/ppermute | solution.py:1032
  596.9 37.4 %collective-permute-start.88 = (bf16[512,192]{1,0:T(8,128)(2,1)S(1)}, bf16[512,192]{1,0:T(8,128)(2,1)S(1)}, u32[]{:S(2)}, u32[]{:S(2)}) collective-permute-start(bf16[512,192]{1,0:T(8,128)(2,1)S(1)} %get-tuple-element.410), channel_id=1, source_target_pairs={{4,0},{0,4},{5,1},{1,5},{6,2},{2,6},{7,3},{3,7},{12,8},{8,12},{13,... | collective-permute-start | bytes 589832 | tf_op jit(solution)/shard_map/ppermute | solution.py:1243
  888.7 36.9 %collective-permute-start.130 = (bf16[768,1024]{1,0:T(8,128)(2,1)}, bf16[768,1024]{1,0:T(8,128)(2,1)S(1)}, u32[]{:S(2)}, u32[]{:S(2)}) collective-permute-start(bf16[768,1024]{1,0:T(8,128)(2,1)} %get-tuple-element.508.refs_21_), channel_id=1, source_target_pairs={{0,4},{4,0},{1,5},{5,1},{2,6},{6,2},{3,7},{7,3},{8,12},{12,8},{9,1... | collective-permute-start | bytes 4718600 | tf_op jit(solution)/shard_map/ppermute | solution.py:1298
  890.5 31.7 %collective-permute-start.129 = (bf16[768,768]{1,0:T(8,128)(2,1)}, bf16[768,768]{1,0:T(8,128)(2,1)S(1)}, u32[]{:S(2)}, u32[]{:S(2)}) collective-permute-start(bf16[768,768]{1,0:T(8,128)(2,1)} %get-tuple-element.507.refs_20_), channel_id=1, source_target_pairs={{0,2},{2,0},{1,3},{3,1},{4,6},{6,4},{5,7},{7,5},{8,10},{10,8},{9,1... | collective-permute-start | bytes 3538952 | tf_op jit(solution)/shard_map/ppermute | solution.py:1298
  983.5 30.0 %collective-permute-start.144 = (bf16[384,768]{1,0:T(8,128)(2,1)}, bf16[384,768]{1,0:T(8,128)(2,1)}, u32[]{:S(2)}, u32[]{:S(2)}) collective-permute-start(bf16[384,768]{1,0:T(8,128)(2,1)} %get-tuple-element.529.refs_14_), channel_id=1, source_target_pairs={{0,4},{4,0},{1,5},{5,1},{2,6},{6,2},{3,7},{7,3},{8,12},{12,8},{9,1... | collective-permute-start | bytes 1769480 | tf_op jit(solution)/shard_map/ppermute | solution.py:1298
  1008.9 44.0 %collective-permute-start.149 = (bf16[768,1024]{1,0:T(8,128)(2,1)}, bf16[768,1024]{1,0:T(8,128)(2,1)S(1)}, u32[]{:S(2)}, u32[]{:S(2)}) collective-permute-start(bf16[768,1024]{1,0:T(8,128)(2,1)} %get-tuple-element.560.refs_25_), channel_id=1, source_target_pairs={{0,4},{4,0},{1,5},{5,1},{2,6},{6,2},{3,7},{7,3},{8,12},{12,8},{9,1... | collective-permute-start | bytes 4718600 | tf_op jit(solution)/shard_map/ppermute | solution.py:1298
  1010.1 40.3 %collective-permute-start.148 = (bf16[768,768]{1,0:T(8,128)(2,1)}, bf16[768,768]{1,0:T(8,128)(2,1)S(1)}, u32[]{:S(2)}, u32[]{:S(2)}) collective-permute-start(bf16[768,768]{1,0:T(8,128)(2,1)} %get-tuple-element.559.refs_24_), channel_id=1, source_target_pairs={{0,2},{2,0},{1,3},{3,1},{4,6},{6,4},{5,7},{7,5},{8,10},{10,8},{9,1... | collective-permute-start | bytes 3538952 | tf_op jit(solution)/shard_map/ppermute | solution.py:1298
  1011.4 37.7 %collective-permute-start.145 = (bf16[192,768]{1,0:T(8,128)(2,1)}, bf16[192,768]{1,0:T(8,128)(2,1)S(1)}, u32[]{:S(2)}, u32[]{:S(2)}) collective-permute-start(bf16[192,768]{1,0:T(8,128)(2,1)} %copy-done.150), channel_id=1, source_target_pairs={{0,8},{8,0},{16,24},{24,16},{1,9},{9,1},{17,25},{25,17},{2,10},{10... | collective-permute-start | bytes 884744 | tf_op jit(solution)/shard_map/ppermute | solution.py:1298
  1013.5 34.0 %collective-permute-start.146 = (bf16[192,1024]{1,0:T(8,128)(2,1)}, bf16[192,1024]{1,0:T(8,128)(2,1)S(1)}, u32[]{:S(2)}, u32[]{:S(2)}) collective-permute-start(bf16[192,1024]{1,0:T(8,128)(2,1)} %copy-done.141), channel_id=1, source_target_pairs={{0,8},{8,0},{16,24},{24,16},{1,9},{9,1},{17,25},{25,17},{2,10},{10... | collective-permute-start | bytes 1179656 | tf_op jit(solution)/shard_map/ppermute | solution.py:1298
  1015.3 34.4 %collective-permute-start.147 = (bf16[192,768]{1,0:T(8,128)(2,1)S(1)}, bf16[192,768]{1,0:T(8,128)(2,1)S(1)}, u32[]{:S(2)}, u32[]{:S(2)}) collective-permute-start(bf16[192,768]{1,0:T(8,128)(2,1)S(1)} %get-tuple-element.556.refs_20_.refs_23_), channel_id=1, source_target_pairs={{0,8},{8,0},{16,24},{24,16},{1,9},{9,1},{17,25},{25,17},{2,10},{10... | collective-permute-start | bytes 884744 | tf_op jit(solution)/shard_map/ppermute | solution.py:1298
  1140.4 36.9 %collective-permute-start.166 = (bf16[768,1024]{1,0:T(8,128)(2,1)}, bf16[768,1024]{1,0:T(8,128)(2,1)S(1)}, u32[]{:S(2)}, u32[]{:S(2)}) collective-permute-start(bf16[768,1024]{1,0:T(8,128)(2,1)} %get-tuple-element.614.refs_25_), channel_id=1, source_target_pairs={{0,4},{4,0},{1,5},{5,1},{2,6},{6,2},{3,7},{7,3},{8,12},{12,8},{9,1... | collective-permute-start | bytes 4718600 | tf_op jit(solution)/shard_map/ppermute | solution.py:1298
  1141.3 39.0 %collective-permute-start.164 = (bf16[768,768]{1,0:T(8,128)(2,1)}, bf16[768,768]{1,0:T(8,128)(2,1)S(1)}, u32[]{:S(2)}, u32[]{:S(2)}) collective-permute-start(bf16[768,768]{1,0:T(8,128)(2,1)} %get-tuple-element.613.refs_24_), channel_id=1, source_target_pairs={{0,2},{2,0},{1,3},{3,1},{4,6},{6,4},{5,7},{7,5},{8,10},{10,8},{9,1... | collective-permute-start | bytes 3538952 | tf_op jit(solution)/shard_map/ppermute | solution.py:1298
  1267.3 33.1 %collective-permute-start.194 = (bf16[96,1024]{1,0:T(8,128)(2,1)S(1)}, bf16[96,1024]{1,0:T(8,128)(2,1)S(1)}, u32[]{:S(2)}, u32[]{:S(2)}) collective-permute-start(bf16[96,1024]{1,0:T(8,128)(2,1)S(1)} %get-tuple-element.669), channel_id=1, source_target_pairs={{0,16},{8,24},{16,0},{24,8},{1,17},{9,25},{17,1},{25,9},{2,18},{10... | collective-permute-start | bytes 589832 | tf_op jit(solution)/shard_map/ppermute | solution.py:1298
  1270.4 30.1 %collective-permute-start.187 = (f32[3,8,768]{2,1,0:T(8,128)S(1)}, f32[3,8,768]{2,1,0:T(8,128)S(1)}, u32[]{:S(2)}, u32[]{:S(2)}) collective-permute-start(f32[3,8,768]{2,1,0:T(8,128)S(1)} %add.308), channel_id=1, source_target_pairs={{0,16},{8,24},{16,0},{24,8},{1,17},{9,25},{17,1},{25,9},{2,18},{10... | collective-permute-start | bytes 221192 | tf_op jit(solution)/shard_map/ppermute | solution.py:1465
  1272.7 35.1 %collective-permute-start.190 = (bf16[96,1024]{1,0:T(8,128)(2,1)S(1)}, bf16[96,1024]{1,0:T(8,128)(2,1)S(1)}, u32[]{:S(2)}, u32[]{:S(2)}) collective-permute-start(bf16[96,1024]{1,0:T(8,128)(2,1)S(1)} %get-tuple-element.638.refs_10_), channel_id=1, source_target_pairs={{0,16},{8,24},{16,0},{24,8},{1,17},{9,25},{17,1},{25,9},{2,18},{10... | collective-permute-start | bytes 589832 | tf_op jit(solution)/shard_map/ppermute | solution.py:1298
  1277.2 36.9 %collective-permute-start.183 = (bf16[96,768]{1,0:T(8,128)(2,1)S(1)}, bf16[96,768]{1,0:T(8,128)(2,1)}, u32[]{:S(2)}, u32[]{:S(2)}) collective-permute-start(bf16[96,768]{1,0:T(8,128)(2,1)S(1)} %copy-done.194), channel_id=1, source_target_pairs={{0,16},{8,24},{16,0},{24,8},{1,17},{9,25},{17,1},{25,9},{2,18},{10... | collective-permute-start | bytes 442376 | tf_op jit(solution)/shard_map/ppermute | solution.py:1298
  (558 other events, 7175.5 us)
Sparse Core Ops, SparseCore 0:
  18.1 115.9 all-gather.3
  137.6 123.2 all-gather.5
  263.8 100.7 all-gather.7

commit v4 on v3

--- a/solution.py
+++ b/solution.py
@@ -487,7 +487,7 @@
     npc = 4 * rows
     mine_out, theirs_out = outs[:2]
     dq_out, dkv_out, bias_out = outs[2:5]
-    do_s, drow, drowc, dq_s, dkv_s, da_s = outs[5:]
+    do_s, drow, drowc, dq_s, dkv_s = outs[5:]
     head = pl.program_id(0)
     base_b = chunk * rows
     base_c = 2 * chunk * rows
@@ -558,61 +558,48 @@
     mask = (ccol[...] <= crow[0:1, :]) & (scol[...] == srow[0:1, :])
     pair(at_c, pl.ds(base_c, cont), lsec_ref[0], drowc[...], mask)
 
-    weight = w_ref[0]
     lower = jnp.logical_not(upper)
     dq_all = jnp.where(lower, dq_s[...] * 0.125, 0.0).astype(BF16)
     q_sum = colsum(dq_all.astype(F32))
     kv_sum = jnp.zeros((1, 128), F32)
-
-    def gather3(value, where):
-        return jnp.concatenate([value[a : a + n] for a, n in where], axis=0)
-
-    def emit(slot, count, ref, row, term):
-        at = pl.ds(slot, count)
-
-        def set_first():
-            da_s[at, :] = term
-
-        def add_next():
-            da_s[at, :] += term
-
-        def finish():
-            ref[row : row + count, :] = (da_s[at, :] + term).astype(BF16)
-
-        pl.when(head == 0)(set_first)
-        pl.when(head == 1)(add_next)
-        pl.when(head == 2)(finish)
-
+    lanes_q = pl.ds(pl.multiple_of(head * 256, 128), 128)
+    lanes_kv = pl.ds(pl.multiple_of(head * 256 + 128, 128), 128)
+    lanes_oth = pl.ds(pl.multiple_of(head * 128, 128), 128)
     for s in range(4):
-        dq = gather3(
-            dq_all,
-            [(s * piece, piece), (chunk + s * piece, piece), (2 * chunk + s * cpiece, cpiece)],
+        spots = (
+            (s * tok, piece, s * piece, s * piece),
+            (s * tok + piece, piece, chunk + s * piece, base_b + s * piece),
+            (s * tok + 2 * piece, cpiece, 2 * chunk + s * cpiece, base_c + s * cpiece),
         )
-        dkv = jnp.concatenate(
-            [
-                dkv_s[s * piece : (s + 1) * piece, :],
-                dkv_s[base_b + s * piece : base_b + (s + 1) * piece, :],
-                dkv_s[base_c + s * cpiece : base_c + (s + 1) * cpiece, :],
-            ],
-            axis=0,
-        ).astype(BF16)
-        kv_sum = kv_sum + colsum(dkv.astype(F32))
-        both = jnp.concatenate([dq, dkv], axis=1)
-        dq_out[s, 0] = both
-        side = mine_out if s % 2 == 0 else theirs_out
-        emit(s * tok, tok, side, (s // 2) * tok, nt(both, weight))
+        for to, size, q_row, k_row in spots:
+            dkv = dkv_s[k_row : k_row + size, :].astype(BF16)
+            kv_sum = kv_sum + colsum(dkv.astype(F32))
+            dq_out[to : to + size, lanes_q] = dq_all[q_row : q_row + size]
+            dq_out[to : to + size, lanes_kv] = dkv
     for t in range(1, rows):
         for s in range(4):
             at = t * chunk + s * piece
-            dkv = jnp.concatenate(
-                [dkv_s[at : at + piece, :], dkv_s[base_b + at : base_b + at + piece, :]], axis=0
-            ).astype(BF16)
-            kv_sum = kv_sum + colsum(dkv.astype(F32))
-            k = (t - 1) * 4 + s
-            dkv_out[k, 0] = dkv
+            to = ((t - 1) * 4 + s) * 2 * piece
+            for k_row in (at, base_b + at):
+                dkv = dkv_s[k_row : k_row + piece, :].astype(BF16)
+                kv_sum = kv_sum + colsum(dkv.astype(F32))
+                dkv_out[to : to + piece, lanes_oth] = dkv
+                to += piece
+
+    def finish():
+        weight = w_ref[0]
+        for s in range(4):
             side = mine_out if s % 2 == 0 else theirs_out
+            term = nt(dq_out[s * tok : (s + 1) * tok, :], weight)
+            side[(s // 2) * tok : (s // 2 + 1) * tok, :] = term.astype(BF16)
+        narrow = jnp.concatenate([weight[:, h * 256 + 128 : (h + 1) * 256] for h in range(3)], axis=1)
+        for k in range(npc - 4):
+            side = mine_out if k % 2 == 0 else theirs_out
             row = 2 * tok + (k // 2) * 2 * piece
-            emit(4 * tok + k * 2 * piece, 2 * piece, side, row, nt(dkv, weight[:, 128:256]))
+            term = nt(dkv_out[k * 2 * piece : (k + 1) * 2 * piece, :], narrow)
+            side[row : row + 2 * piece, :] = term.astype(BF16)
+
+    pl.when(head == 2)(finish)
     bias_out[0] = jnp.broadcast_to(jnp.concatenate([q_sum, kv_sum], axis=1), (8, 256))
 
 
@@ -624,14 +611,12 @@
     shapes = (
         [jax.ShapeDtypeStruct((2 * tok + noth * piece, D), BF16)] * 2
         + [
-            jax.ShapeDtypeStruct((4, 3, tok, 256), BF16),
-            jax.ShapeDtypeStruct((noth, 3, 2 * piece, 128), BF16),
+            jax.ShapeDtypeStruct((4 * tok, D), BF16),
+            jax.ShapeDtypeStruct((noth * 2 * piece, 384), BF16),
             jax.ShapeDtypeStruct((3, 8, 256), F32),
         ]
     )
-    out_specs = [whole_spec(s.shape) for s in shapes[:2]] + [
-        pl.BlockSpec((4, 1, tok, 256), lambda i, sc: (0, i, 0, 0)),
-        pl.BlockSpec((noth, 1, 2 * piece, 128), lambda i, sc: (0, i, 0, 0)),
+    out_specs = [whole_spec(s.shape) for s in shapes[:4]] + [
         pl.BlockSpec((1, 8, 256), lambda i, sc: (i, 0, 0)),
     ]
     at = layer * 8
@@ -646,7 +631,7 @@
                 pl.BlockSpec((1, nk, 128), lambda i, sc: (i, 0, 0)),
                 pl.BlockSpec((1, 2, 1, chunk), lambda i, sc: (i, 0, 0, 0)),
                 pl.BlockSpec((1, 1, cont), lambda i, sc: (i, 0, 0)),
-                pl.BlockSpec((1, D, 256), lambda i, sc: (sc[at + 1], 0, i)),
+                pl.BlockSpec((1, D, D), lambda i, sc: (sc[at + 1], 0, 0)),
             ]
             + attn_inputs(pos)
             + [ANY] * len(deps),
@@ -657,7 +642,6 @@
                 pltpu.VMEM((1, cont), F32),
                 pltpu.VMEM((nq, 128), F32),
                 pltpu.VMEM((nk, 128), F32),
-                pltpu.VMEM((4 * tok + noth * 2 * piece, D), F32),
             ],
         ),
         out_shape=shapes,
@@ -669,45 +653,34 @@
 
 def dw_qkv_kernel(rows, sc, *refs):
     npc = 4 * rows
-    noth = npc - 4
     srcs, (dq_hbm, dkv_hbm) = refs[:npc], refs[npc : npc + 2]
     new_ref, token = refs[npc + 2 : npc + 4]
     own, oth, dq_s, dkv_s, asem, dsem = refs[npc + 4 :]
     token[...] = jnp.zeros_like(token)
-    head = pl.program_id(0)
+    tok, two = srcs[0].shape[0], srcs[4].shape[0]
 
     def rows_of(k):
-        dst = own.at[k] if k < 4 else oth.at[k - 4]
+        dst = own.at[pl.ds(k * tok, tok)] if k < 4 else oth.at[pl.ds((k - 4) * two, two)]
         return pltpu.make_async_copy(srcs[k], dst, asem.at[k])
 
-    def grads_of(h):
-        return [
-            pltpu.make_async_copy(dq_hbm.at[:, h], dq_s.at[:, h], dsem.at[0, h]),
-            pltpu.make_async_copy(dkv_hbm.at[:, h], dkv_s.at[:, h], dsem.at[1, h]),
-        ]
-
-    def begin():
-        for copy in grads_of(0):
-            copy.start()
-        for k in range(npc):
-            rows_of(k).start()
-        for h in (1, 2):
-            for copy in grads_of(h):
-                copy.start()
-        for k in range(npc):
-            rows_of(k).wait()
-
-    pl.when(head == 0)(begin)
-    for copy in grads_of(head):
+    loads = [rows_of(k) for k in range(npc)]
+    grads = [
+        pltpu.make_async_copy(dq_hbm, dq_s, dsem.at[0]),
+        pltpu.make_async_copy(dkv_hbm, dkv_s, dsem.at[1]),
+    ]
+    for copy in [grads[0], *loads[:4], grads[1], *loads[4:]]:
+        copy.start()
+    for copy in [grads[0], *loads[:4]]:
         copy.wait()
-    total = tn(own[0], dq_s[0, head])
-    for s in range(1, 4):
-        total = total + tn(own[s], dq_s[s, head])
-    right = tn(oth[0], dkv_s[0, head])
-    for k in range(1, noth):
-        right = right + tn(oth[k], dkv_s[k, head])
-    new_ref[:, 0:128] = total[:, 0:128].astype(BF16)
-    new_ref[:, 128:256] = (total[:, 128:256] + right).astype(BF16)
+    total = tn(own[...], dq_s[...])
+    for copy in [grads[1], *loads[4:]]:
+        copy.wait()
+    right = tn(oth[...], dkv_s[...])
+    for h in range(HEADS_COL):
+        lo = h * 256
+        new_ref[:, lo : lo + 128] = total[:, lo : lo + 128].astype(BF16)
+        both = total[:, lo + 128 : lo + 256] + right[:, h * 128 : (h + 1) * 128]
+        new_ref[:, lo + 128 : lo + 256] = both.astype(BF16)
 
 
 def dw_qkv(layer, sc, own, oth, dq, dkv, deps=()):
@@ -719,16 +692,16 @@
         strip(functools.partial(dw_qkv_kernel, rows), layer, len(ins), len(deps)),
         grid_spec=pltpu.PrefetchScalarGridSpec(
             num_scalar_prefetch=1,
-            grid=(3,),
+            grid=(1,),
             in_specs=[ANY] * len(ins) + [ANY] * len(deps),
-            out_specs=[pl.BlockSpec((D, 256), lambda i, sc: (0, i)), whole_spec((8, 128))],
+            out_specs=[whole_spec((D, D)), whole_spec((8, 128))],
             scratch_shapes=[
-                pltpu.VMEM((4, tok, D), BF16),
-                pltpu.VMEM((noth, two, D), BF16),
-                pltpu.VMEM((4, 3, tok, 256), BF16),
-                pltpu.VMEM((noth, 3, two, 128), BF16),
+                pltpu.VMEM((4 * tok, D), BF16),
+                pltpu.VMEM((noth * two, D), BF16),
+                pltpu.VMEM(dq.shape, BF16),
+                pltpu.VMEM(dkv.shape, BF16),
                 pltpu.SemaphoreType.DMA((4 * rows,)),
-                pltpu.SemaphoreType.DMA((2, 3)),
+                pltpu.SemaphoreType.DMA((2,)),
             ],
         ),
         out_shape=[

time: 1340 us -> 1320 us (0.985)
  Pallas kernels: 636 us -> 604 us
    pallas_call x6, Pallas kernels: 181 us -> 150 us  [attn_bwd(): pl.pallas_call(strip(functools.partial(attn_bwd_kernel, dims), layer, 13...]
  transfers between devices with their start and end apart: 200 -> 200, of which waited for: 75 -> 77; matrix products, arithmetic and copies ran while one was open for 2% -> 2% of each run, Pallas kernels for 34% -> 33%
where the time goes in v4:
time: 1320 us; the launch traced here: 1310 us
  Pallas kernels  604 us (46%)
  waiting for transfers between devices  377 us (29%)
  starting transfers between devices  174 us (13%)
  local copies, waits for them, and re-layouts  122 us (9%)
  between operations  24.2 us (2%)
    pallas_call x6, Pallas kernels, attn_bwd(): pl.pallas_call(strip(functools.partial(attn_bwd_kernel, dims), layer, 13...  150 us
    pallas_call x6, Pallas kernels, attn_fwd(): pl.pallas_call(strip(functools.partial(attn_fwd_kernel, dims), layer, cou...  132 us
    unnamed x792, local copies, waits for them, and re-layouts  109 us
    ppermute x14, waiting for transfers between devices, gather_begin(): lax.ppermute(value, names, [(i, i ^ t) for i in range(total)])  100 us
    pallas_call x6, Pallas kernels, mlp_bwd(): pl.pallas_call(strip(kernel, layer, len(ins), len(deps)), grid_spec=pltpu...  79.5 us
    ppermute x51, waiting for transfers between devices, exchange_heads(): out.append(lax.ppermute(parts[s], ('x', 'core'), pairs))  60.5 us
    ppermute x13, waiting for transfers between devices, swap_x(): return lax.ppermute(value, 'x', SWAP)  55.1 us
    pallas_call x3, Pallas kernels, dw_last(): pl.pallas_call(strip(functools.partial(dw_last_kernel, layer, groups, slo...  53.6 us
  transfers between devices with their start and end apart: 200, of which 77 were waited for; matrix products, arithmetic and copies ran while one was open for 2% of the time, Pallas kernels for 33%

profile of v4, /device:TPU:0, one launch (start us, length us, event | category | flops | bytes accessed | tf_op | source)
XLA Modules:
  0.0 1308.7 jit_solution(7628537609448836250)
XLA Ops:
  52.2 11.7 collective-permute-start.17
  104.4 21.9 %attn_fwd.6 = (bf16[288,256]{1,0:T(8,128)(2,1)S(1)}, bf16[288,256]{1,0:T(8,128)(2,1)S(1)}, bf16[288,256]{1,0:T(8,128)(2,1)S(1)}, bf16[288,256]{1,0:T(8,128)(2,1)...) custom-call(s32[55]{0:T(128)S(1)} %concatenate.19.sc, ...), custom_call_target="tpu_custom_call" | custom-call | flops 6568280064 | bytes 12000000 | tf_op jit(solution)/shard_map/attn_fwd/pallas_call | solution.py:455
  155.7 37.6 %collective-permute-done.35.refs_5_ = bf16[2,96,768]{2,1,0:T(8,128)(2,1)} collective-permute-done((bf16[2,96,768]{2,1,0:T(8,128)(2,1)}, bf16[2,96,768]{2,1,0:T(8,128)(2,1)}, u32[]{:S(2)}, u32[]{:S(2)}) %collective-permute-start.35) | collective-permute-done | bytes 294944 | tf_op jit(solution)/shard_map/ppermute | solution.py:1077
  195.9 11.6 collective-permute-done.34.refs_4_
  222.2 14.9 %collective-permute-done.31.refs_1_ = bf16[2,96,768]{2,1,0:T(8,128)(2,1)S(1)} collective-permute-done((bf16[2,96,768]{2,1,0:T(8,128)(2,1)S(1)}, bf16[2,96,768]{2,1,0:T(8,128)(2,1)S(1)}, u32[]{:S(2)}, u32[]{:S(2)}) %collective-permute-start.31) | collective-permute-done | bytes 294944 | tf_op jit(solution)/shard_map/ppermute | solution.py:1077
  242.6 22.0 %attn_fwd.7 = (bf16[288,256]{1,0:T(8,128)(2,1)S(1)}, bf16[288,256]{1,0:T(8,128)(2,1)S(1)}, bf16[288,256]{1,0:T(8,128)(2,1)S(1)}, bf16[288,256]{1,0:T(8,128)(2,1)...) custom-call(s32[55]{0:T(128)S(1)} %concatenate.19.sc, ...), custom_call_target="tpu_custom_call" | custom-call | flops 6568280064 | bytes 12000000 | tf_op jit(solution)/shard_map/attn_fwd/pallas_call | solution.py:455
  293.0 19.2 %collective-permute-done.42.refs_2_ = bf16[288,768]{1,0:T(8,128)(2,1)} collective-permute-done((bf16[288,768]{1,0:T(8,128)(2,1)}, bf16[288,768]{1,0:T(8,128)(2,1)}, u32[]{:S(2)}, u32[]{:S(2)}) %collective-permute-start.42) | collective-permute-done | bytes 442400 | tf_op jit(solution)/shard_map/ppermute | solution.py:972
  324.2 22.7 %attn_fwd.8 = (bf16[288,256]{1,0:T(8,128)(2,1)S(1)}, bf16[288,256]{1,0:T(8,128)(2,1)S(1)}, bf16[288,256]{1,0:T(8,128)(2,1)}, bf16[288,256]{1,0:T(8,128)(2,1)}, b...) custom-call(s32[55]{0:T(128)S(1)} %concatenate.19.sc, ...), custom_call_target="tpu_custom_call" | custom-call | flops 6568280064 | bytes 12000000 | tf_op jit(solution)/shard_map/attn_fwd/pallas_call | solution.py:455
  352.1 12.5 all-gather.8.cloned.1.call-done
  398.0 21.9 %attn_fwd.9 = (bf16[288,256]{1,0:T(8,128)(2,1)S(1)}, bf16[288,256]{1,0:T(8,128)(2,1)S(1)}, bf16[288,256]{1,0:T(8,128)(2,1)S(1)}, bf16[288,256]{1,0:T(8,128)(2,1)...) custom-call(s32[55]{0:T(128)S(1)} %concatenate.19.sc, ...), custom_call_target="tpu_custom_call" | custom-call | flops 6568280064 | bytes 12000000 | tf_op jit(solution)/shard_map/attn_fwd/pallas_call | solution.py:455
  469.9 22.0 %attn_fwd.10 = (bf16[288,256]{1,0:T(8,128)(2,1)S(1)}, bf16[288,256]{1,0:T(8,128)(2,1)S(1)}, bf16[288,256]{1,0:T(8,128)(2,1)S(1)}, bf16[288,256]{1,0:T(8,128)(2,1...) custom-call(s32[55]{0:T(128)S(1)} %concatenate.19.sc, ...), custom_call_target="tpu_custom_call" | custom-call | flops 6568280064 | bytes 12000000 | tf_op jit(solution)/shard_map/attn_fwd/pallas_call | solution.py:455
  513.7 9.5 collective-permute-done.76.refs_2_
  534.2 21.8 %attn_fwd.11 = (bf16[288,256]{1,0:T(8,128)(2,1)S(1)}, bf16[288,256]{1,0:T(8,128)(2,1)S(1)}, bf16[288,256]{1,0:T(8,128)(2,1)S(1)}, bf16[288,256]{1,0:T(8,128)(2,1...) custom-call(s32[55]{0:T(128)S(1)} %concatenate.19.sc, ...), custom_call_target="tpu_custom_call" | custom-call | flops 6568280064 | bytes 12000000 | tf_op jit(solution)/shard_map/attn_fwd/pallas_call | solution.py:455
  577.9 12.5 mlp_bwd.6
  604.4 24.8 %attn_bwd.6 = (bf16[1088,768]{1,0:T(8,128)(2,1)}, bf16[1088,768]{1,0:T(8,128)(2,1)}, bf16[1152,768]{1,0:T(8,128)(2,1)}, bf16[1024,384]{1,0:T(8,128)(2,1)}, f32[3,8,256]{2,1,0:T(8,128)}) custom-call(s32[55]{0:T(128)} %copy-done.42, bf16[288,256]{1,0:T(8,128)(2,1)} %get-tuple-element.417.refs_0_, bf16[288,256]{1,0:T(8,128)(2,1)} %copy-done.380, ...), custom_call_target="tpu_custom_call" | custom-call | flops 12343836672 | bytes 14000000 | tf_op jit(solution)/shard_map/attn_bwd/pallas_call | solution.py:623
  652.1 12.8 dw_mlp.3
  665.7 13.0 mlp_bwd.7
  689.6 25.0 %attn_bwd.7 = (bf16[1088,768]{1,0:T(8,128)(2,1)}, bf16[1088,768]{1,0:T(8,128)(2,1)}, bf16[1152,768]{1,0:T(8,128)(2,1)}, bf16[1024,384]{1,0:T(8,128)(2,1)}, f32[3,8,256]{2,1,0:T(8,128)}) custom-call(s32[55]{0:T(128)} %copy-done.42, bf16[288,256]{1,0:T(8,128)(2,1)} %copy-done.308, bf16[288,256]{1,0:T(8,128)(2,1)} %copy-done.382, bf16[288,256]{1,0:T(8,128)(2,1)} %copy-done.385, ...), custom_call_target="tpu_custom_call" | custom-call | flops 12343836672 | bytes 14000000 | tf_op jit(solution)/shard_map/attn_bwd/pallas_call | solution.py:623
  734.3 13.1 %dw_mlp.4 = (bf16[3,2,768,1792]{3,2,1,0:T(8,128)(2,1)}, f32[8,128]{1,0:T(8,128)}) custom-call(s32[55]{0:T(128)} %copy-done.42, bf16[3,288,768]{2,1,0:T(8,128)(2,1)} %get-tuple-element.463.refs_0_, bf16[3,288,768]{2,1,0:T(8,128)(2,1)} %collective-permute-done.107.refs_1_, ...), custom_call_target="tpu_custom_call", output_to_operand_aliasing={{0}: (9, {})} | custom-call | flops 3170893824 | bytes 20000000 | tf_op jit(solution)/shard_map/dw_mlp/pallas_call | solution.py:800
  748.2 13.0 mlp_bwd.8
  772.1 25.0 %attn_bwd.8 = (bf16[1088,768]{1,0:T(8,128)(2,1)}, bf16[1088,768]{1,0:T(8,128)(2,1)}, bf16[1152,768]{1,0:T(8,128)(2,1)}, bf16[1024,384]{1,0:T(8,128)(2,1)}, f32[3,8,256]{2,1,0:T(8,128)}) custom-call(s32[55]{0:T(128)} %copy-done.42, bf16[288,256]{1,0:T(8,128)(2,1)} %copy-done.309, bf16[288,256]{1,0:T(8,128)(2,1)} %copy-done.383, bf16[288,256]{1,0:T(8,128)(2,1)} %copy-done.386, ...), custom_call_target="tpu_custom_call" | custom-call | flops 12343836672 | bytes 14000000 | tf_op jit(solution)/shard_map/attn_bwd/pallas_call | solution.py:623
  816.7 12.9 dw_mlp.5
  830.4 13.0 mlp_bwd.9
  853.8 18.1 %dw_last.3 = (bf16[768,768]{1,0:T(8,128)(2,1)}, bf16[768,768]{1,0:T(8,128)(2,1)}, bf16[768,1024]{1,0:T(8,128)(2,1)}, bf16[768,1024]{1,0:T(8,128)(2,1)}, bf16[3,2...) custom-call(s32[55]{0:T(128)} %copy-done.42, ...), custom_call_target="tpu_custom_call", output_to_operand_aliasing={{4}: (9, {})} | custom-call | flops 3170893824 | bytes 20000000 | tf_op jit(solution)/shard_map/dw_last/pallas_call | solution.py:901
  876.1 24.9 %attn_bwd.9 = (bf16[1088,768]{1,0:T(8,128)(2,1)}, bf16[1088,768]{1,0:T(8,128)(2,1)}, bf16[1152,768]{1,0:T(8,128)(2,1)}, bf16[1024,384]{1,0:T(8,128)(2,1)}, f32[3,8,256]{2,1,0:T(8,128)}) custom-call(s32[55]{0:T(128)} %copy-done.42, bf16[288,256]{1,0:T(8,128)(2,1)} %copy-done.303, bf16[288,256]{1,0:T(8,128)(2,1)} %copy-done.342, bf16[288,256]{1,0:T(8,128)(2,1)} %copy-done.343, ...), custom_call_target="tpu_custom_call" | custom-call | flops 12343836672 | bytes 14000000 | tf_op jit(solution)/shard_map/attn_bwd/pallas_call | solution.py:623
  946.6 14.0 %mlp_bwd.10 = (bf16[3,288,768]{2,1,0:T(8,128)(2,1)}, bf16[4,288,768]{2,1,0:T(8,128)(2,1)}, bf16[4,288,768]{2,1,0:T(8,128)(2,1)}, f32[288,768]{1,0:T(8,128)S(1)},...) custom-call(s32[55]{0:T(128)S(1)} %copy-done.48, ...), custom_call_target="tpu_custom_call" | custom-call | flops 3057647616 | bytes 16000000 | tf_op jit(solution)/shard_map/mlp_bwd/pallas_call | solution.py:296
  974.6 17.8 %dw_last.4 = (bf16[768,768]{1,0:T(8,128)(2,1)}, bf16[768,768]{1,0:T(8,128)(2,1)}, bf16[768,1024]{1,0:T(8,128)(2,1)}, bf16[768,1024]{1,0:T(8,128)(2,1)}, bf16[3,2...) custom-call(s32[55]{0:T(128)} %copy-done.42, ...), custom_call_target="tpu_custom_call", output_to_operand_aliasing={{4}: (9, {})} | custom-call | flops 3170893824 | bytes 20000000 | tf_op jit(solution)/shard_map/dw_last/pallas_call | solution.py:901
  1001.6 25.3 %attn_bwd.10 = (bf16[1088,768]{1,0:T(8,128)(2,1)}, bf16[1088,768]{1,0:T(8,128)(2,1)}, bf16[1152,768]{1,0:T(8,128)(2,1)}, bf16[1024,384]{1,0:T(8,128)(2,1)}, f32[3,8,256]{2,1,0:T(8,128)}) custom-call(s32[55]{0:T(128)} %copy-done.42, bf16[288,256]{1,0:T(8,128)(2,1)} %get-tuple-element.542.refs_0_, bf16[288,256]{1,0:T(8,128)(2,1)} %copy-done.340, ...), custom_call_target="tpu_custom_call" | custom-call | flops 12343836672 | bytes 14000000 | tf_op jit(solution)/shard_map/attn_bwd/pallas_call | solution.py:623
  1072.0 14.0 %mlp_bwd.11 = (bf16[3,288,768]{2,1,0:T(8,128)(2,1)}, bf16[4,288,768]{2,1,0:T(8,128)(2,1)}, bf16[4,288,768]{2,1,0:T(8,128)(2,1)}, f32[288,768]{1,0:T(8,128)S(1)},...) custom-call(s32[55]{0:T(128)S(1)} %copy-done.51, ...), custom_call_target="tpu_custom_call" | custom-call | flops 3057647616 | bytes 16000000 | tf_op jit(solution)/shard_map/mlp_bwd/pallas_call | solution.py:296
  1101.5 17.8 %dw_last.5 = (bf16[768,768]{1,0:T(8,128)(2,1)}, bf16[768,768]{1,0:T(8,128)(2,1)}, bf16[768,1024]{1,0:T(8,128)(2,1)}, bf16[768,1024]{1,0:T(8,128)(2,1)}, bf16[3,2...) custom-call(s32[55]{0:T(128)} %copy-done.42, ...), custom_call_target="tpu_custom_call", output_to_operand_aliasing={{4}: (9, {})} | custom-call | flops 3170893824 | bytes 20000000 | tf_op jit(solution)/shard_map/dw_last/pallas_call | solution.py:901
  1125.1 24.9 %attn_bwd.11 = (bf16[1088,768]{1,0:T(8,128)(2,1)}, bf16[1088,768]{1,0:T(8,128)(2,1)}, bf16[1152,768]{1,0:T(8,128)(2,1)}, bf16[1024,384]{1,0:T(8,128)(2,1)}, f32[3,8,256]{2,1,0:T(8,128)}) custom-call(s32[55]{0:T(128)} %copy-done.42, bf16[288,256]{1,0:T(8,128)(2,1)} %get-tuple-element.597.refs_0_, bf16[288,256]{1,0:T(8,128)(2,1)} %collective-permute-done.156.refs_2_.refs_1_, ...), custom_call_target="tpu_custom_call" | custom-call | flops 12343836672 | bytes 14000000 | tf_op jit(solution)/shard_map/attn_bwd/pallas_call | solution.py:623
  1259.1 11.9 collective-permute-done.189.refs_1_
  (1332 shorter events, 701.3 us)
Async XLA Ops:
  7.2 134.0 %all-gather.4.cloned.1.call-start = ((), (), s32[]{:S(2)}) async-start(), calls=%async_computation | async-start | bytes 11354112 | tf_op jit(solution)/shard_map/all_gather | solution.py:1531
  18.0 251.8 %all-gather.6.cloned.1.call-start = ((), (), s32[]{:S(2)}) async-start(), calls=%async_computation.1 | async-start | bytes 11354112 | tf_op jit(solution)/shard_map/all_gather | solution.py:1531
  18.7 345.9 %all-gather.8.cloned.1.call-start = ((), (), s32[]{:S(2)}) async-start(), calls=%async_computation.2 | async-start | bytes 11354112 | tf_op jit(solution)/shard_map/all_gather | solution.py:1531
  43.6 28.9 %collective-permute-start.18 = (bf16[1,96,768]{2,1,0:T(8,128)(2,1)}, bf16[1,96,768]{2,1,0:T(8,128)(2,1)S(1)}, u32[]{:S(2)}, u32[]{:S(2)}) collective-permute-start(bf16[1,96,768]{2,1,0:T(8,128)(2,1)} %held.2.refs_0_), channel_id=1, source_target_pairs={{0,20},{4,16},{8,28},{12,24},{16,4},{20,0},{24,12},{28,8},{1,21},{... | collective-permute-start | bytes 442376 | tf_op jit(solution)/shard_map/ppermute | solution.py:1077
  45.7 39.0 %collective-permute-start.12 = (bf16[256,768]{1,0:T(8,128)(2,1)S(1)}, bf16[256,768]{1,0:T(8,128)(2,1)}, u32[]{:S(2)}, u32[]{:S(2)}) collective-permute-start(bf16[256,768]{1,0:T(8,128)(2,1)S(1)} %get-tuple-element.355), channel_id=1, source_target_pairs={{0,6},{2,4},{4,2},{6,0},{1,7},{3,5},{5,3},{7,1},{8,14},{10,12},{12... | collective-permute-start | bytes 1179656 | tf_op jit(solution)/shard_map/ppermute | solution.py:983
  48.6 36.6 %collective-permute-start.10 = (bf16[256,768]{1,0:T(8,128)(2,1)S(1)}, bf16[256,768]{1,0:T(8,128)(2,1)S(1)}, u32[]{:S(2)}, u32[]{:S(2)}) collective-permute-start(bf16[256,768]{1,0:T(8,128)(2,1)S(1)} %get-tuple-element.355), channel_id=1, source_target_pairs={{0,4},{4,0},{1,5},{5,1},{2,6},{6,2},{3,7},{7,3},{8,12},{12,8},{9,1... | collective-permute-start | bytes 1179656 | tf_op jit(solution)/shard_map/ppermute | solution.py:977
  48.7 36.5 %collective-permute-start.8 = (bf16[288,768]{1,0:T(8,128)(2,1)S(1)}, bf16[288,768]{1,0:T(8,128)(2,1)}, u32[]{:S(2)}, u32[]{:S(2)}) collective-permute-start(bf16[288,768]{1,0:T(8,128)(2,1)S(1)} %get-tuple-element.354.refs_8_.refs_0_), channel_id=1, source_target_pairs={{0,2},{2,0},{1,3},{3,1},{4,6},{6,4},{5,7},{7,5},{8,10},{10,8},{9,1... | collective-permute-start | bytes 1327112 | tf_op jit(solution)/shard_map/ppermute | solution.py:972
  136.1 57.3 %collective-permute-start.35 = (bf16[2,96,768]{2,1,0:T(8,128)(2,1)}, bf16[2,96,768]{2,1,0:T(8,128)(2,1)}, u32[]{:S(2)}, u32[]{:S(2)}) collective-permute-start(bf16[2,96,768]{2,1,0:T(8,128)(2,1)} %held.3.refs_0_), channel_id=1, source_target_pairs={{0,20},{4,16},{8,28},{12,24},{16,4},{20,0},{24,12},{28,8},{1,21},{... | collective-permute-start | bytes 884744 | tf_op jit(solution)/shard_map/ppermute | solution.py:1077
  137.1 70.4 %collective-permute-start.34 = (bf16[2,96,768]{2,1,0:T(8,128)(2,1)}, bf16[2,96,768]{2,1,0:T(8,128)(2,1)}, u32[]{:S(2)}, u32[]{:S(2)}) collective-permute-start(bf16[2,96,768]{2,1,0:T(8,128)(2,1)} %held.3.refs_0_), channel_id=1, source_target_pairs={{0,16},{4,20},{8,24},{12,28},{16,0},{20,4},{24,8},{28,12},{1,17},{... | collective-permute-start | bytes 884744 | tf_op jit(solution)/shard_map/ppermute | solution.py:1077
  152.2 62.4 %collective-permute-start.25 = (bf16[288,768]{1,0:T(8,128)(2,1)S(1)}, bf16[288,768]{1,0:T(8,128)(2,1)S(1)}, u32[]{:S(2)}, u32[]{:S(2)}) collective-permute-start(bf16[288,768]{1,0:T(8,128)(2,1)S(1)} %get-tuple-element.361.refs_9_.refs_0_), channel_id=1, source_target_pairs={{0,2},{2,0},{1,3},{3,1},{4,6},{6,4},{5,7},{7,5},{8,10},{10,8},{9,1... | collective-permute-start | bytes 1327112 | tf_op jit(solution)/shard_map/ppermute | solution.py:972
  154.0 61.2 %collective-permute-start.29 = (bf16[256,768]{1,0:T(8,128)(2,1)S(1)}, bf16[256,768]{1,0:T(8,128)(2,1)S(1)}, u32[]{:S(2)}, u32[]{:S(2)}) collective-permute-start(bf16[256,768]{1,0:T(8,128)(2,1)S(1)} %get-tuple-element.362), channel_id=1, source_target_pairs={{0,6},{2,4},{4,2},{6,0},{1,7},{3,5},{5,3},{7,1},{8,14},{10,12},{12... | collective-permute-start | bytes 1179656 | tf_op jit(solution)/shard_map/ppermute | solution.py:983
  154.0 61.2 %collective-permute-start.27 = (bf16[256,768]{1,0:T(8,128)(2,1)S(1)}, bf16[256,768]{1,0:T(8,128)(2,1)S(1)}, u32[]{:S(2)}, u32[]{:S(2)}) collective-permute-start(bf16[256,768]{1,0:T(8,128)(2,1)S(1)} %get-tuple-element.362), channel_id=1, source_target_pairs={{0,4},{4,0},{1,5},{5,1},{2,6},{6,2},{3,7},{7,3},{8,12},{12,8},{9,1... | collective-permute-start | bytes 1179656 | tf_op jit(solution)/shard_map/ppermute | solution.py:977
  291.0 29.5 %collective-permute-start.46 = (bf16[256,768]{1,0:T(8,128)(2,1)S(1)}, bf16[256,768]{1,0:T(8,128)(2,1)}, u32[]{:S(2)}, u32[]{:S(2)}) collective-permute-start(bf16[256,768]{1,0:T(8,128)(2,1)S(1)} %get-tuple-element.370), channel_id=1, source_target_pairs={{0,6},{2,4},{4,2},{6,0},{1,7},{3,5},{5,3},{7,1},{8,14},{10,12},{12... | collective-permute-start | bytes 1179656 | tf_op jit(solution)/shard_map/ppermute | solution.py:983
  291.4 29.1 %collective-permute-start.44 = (bf16[256,768]{1,0:T(8,128)(2,1)S(1)}, bf16[256,768]{1,0:T(8,128)(2,1)S(1)}, u32[]{:S(2)}, u32[]{:S(2)}) collective-permute-start(bf16[256,768]{1,0:T(8,128)(2,1)S(1)} %get-tuple-element.370), channel_id=1, source_target_pairs={{0,4},{4,0},{1,5},{5,1},{2,6},{6,2},{3,7},{7,3},{8,12},{12,8},{9,1... | collective-permute-start | bytes 1179656 | tf_op jit(solution)/shard_map/ppermute | solution.py:977
  293.0 31.2 %collective-permute-start.41 = (bf16[288,768]{1,0:T(8,128)(2,1)}, bf16[288,768]{1,0:T(8,128)(2,1)}, u32[]{:S(2)}, u32[]{:S(2)}) collective-permute-start(bf16[288,768]{1,0:T(8,128)(2,1)} %get-tuple-element.369.refs_0_), channel_id=1, source_target_pairs={{0,1},{1,0},{2,3},{3,2},{4,5},{5,4},{6,7},{7,6},{8,9},{9,8},{10,11... | collective-permute-start | bytes 1327112 | tf_op jit(solution)/shard_map/ppermute | solution.py:968
  322.6 27.5 %collective-permute-start.51 = (bf16[512,192]{1,0:T(8,128)(2,1)}, bf16[512,192]{1,0:T(8,128)(2,1)S(1)}, u32[]{:S(2)}, u32[]{:S(2)}) collective-permute-start(bf16[512,192]{1,0:T(8,128)(2,1)} %bitcast.40), channel_id=1, source_target_pairs={{0,4},{4,0},{1,5},{5,1},{2,6},{6,2},{3,7},{7,3},{8,12},{12,8},{9,1... | collective-permute-start | bytes 589832 | tf_op jit(solution)/shard_map/ppermute | solution.py:1177
  395.4 28.1 %collective-permute-start.62 = (bf16[288,192]{1,0:T(8,128)(2,1)S(1)}, bf16[288,192]{1,0:T(8,128)(2,1)S(1)}, u32[]{:S(2)}, u32[]{:S(2)}) collective-permute-start(bf16[288,192]{1,0:T(8,128)(2,1)S(1)} %copy-done.307), channel_id=1, source_target_pairs={{0,1},{1,0},{2,3},{3,2},{4,5},{5,4},{6,7},{7,6},{8,9},{9,8},{10,11... | collective-permute-start | bytes 331784 | tf_op jit(solution)/shard_map/ppermute | solution.py:1005
  596.9 32.2 %collective-permute-start.88 = (bf16[512,192]{1,0:T(8,128)(2,1)S(1)}, bf16[512,192]{1,0:T(8,128)(2,1)S(1)}, u32[]{:S(2)}, u32[]{:S(2)}) collective-permute-start(bf16[512,192]{1,0:T(8,128)(2,1)S(1)} %get-tuple-element.410), channel_id=1, source_target_pairs={{4,0},{0,4},{5,1},{1,5},{6,2},{2,6},{7,3},{3,7},{12,8},{8,12},{13,... | collective-permute-start | bytes 589832 | tf_op jit(solution)/shard_map/ppermute | solution.py:1216
  872.7 36.7 %collective-permute-start.130 = (bf16[768,1024]{1,0:T(8,128)(2,1)}, bf16[768,1024]{1,0:T(8,128)(2,1)S(1)}, u32[]{:S(2)}, u32[]{:S(2)}) collective-permute-start(bf16[768,1024]{1,0:T(8,128)(2,1)} %get-tuple-element.508.refs_21_), channel_id=1, source_target_pairs={{0,4},{4,0},{1,5},{5,1},{2,6},{6,2},{3,7},{7,3},{8,12},{12,8},{9,1... | collective-permute-start | bytes 4718600 | tf_op jit(solution)/shard_map/ppermute | solution.py:1271
  874.5 27.9 %collective-permute-start.129 = (bf16[768,768]{1,0:T(8,128)(2,1)}, bf16[768,768]{1,0:T(8,128)(2,1)S(1)}, u32[]{:S(2)}, u32[]{:S(2)}) collective-permute-start(bf16[768,768]{1,0:T(8,128)(2,1)} %get-tuple-element.507.refs_20_), channel_id=1, source_target_pairs={{0,2},{2,0},{1,3},{3,1},{4,6},{6,4},{5,7},{7,5},{8,10},{10,8},{9,1... | collective-permute-start | bytes 3538952 | tf_op jit(solution)/shard_map/ppermute | solution.py:1271
  967.5 30.2 %collective-permute-start.144 = (bf16[384,768]{1,0:T(8,128)(2,1)}, bf16[384,768]{1,0:T(8,128)(2,1)}, u32[]{:S(2)}, u32[]{:S(2)}) collective-permute-start(bf16[384,768]{1,0:T(8,128)(2,1)} %get-tuple-element.529.refs_14_), channel_id=1, source_target_pairs={{0,4},{4,0},{1,5},{5,1},{2,6},{6,2},{3,7},{7,3},{8,12},{12,8},{9,1... | collective-permute-start | bytes 1769480 | tf_op jit(solution)/shard_map/ppermute | solution.py:1271
  993.1 39.2 %collective-permute-start.149 = (bf16[768,1024]{1,0:T(8,128)(2,1)}, bf16[768,1024]{1,0:T(8,128)(2,1)S(1)}, u32[]{:S(2)}, u32[]{:S(2)}) collective-permute-start(bf16[768,1024]{1,0:T(8,128)(2,1)} %get-tuple-element.560.refs_25_), channel_id=1, source_target_pairs={{0,4},{4,0},{1,5},{5,1},{2,6},{6,2},{3,7},{7,3},{8,12},{12,8},{9,1... | collective-permute-start | bytes 4718600 | tf_op jit(solution)/shard_map/ppermute | solution.py:1271
  994.3 35.5 %collective-permute-start.148 = (bf16[768,768]{1,0:T(8,128)(2,1)}, bf16[768,768]{1,0:T(8,128)(2,1)S(1)}, u32[]{:S(2)}, u32[]{:S(2)}) collective-permute-start(bf16[768,768]{1,0:T(8,128)(2,1)} %get-tuple-element.559.refs_24_), channel_id=1, source_target_pairs={{0,2},{2,0},{1,3},{3,1},{4,6},{6,4},{5,7},{7,5},{8,10},{10,8},{9,1... | collective-permute-start | bytes 3538952 | tf_op jit(solution)/shard_map/ppermute | solution.py:1271
  995.6 32.9 %collective-permute-start.145 = (bf16[192,768]{1,0:T(8,128)(2,1)}, bf16[192,768]{1,0:T(8,128)(2,1)S(1)}, u32[]{:S(2)}, u32[]{:S(2)}) collective-permute-start(bf16[192,768]{1,0:T(8,128)(2,1)} %copy-done.150), channel_id=1, source_target_pairs={{0,8},{8,0},{16,24},{24,16},{1,9},{9,1},{17,25},{25,17},{2,10},{10... | collective-permute-start | bytes 884744 | tf_op jit(solution)/shard_map/ppermute | solution.py:1271
  997.7 29.2 %collective-permute-start.146 = (bf16[192,1024]{1,0:T(8,128)(2,1)}, bf16[192,1024]{1,0:T(8,128)(2,1)S(1)}, u32[]{:S(2)}, u32[]{:S(2)}) collective-permute-start(bf16[192,1024]{1,0:T(8,128)(2,1)} %copy-done.141), channel_id=1, source_target_pairs={{0,8},{8,0},{16,24},{24,16},{1,9},{9,1},{17,25},{25,17},{2,10},{10... | collective-permute-start | bytes 1179656 | tf_op jit(solution)/shard_map/ppermute | solution.py:1271
  999.5 29.6 %collective-permute-start.147 = (bf16[192,768]{1,0:T(8,128)(2,1)S(1)}, bf16[192,768]{1,0:T(8,128)(2,1)S(1)}, u32[]{:S(2)}, u32[]{:S(2)}) collective-permute-start(bf16[192,768]{1,0:T(8,128)(2,1)S(1)} %get-tuple-element.556.refs_20_.refs_23_), channel_id=1, source_target_pairs={{0,8},{8,0},{16,24},{24,16},{1,9},{9,1},{17,25},{25,17},{2,10},{10... | collective-permute-start | bytes 884744 | tf_op jit(solution)/shard_map/ppermute | solution.py:1271
  1120.0 36.9 %collective-permute-start.166 = (bf16[768,1024]{1,0:T(8,128)(2,1)}, bf16[768,1024]{1,0:T(8,128)(2,1)S(1)}, u32[]{:S(2)}, u32[]{:S(2)}) collective-permute-start(bf16[768,1024]{1,0:T(8,128)(2,1)} %get-tuple-element.614.refs_25_), channel_id=1, source_target_pairs={{0,4},{4,0},{1,5},{5,1},{2,6},{6,2},{3,7},{7,3},{8,12},{12,8},{9,1... | collective-permute-start | bytes 4718600 | tf_op jit(solution)/shard_map/ppermute | solution.py:1271
  1120.9 39.0 %collective-permute-start.164 = (bf16[768,768]{1,0:T(8,128)(2,1)}, bf16[768,768]{1,0:T(8,128)(2,1)S(1)}, u32[]{:S(2)}, u32[]{:S(2)}) collective-permute-start(bf16[768,768]{1,0:T(8,128)(2,1)} %get-tuple-element.613.refs_24_), channel_id=1, source_target_pairs={{0,2},{2,0},{1,3},{3,1},{4,6},{6,4},{5,7},{7,5},{8,10},{10,8},{9,1... | collective-permute-start | bytes 3538952 | tf_op jit(solution)/shard_map/ppermute | solution.py:1271
  1247.0 33.1 %collective-permute-start.194 = (bf16[96,1024]{1,0:T(8,128)(2,1)S(1)}, bf16[96,1024]{1,0:T(8,128)(2,1)S(1)}, u32[]{:S(2)}, u32[]{:S(2)}) collective-permute-start(bf16[96,1024]{1,0:T(8,128)(2,1)S(1)} %get-tuple-element.669), channel_id=1, source_target_pairs={{0,16},{8,24},{16,0},{24,8},{1,17},{9,25},{17,1},{25,9},{2,18},{10... | collective-permute-start | bytes 589832 | tf_op jit(solution)/shard_map/ppermute | solution.py:1271
  1250.0 30.0 %collective-permute-start.187 = (f32[3,8,768]{2,1,0:T(8,128)S(1)}, f32[3,8,768]{2,1,0:T(8,128)S(1)}, u32[]{:S(2)}, u32[]{:S(2)}) collective-permute-start(f32[3,8,768]{2,1,0:T(8,128)S(1)} %add.308), channel_id=1, source_target_pairs={{0,16},{8,24},{16,0},{24,8},{1,17},{9,25},{17,1},{25,9},{2,18},{10... | collective-permute-start | bytes 221192 | tf_op jit(solution)/shard_map/ppermute | solution.py:1438
  1252.3 35.1 %collective-permute-start.190 = (bf16[96,1024]{1,0:T(8,128)(2,1)S(1)}, bf16[96,1024]{1,0:T(8,128)(2,1)S(1)}, u32[]{:S(2)}, u32[]{:S(2)}) collective-permute-start(bf16[96,1024]{1,0:T(8,128)(2,1)S(1)} %get-tuple-element.638.refs_10_), channel_id=1, source_target_pairs={{0,16},{8,24},{16,0},{24,8},{1,17},{9,25},{17,1},{25,9},{2,18},{10... | collective-permute-start | bytes 589832 | tf_op jit(solution)/shard_map/ppermute | solution.py:1271
  1256.8 36.8 %collective-permute-start.183 = (bf16[96,768]{1,0:T(8,128)(2,1)S(1)}, bf16[96,768]{1,0:T(8,128)(2,1)}, u32[]{:S(2)}, u32[]{:S(2)}) collective-permute-start(bf16[96,768]{1,0:T(8,128)(2,1)S(1)} %copy-done.194), channel_id=1, source_target_pairs={{0,16},{8,24},{16,0},{24,8},{1,17},{9,25},{17,1},{25,9},{2,18},{10... | collective-permute-start | bytes 442376 | tf_op jit(solution)/shard_map/ppermute | solution.py:1271
  (558 other events, 7117.1 us)
Sparse Core Ops, SparseCore 0:
  18.1 115.9 all-gather.3
  137.6 123.2 all-gather.5
  263.8 100.7 all-gather.7

commit v5 on v4

--- a/solution.py
+++ b/solution.py
@@ -14,6 +14,7 @@
 NB = 3
 HEADS_COL = 3
 PACK = 1792
+HALF = 896
 NORM_EPS = 1e-05
 MASK_FILL = -1000000000.0
 GELU_COEF = 0.7978845608028654
@@ -755,13 +756,13 @@
         pl.when(tile == 1)(lambda: self.wait(name, 3 if index == "down" else 1))
 
 
-def dw_products(tile, loads, tok, side, outp, put):
+def dw_products(tile, loads, tok, side, outp, put, splits=((0, 256), (256, 512), (512, 768))):
     loads.wait_tile(tile, "side", "up")
     for j in range(3):
         put(j * 256, tn(tok[0], side[tile, :, j * 256 : (j + 1) * 256]))
     loads.wait_tile(tile, "side", "down")
-    for j in range(3):
-        put(768 + j * 256, tn(tok[1], side[2 + tile, :, j * 256 : (j + 1) * 256]))
+    for lo, hi in splits:
+        put(768 + lo, tn(tok[1], side[2 + tile, :, lo:hi]))
     loads.wait_tile(tile, "outp", "out")
     put(1536, tn(tok[2], outp[tile]))
 
@@ -848,10 +849,10 @@
         cols = slice(lo, lo + size)
         old = jnp.where(used, done[tile, :, cols].astype(F32), 0.0)
         total = (old + jnp.where(same, value, 0.0)).astype(BF16)
-        if lo < D:
+        if lo < HALF:
             out_a[tile, :, cols] = total
         else:
-            out_b[tile, :, lo - D : lo - D + size] = total
+            out_b[tile, :, lo - HALF : lo - HALF + size] = total
 
         def add_other():
             before = jnp.where(keep, other[:, cols].astype(F32), 0.0)
@@ -859,7 +860,8 @@
 
         pl.when(jnp.logical_not(same))(add_other)
 
-    dw_products(tile, loads, tok, side, outp, put)
+    splits = ((0, HALF - D), (HALF - D, 384), (384, 640), (640, 768))
+    dw_products(tile, loads, tok, side, outp, put, splits)
 
     def store_other():
         copy = pltpu.make_async_copy(other, acc.at[sc[1], tile], osem)
@@ -897,7 +899,7 @@
 def dw_last(layer, sc, ins, acc, groups, deps=()):
     tok = ins[0].shape[1]
     slot = LAYERS * 8 + 1 + len(bits_of("dp")) - layer * 8
-    halves = [jax.ShapeDtypeStruct((D, n), BF16) for n in (D, D, PACK - D, PACK - D)]
+    halves = [jax.ShapeDtypeStruct((D, n), BF16) for n in (HALF, HALF, PACK - HALF, PACK - HALF)]
     return pl.pallas_call(
         strip(functools.partial(dw_last_kernel, layer, groups, slot), layer, 9, len(deps)),
         grid_spec=pltpu.PrefetchScalarGridSpec(
@@ -911,8 +913,8 @@
                 pltpu.VMEM((D, PACK), BF16),
                 pltpu.SemaphoreType.DMA((2,)),
                 pltpu.SemaphoreType.DMA(()),
-                pltpu.VMEM((2, D, D), BF16),
-                pltpu.VMEM((2, D, PACK - D), BF16),
+                pltpu.VMEM((2, D, HALF), BF16),
+                pltpu.VMEM((2, D, PACK - HALF), BF16),
                 pltpu.SemaphoreType.DMA((2,)),
                 pltpu.SemaphoreType.DMA((2, 2 * groups)),
             ],
@@ -1380,9 +1382,10 @@
             for b in range(NB):
 
                 def put(b=b, left=left, right=right):
-                    up[b] = left
-                    down[b] = right[:, 0:D]
-                    out[b] = right[:, D : D + width]
+                    up[b] = left[:, 0:D]
+                    down[b, :, 0 : HALF - D] = left[:, D:]
+                    down[b, :, HALF - D :] = right[:, 0 : 2 * D - HALF]
+                    out[b] = right[:, 2 * D - HALF : 2 * D - HALF + width]
 
                 pl.when(sc[slot + b] == k)(put)
 

time: 1320 us -> 1310 us (level)
    unnamed x792 -> x778, local copies, waits for them, and re-layouts: 109 us -> 105 us
  transfers between devices with their start and end apart: 200 -> 200, of which waited for: 77 -> 72; matrix products, arithmetic and copies ran while one was open for 2% -> 2% of each run, Pallas kernels for 33% -> 34%
where the time goes in v5:
time: 1310 us
  Pallas kernels  609 us (46%)
  waiting for transfers between devices  376 us (29%)
  starting transfers between devices  171 us (13%)
  local copies, waits for them, and re-layouts  117 us (9%)
  between operations  24.2 us (2%)
    pallas_call x6, Pallas kernels, attn_bwd(): pl.pallas_call(strip(functools.partial(attn_bwd_kernel, dims), layer, 13...  150 us
    pallas_call x6, Pallas kernels, attn_fwd(): pl.pallas_call(strip(functools.partial(attn_fwd_kernel, dims), layer, cou...  132 us
    unnamed x778, local copies, waits for them, and re-layouts  105 us
    ppermute x14, waiting for transfers between devices, gather_begin(): lax.ppermute(value, names, [(i, i ^ t) for i in range(total)])  100 us
    pallas_call x6, Pallas kernels, mlp_bwd(): pl.pallas_call(strip(kernel, layer, len(ins), len(deps)), grid_spec=pltpu...  79.4 us
    pallas_call x3, Pallas kernels, dw_last(): pl.pallas_call(strip(functools.partial(dw_last_kernel, layer, groups, slo...  56.9 us
    ppermute x13, waiting for transfers between devices, swap_x(): return lax.ppermute(value, 'x', SWAP)  54.9 us
    ppermute x51, waiting for transfers between devices, exchange_heads(): out.append(lax.ppermute(parts[s], ('x', 'core'), pairs))  54.3 us
  transfers between devices with their start and end apart: 200, of which 72 were waited for; matrix products, arithmetic and copies ran while one was open for 2% of the time, Pallas kernels for 34%

profile of v5, /device:TPU:0, one launch (start us, length us, event | category | flops | bytes accessed | tf_op | source)
XLA Modules:
  0.0 1305.4 jit_solution(7213916886434160158)
XLA Ops:
  52.2 11.7 collective-permute-start.17
  104.4 21.9 %attn_fwd.6 = (bf16[288,256]{1,0:T(8,128)(2,1)S(1)}, bf16[288,256]{1,0:T(8,128)(2,1)S(1)}, bf16[288,256]{1,0:T(8,128)(2,1)S(1)}, bf16[288,256]{1,0:T(8,128)(2,1)...) custom-call(s32[55]{0:T(128)S(1)} %concatenate.19.sc, ...), custom_call_target="tpu_custom_call" | custom-call | flops 6568280064 | bytes 12000000 | tf_op jit(solution)/shard_map/attn_fwd/pallas_call | solution.py:456
  155.8 37.5 %collective-permute-done.35.refs_5_ = bf16[2,96,768]{2,1,0:T(8,128)(2,1)} collective-permute-done((bf16[2,96,768]{2,1,0:T(8,128)(2,1)}, bf16[2,96,768]{2,1,0:T(8,128)(2,1)}, u32[]{:S(2)}, u32[]{:S(2)}) %collective-permute-start.35) | collective-permute-done | bytes 294944 | tf_op jit(solution)/shard_map/ppermute | solution.py:1079
  195.9 11.6 collective-permute-done.34.refs_4_
  222.2 14.9 %collective-permute-done.31.refs_1_ = bf16[2,96,768]{2,1,0:T(8,128)(2,1)S(1)} collective-permute-done((bf16[2,96,768]{2,1,0:T(8,128)(2,1)S(1)}, bf16[2,96,768]{2,1,0:T(8,128)(2,1)S(1)}, u32[]{:S(2)}, u32[]{:S(2)}) %collective-permute-start.31) | collective-permute-done | bytes 294944 | tf_op jit(solution)/shard_map/ppermute | solution.py:1079
  242.5 22.0 %attn_fwd.7 = (bf16[288,256]{1,0:T(8,128)(2,1)S(1)}, bf16[288,256]{1,0:T(8,128)(2,1)S(1)}, bf16[288,256]{1,0:T(8,128)(2,1)S(1)}, bf16[288,256]{1,0:T(8,128)(2,1)...) custom-call(s32[55]{0:T(128)S(1)} %concatenate.19.sc, ...), custom_call_target="tpu_custom_call" | custom-call | flops 6568280064 | bytes 12000000 | tf_op jit(solution)/shard_map/attn_fwd/pallas_call | solution.py:456
  292.9 19.2 %collective-permute-done.42.refs_2_ = bf16[288,768]{1,0:T(8,128)(2,1)} collective-permute-done((bf16[288,768]{1,0:T(8,128)(2,1)}, bf16[288,768]{1,0:T(8,128)(2,1)}, u32[]{:S(2)}, u32[]{:S(2)}) %collective-permute-start.42) | collective-permute-done | bytes 442400 | tf_op jit(solution)/shard_map/ppermute | solution.py:974
  324.2 22.7 %attn_fwd.8 = (bf16[288,256]{1,0:T(8,128)(2,1)S(1)}, bf16[288,256]{1,0:T(8,128)(2,1)S(1)}, bf16[288,256]{1,0:T(8,128)(2,1)}, bf16[288,256]{1,0:T(8,128)(2,1)}, b...) custom-call(s32[55]{0:T(128)S(1)} %concatenate.19.sc, ...), custom_call_target="tpu_custom_call" | custom-call | flops 6568280064 | bytes 12000000 | tf_op jit(solution)/shard_map/attn_fwd/pallas_call | solution.py:456
  352.0 12.6 all-gather.8.cloned.1.call-done
  398.0 21.9 %attn_fwd.9 = (bf16[288,256]{1,0:T(8,128)(2,1)S(1)}, bf16[288,256]{1,0:T(8,128)(2,1)S(1)}, bf16[288,256]{1,0:T(8,128)(2,1)S(1)}, bf16[288,256]{1,0:T(8,128)(2,1)...) custom-call(s32[55]{0:T(128)S(1)} %concatenate.19.sc, ...), custom_call_target="tpu_custom_call" | custom-call | flops 6568280064 | bytes 12000000 | tf_op jit(solution)/shard_map/attn_fwd/pallas_call | solution.py:456
  469.9 22.0 %attn_fwd.10 = (bf16[288,256]{1,0:T(8,128)(2,1)S(1)}, bf16[288,256]{1,0:T(8,128)(2,1)S(1)}, bf16[288,256]{1,0:T(8,128)(2,1)S(1)}, bf16[288,256]{1,0:T(8,128)(2,1...) custom-call(s32[55]{0:T(128)S(1)} %concatenate.19.sc, ...), custom_call_target="tpu_custom_call" | custom-call | flops 6568280064 | bytes 12000000 | tf_op jit(solution)/shard_map/attn_fwd/pallas_call | solution.py:456
  513.6 9.5 collective-permute-done.76.refs_2_
  534.1 21.8 %attn_fwd.11 = (bf16[288,256]{1,0:T(8,128)(2,1)S(1)}, bf16[288,256]{1,0:T(8,128)(2,1)S(1)}, bf16[288,256]{1,0:T(8,128)(2,1)S(1)}, bf16[288,256]{1,0:T(8,128)(2,1...) custom-call(s32[55]{0:T(128)S(1)} %concatenate.19.sc, ...), custom_call_target="tpu_custom_call" | custom-call | flops 6568280064 | bytes 12000000 | tf_op jit(solution)/shard_map/attn_fwd/pallas_call | solution.py:456
  577.9 12.5 mlp_bwd.6
  604.4 24.8 %attn_bwd.6 = (bf16[1088,768]{1,0:T(8,128)(2,1)}, bf16[1088,768]{1,0:T(8,128)(2,1)}, bf16[1152,768]{1,0:T(8,128)(2,1)}, bf16[1024,384]{1,0:T(8,128)(2,1)}, f32[3,8,256]{2,1,0:T(8,128)}) custom-call(s32[55]{0:T(128)} %copy-done.42, bf16[288,256]{1,0:T(8,128)(2,1)} %get-tuple-element.417.refs_0_, bf16[288,256]{1,0:T(8,128)(2,1)} %copy-done.373, ...), custom_call_target="tpu_custom_call" | custom-call | flops 12343836672 | bytes 14000000 | tf_op jit(solution)/shard_map/attn_bwd/pallas_call | solution.py:624
  652.2 12.8 dw_mlp.3
  665.8 13.0 mlp_bwd.7
  689.8 25.0 %attn_bwd.7 = (bf16[1088,768]{1,0:T(8,128)(2,1)}, bf16[1088,768]{1,0:T(8,128)(2,1)}, bf16[1152,768]{1,0:T(8,128)(2,1)}, bf16[1024,384]{1,0:T(8,128)(2,1)}, f32[3,8,256]{2,1,0:T(8,128)}) custom-call(s32[55]{0:T(128)} %copy-done.42, bf16[288,256]{1,0:T(8,128)(2,1)} %copy-done.301, bf16[288,256]{1,0:T(8,128)(2,1)} %copy-done.375, bf16[288,256]{1,0:T(8,128)(2,1)} %copy-done.378, ...), custom_call_target="tpu_custom_call" | custom-call | flops 12343836672 | bytes 14000000 | tf_op jit(solution)/shard_map/attn_bwd/pallas_call | solution.py:624
  734.5 13.0 dw_mlp.4
  748.3 12.9 mlp_bwd.8
  772.1 25.0 %attn_bwd.8 = (bf16[1088,768]{1,0:T(8,128)(2,1)}, bf16[1088,768]{1,0:T(8,128)(2,1)}, bf16[1152,768]{1,0:T(8,128)(2,1)}, bf16[1024,384]{1,0:T(8,128)(2,1)}, f32[3,8,256]{2,1,0:T(8,128)}) custom-call(s32[55]{0:T(128)} %copy-done.42, bf16[288,256]{1,0:T(8,128)(2,1)} %copy-done.302, bf16[288,256]{1,0:T(8,128)(2,1)} %copy-done.376, bf16[288,256]{1,0:T(8,128)(2,1)} %copy-done.379, ...), custom_call_target="tpu_custom_call" | custom-call | flops 12343836672 | bytes 14000000 | tf_op jit(solution)/shard_map/attn_bwd/pallas_call | solution.py:624
  816.7 12.9 dw_mlp.5
  830.4 12.9 mlp_bwd.9
  853.6 19.1 %dw_last.3 = (bf16[768,896]{1,0:T(8,128)(2,1)}, bf16[768,896]{1,0:T(8,128)(2,1)}, bf16[768,896]{1,0:T(8,128)(2,1)}, bf16[768,896]{1,0:T(8,128)(2,1)}, bf16[3,2,7...) custom-call(s32[55]{0:T(128)} %copy-done.42, ...), custom_call_target="tpu_custom_call", output_to_operand_aliasing={{4}: (9, {})} | custom-call | flops 3170893824 | bytes 20000000 | tf_op jit(solution)/shard_map/dw_last/pallas_call | solution.py:903
  876.9 24.8 %attn_bwd.9 = (bf16[1088,768]{1,0:T(8,128)(2,1)}, bf16[1088,768]{1,0:T(8,128)(2,1)}, bf16[1152,768]{1,0:T(8,128)(2,1)}, bf16[1024,384]{1,0:T(8,128)(2,1)}, f32[3,8,256]{2,1,0:T(8,128)}) custom-call(s32[55]{0:T(128)} %copy-done.42, bf16[288,256]{1,0:T(8,128)(2,1)} %copy-done.296, bf16[288,256]{1,0:T(8,128)(2,1)} %copy-done.335, bf16[288,256]{1,0:T(8,128)(2,1)} %copy-done.336, ...), custom_call_target="tpu_custom_call" | custom-call | flops 12343836672 | bytes 14000000 | tf_op jit(solution)/shard_map/attn_bwd/pallas_call | solution.py:624
  945.6 14.0 %mlp_bwd.10 = (bf16[3,288,768]{2,1,0:T(8,128)(2,1)}, bf16[4,288,768]{2,1,0:T(8,128)(2,1)}, bf16[4,288,768]{2,1,0:T(8,128)(2,1)}, f32[288,768]{1,0:T(8,128)S(1)},...) custom-call(s32[55]{0:T(128)S(1)} %copy-done.48, ...), custom_call_target="tpu_custom_call" | custom-call | flops 3057647616 | bytes 16000000 | tf_op jit(solution)/shard_map/mlp_bwd/pallas_call | solution.py:297
  974.4 18.9 %dw_last.4 = (bf16[768,896]{1,0:T(8,128)(2,1)}, bf16[768,896]{1,0:T(8,128)(2,1)}, bf16[768,896]{1,0:T(8,128)(2,1)}, bf16[768,896]{1,0:T(8,128)(2,1)}, bf16[3,2,7...) custom-call(s32[55]{0:T(128)} %copy-done.42, ...), custom_call_target="tpu_custom_call", output_to_operand_aliasing={{4}: (9, {})} | custom-call | flops 3170893824 | bytes 20000000 | tf_op jit(solution)/shard_map/dw_last/pallas_call | solution.py:903
  1002.7 25.5 %attn_bwd.10 = (bf16[1088,768]{1,0:T(8,128)(2,1)}, bf16[1088,768]{1,0:T(8,128)(2,1)}, bf16[1152,768]{1,0:T(8,128)(2,1)}, bf16[1024,384]{1,0:T(8,128)(2,1)}, f32[3,8,256]{2,1,0:T(8,128)}) custom-call(s32[55]{0:T(128)} %copy-done.42, bf16[288,256]{1,0:T(8,128)(2,1)} %get-tuple-element.542.refs_0_, bf16[288,256]{1,0:T(8,128)(2,1)} %copy-done.333, ...), custom_call_target="tpu_custom_call" | custom-call | flops 12343836672 | bytes 14000000 | tf_op jit(solution)/shard_map/attn_bwd/pallas_call | solution.py:624
  1073.9 14.1 %mlp_bwd.11 = (bf16[3,288,768]{2,1,0:T(8,128)(2,1)}, bf16[4,288,768]{2,1,0:T(8,128)(2,1)}, bf16[4,288,768]{2,1,0:T(8,128)(2,1)}, f32[288,768]{1,0:T(8,128)S(1)},...) custom-call(s32[55]{0:T(128)S(1)} %copy-done.51, ...), custom_call_target="tpu_custom_call" | custom-call | flops 3057647616 | bytes 16000000 | tf_op jit(solution)/shard_map/mlp_bwd/pallas_call | solution.py:297
  1104.0 18.8 %dw_last.5 = (bf16[768,896]{1,0:T(8,128)(2,1)}, bf16[768,896]{1,0:T(8,128)(2,1)}, bf16[768,896]{1,0:T(8,128)(2,1)}, bf16[768,896]{1,0:T(8,128)(2,1)}, bf16[3,2,7...) custom-call(s32[55]{0:T(128)} %copy-done.42, ...), custom_call_target="tpu_custom_call", output_to_operand_aliasing={{4}: (9, {})} | custom-call | flops 3170893824 | bytes 20000000 | tf_op jit(solution)/shard_map/dw_last/pallas_call | solution.py:903
  1128.4 25.2 %attn_bwd.11 = (bf16[1088,768]{1,0:T(8,128)(2,1)}, bf16[1088,768]{1,0:T(8,128)(2,1)}, bf16[1152,768]{1,0:T(8,128)(2,1)}, bf16[1024,384]{1,0:T(8,128)(2,1)}, f32[3,8,256]{2,1,0:T(8,128)}) custom-call(s32[55]{0:T(128)} %copy-done.42, bf16[288,256]{1,0:T(8,128)(2,1)} %get-tuple-element.597.refs_0_, bf16[288,256]{1,0:T(8,128)(2,1)} %copy-done.334, ...), custom_call_target="tpu_custom_call" | custom-call | flops 12343836672 | bytes 14000000 | tf_op jit(solution)/shard_map/attn_bwd/pallas_call | solution.py:624
  1256.6 10.3 collective-permute-done.194.refs_7_
  (1318 shorter events, 696.2 us)
Async XLA Ops:
  7.2 133.9 %all-gather.4.cloned.1.call-start = ((), (), s32[]{:S(2)}) async-start(), calls=%async_computation | async-start | bytes 11354112 | tf_op jit(solution)/shard_map/all_gather | solution.py:1534
  18.0 251.8 %all-gather.6.cloned.1.call-start = ((), (), s32[]{:S(2)}) async-start(), calls=%async_computation.1 | async-start | bytes 11354112 | tf_op jit(solution)/shard_map/all_gather | solution.py:1534
  18.7 345.9 %all-gather.8.cloned.1.call-start = ((), (), s32[]{:S(2)}) async-start(), calls=%async_computation.2 | async-start | bytes 11354112 | tf_op jit(solution)/shard_map/all_gather | solution.py:1534
  43.6 28.9 %collective-permute-start.18 = (bf16[1,96,768]{2,1,0:T(8,128)(2,1)}, bf16[1,96,768]{2,1,0:T(8,128)(2,1)S(1)}, u32[]{:S(2)}, u32[]{:S(2)}) collective-permute-start(bf16[1,96,768]{2,1,0:T(8,128)(2,1)} %held.2.refs_0_), channel_id=1, source_target_pairs={{0,20},{4,16},{8,28},{12,24},{16,4},{20,0},{24,12},{28,8},{1,21},{... | collective-permute-start | bytes 442376 | tf_op jit(solution)/shard_map/ppermute | solution.py:1079
  45.7 39.1 %collective-permute-start.12 = (bf16[256,768]{1,0:T(8,128)(2,1)S(1)}, bf16[256,768]{1,0:T(8,128)(2,1)}, u32[]{:S(2)}, u32[]{:S(2)}) collective-permute-start(bf16[256,768]{1,0:T(8,128)(2,1)S(1)} %get-tuple-element.355), channel_id=1, source_target_pairs={{0,6},{2,4},{4,2},{6,0},{1,7},{3,5},{5,3},{7,1},{8,14},{10,12},{12... | collective-permute-start | bytes 1179656 | tf_op jit(solution)/shard_map/ppermute | solution.py:985
  48.6 36.6 %collective-permute-start.10 = (bf16[256,768]{1,0:T(8,128)(2,1)S(1)}, bf16[256,768]{1,0:T(8,128)(2,1)S(1)}, u32[]{:S(2)}, u32[]{:S(2)}) collective-permute-start(bf16[256,768]{1,0:T(8,128)(2,1)S(1)} %get-tuple-element.355), channel_id=1, source_target_pairs={{0,4},{4,0},{1,5},{5,1},{2,6},{6,2},{3,7},{7,3},{8,12},{12,8},{9,1... | collective-permute-start | bytes 1179656 | tf_op jit(solution)/shard_map/ppermute | solution.py:979
  48.7 36.6 %collective-permute-start.8 = (bf16[288,768]{1,0:T(8,128)(2,1)S(1)}, bf16[288,768]{1,0:T(8,128)(2,1)}, u32[]{:S(2)}, u32[]{:S(2)}) collective-permute-start(bf16[288,768]{1,0:T(8,128)(2,1)S(1)} %get-tuple-element.354.refs_8_.refs_0_), channel_id=1, source_target_pairs={{0,2},{2,0},{1,3},{3,1},{4,6},{6,4},{5,7},{7,5},{8,10},{10,8},{9,1... | collective-permute-start | bytes 1327112 | tf_op jit(solution)/shard_map/ppermute | solution.py:974
  136.1 57.2 %collective-permute-start.35 = (bf16[2,96,768]{2,1,0:T(8,128)(2,1)}, bf16[2,96,768]{2,1,0:T(8,128)(2,1)}, u32[]{:S(2)}, u32[]{:S(2)}) collective-permute-start(bf16[2,96,768]{2,1,0:T(8,128)(2,1)} %held.3.refs_0_), channel_id=1, source_target_pairs={{0,20},{4,16},{8,28},{12,24},{16,4},{20,0},{24,12},{28,8},{1,21},{... | collective-permute-start | bytes 884744 | tf_op jit(solution)/shard_map/ppermute | solution.py:1079
  137.1 70.4 %collective-permute-start.34 = (bf16[2,96,768]{2,1,0:T(8,128)(2,1)}, bf16[2,96,768]{2,1,0:T(8,128)(2,1)}, u32[]{:S(2)}, u32[]{:S(2)}) collective-permute-start(bf16[2,96,768]{2,1,0:T(8,128)(2,1)} %held.3.refs_0_), channel_id=1, source_target_pairs={{0,16},{4,20},{8,24},{12,28},{16,0},{20,4},{24,8},{28,12},{1,17},{... | collective-permute-start | bytes 884744 | tf_op jit(solution)/shard_map/ppermute | solution.py:1079
  152.3 62.4 %collective-permute-start.25 = (bf16[288,768]{1,0:T(8,128)(2,1)S(1)}, bf16[288,768]{1,0:T(8,128)(2,1)S(1)}, u32[]{:S(2)}, u32[]{:S(2)}) collective-permute-start(bf16[288,768]{1,0:T(8,128)(2,1)S(1)} %get-tuple-element.361.refs_9_.refs_0_), channel_id=1, source_target_pairs={{0,2},{2,0},{1,3},{3,1},{4,6},{6,4},{5,7},{7,5},{8,10},{10,8},{9,1... | collective-permute-start | bytes 1327112 | tf_op jit(solution)/shard_map/ppermute | solution.py:974
  154.0 61.1 %collective-permute-start.29 = (bf16[256,768]{1,0:T(8,128)(2,1)S(1)}, bf16[256,768]{1,0:T(8,128)(2,1)S(1)}, u32[]{:S(2)}, u32[]{:S(2)}) collective-permute-start(bf16[256,768]{1,0:T(8,128)(2,1)S(1)} %get-tuple-element.362), channel_id=1, source_target_pairs={{0,6},{2,4},{4,2},{6,0},{1,7},{3,5},{5,3},{7,1},{8,14},{10,12},{12... | collective-permute-start | bytes 1179656 | tf_op jit(solution)/shard_map/ppermute | solution.py:985
  154.0 61.2 %collective-permute-start.27 = (bf16[256,768]{1,0:T(8,128)(2,1)S(1)}, bf16[256,768]{1,0:T(8,128)(2,1)S(1)}, u32[]{:S(2)}, u32[]{:S(2)}) collective-permute-start(bf16[256,768]{1,0:T(8,128)(2,1)S(1)} %get-tuple-element.362), channel_id=1, source_target_pairs={{0,4},{4,0},{1,5},{5,1},{2,6},{6,2},{3,7},{7,3},{8,12},{12,8},{9,1... | collective-permute-start | bytes 1179656 | tf_op jit(solution)/shard_map/ppermute | solution.py:979
  291.0 29.2 %collective-permute-start.46 = (bf16[256,768]{1,0:T(8,128)(2,1)S(1)}, bf16[256,768]{1,0:T(8,128)(2,1)}, u32[]{:S(2)}, u32[]{:S(2)}) collective-permute-start(bf16[256,768]{1,0:T(8,128)(2,1)S(1)} %get-tuple-element.370), channel_id=1, source_target_pairs={{0,6},{2,4},{4,2},{6,0},{1,7},{3,5},{5,3},{7,1},{8,14},{10,12},{12... | collective-permute-start | bytes 1179656 | tf_op jit(solution)/shard_map/ppermute | solution.py:985
  291.0 29.2 %collective-permute-start.44 = (bf16[256,768]{1,0:T(8,128)(2,1)S(1)}, bf16[256,768]{1,0:T(8,128)(2,1)S(1)}, u32[]{:S(2)}, u32[]{:S(2)}) collective-permute-start(bf16[256,768]{1,0:T(8,128)(2,1)S(1)} %get-tuple-element.370), channel_id=1, source_target_pairs={{0,4},{4,0},{1,5},{5,1},{2,6},{6,2},{3,7},{7,3},{8,12},{12,8},{9,1... | collective-permute-start | bytes 1179656 | tf_op jit(solution)/shard_map/ppermute | solution.py:979
  292.9 31.2 %collective-permute-start.41 = (bf16[288,768]{1,0:T(8,128)(2,1)}, bf16[288,768]{1,0:T(8,128)(2,1)}, u32[]{:S(2)}, u32[]{:S(2)}) collective-permute-start(bf16[288,768]{1,0:T(8,128)(2,1)} %get-tuple-element.369.refs_0_), channel_id=1, source_target_pairs={{0,1},{1,0},{2,3},{3,2},{4,5},{5,4},{6,7},{7,6},{8,9},{9,8},{10,11... | collective-permute-start | bytes 1327112 | tf_op jit(solution)/shard_map/ppermute | solution.py:970
  322.3 27.7 %collective-permute-start.51 = (bf16[512,192]{1,0:T(8,128)(2,1)}, bf16[512,192]{1,0:T(8,128)(2,1)S(1)}, u32[]{:S(2)}, u32[]{:S(2)}) collective-permute-start(bf16[512,192]{1,0:T(8,128)(2,1)} %bitcast.40), channel_id=1, source_target_pairs={{0,4},{4,0},{1,5},{5,1},{2,6},{6,2},{3,7},{7,3},{8,12},{12,8},{9,1... | collective-permute-start | bytes 589832 | tf_op jit(solution)/shard_map/ppermute | solution.py:1179
  395.3 28.0 %collective-permute-start.62 = (bf16[288,192]{1,0:T(8,128)(2,1)S(1)}, bf16[288,192]{1,0:T(8,128)(2,1)S(1)}, u32[]{:S(2)}, u32[]{:S(2)}) collective-permute-start(bf16[288,192]{1,0:T(8,128)(2,1)S(1)} %copy-done.300), channel_id=1, source_target_pairs={{0,1},{1,0},{2,3},{3,2},{4,5},{5,4},{6,7},{7,6},{8,9},{9,8},{10,11... | collective-permute-start | bytes 331784 | tf_op jit(solution)/shard_map/ppermute | solution.py:1007
  597.0 32.3 %collective-permute-start.88 = (bf16[512,192]{1,0:T(8,128)(2,1)S(1)}, bf16[512,192]{1,0:T(8,128)(2,1)S(1)}, u32[]{:S(2)}, u32[]{:S(2)}) collective-permute-start(bf16[512,192]{1,0:T(8,128)(2,1)S(1)} %get-tuple-element.410), channel_id=1, source_target_pairs={{4,0},{0,4},{5,1},{1,5},{6,2},{2,6},{7,3},{3,7},{12,8},{8,12},{13,... | collective-permute-start | bytes 589832 | tf_op jit(solution)/shard_map/ppermute | solution.py:1218
  873.6 32.5 %collective-permute-start.130 = (bf16[768,896]{1,0:T(8,128)(2,1)}, bf16[768,896]{1,0:T(8,128)(2,1)S(1)}, u32[]{:S(2)}, u32[]{:S(2)}) collective-permute-start(bf16[768,896]{1,0:T(8,128)(2,1)} %get-tuple-element.508.refs_21_), channel_id=1, source_target_pairs={{0,4},{4,0},{1,5},{5,1},{2,6},{6,2},{3,7},{7,3},{8,12},{12,8},{9,1... | collective-permute-start | bytes 4128776 | tf_op jit(solution)/shard_map/ppermute | solution.py:1273
  875.4 33.2 %collective-permute-start.129 = (bf16[768,896]{1,0:T(8,128)(2,1)}, bf16[768,896]{1,0:T(8,128)(2,1)S(1)}, u32[]{:S(2)}, u32[]{:S(2)}) collective-permute-start(bf16[768,896]{1,0:T(8,128)(2,1)} %get-tuple-element.507.refs_20_), channel_id=1, source_target_pairs={{0,2},{2,0},{1,3},{3,1},{4,6},{6,4},{5,7},{7,5},{8,10},{10,8},{9,1... | collective-permute-start | bytes 4128776 | tf_op jit(solution)/shard_map/ppermute | solution.py:1273
  967.3 31.5 %collective-permute-start.144 = (bf16[384,768]{1,0:T(8,128)(2,1)}, bf16[384,768]{1,0:T(8,128)(2,1)}, u32[]{:S(2)}, u32[]{:S(2)}) collective-permute-start(bf16[384,768]{1,0:T(8,128)(2,1)} %get-tuple-element.529.refs_14_), channel_id=1, source_target_pairs={{0,4},{4,0},{1,5},{5,1},{2,6},{6,2},{3,7},{7,3},{8,12},{12,8},{9,1... | collective-permute-start | bytes 1769480 | tf_op jit(solution)/shard_map/ppermute | solution.py:1273
  994.1 37.6 %collective-permute-start.149 = (bf16[768,896]{1,0:T(8,128)(2,1)}, bf16[768,896]{1,0:T(8,128)(2,1)S(1)}, u32[]{:S(2)}, u32[]{:S(2)}) collective-permute-start(bf16[768,896]{1,0:T(8,128)(2,1)} %get-tuple-element.560.refs_25_), channel_id=1, source_target_pairs={{0,4},{4,0},{1,5},{5,1},{2,6},{6,2},{3,7},{7,3},{8,12},{12,8},{9,1... | collective-permute-start | bytes 4128776 | tf_op jit(solution)/shard_map/ppermute | solution.py:1273
  995.2 39.1 %collective-permute-start.148 = (bf16[768,896]{1,0:T(8,128)(2,1)}, bf16[768,896]{1,0:T(8,128)(2,1)S(1)}, u32[]{:S(2)}, u32[]{:S(2)}) collective-permute-start(bf16[768,896]{1,0:T(8,128)(2,1)} %get-tuple-element.559.refs_24_), channel_id=1, source_target_pairs={{0,2},{2,0},{1,3},{3,1},{4,6},{6,4},{5,7},{7,5},{8,10},{10,8},{9,1... | collective-permute-start | bytes 4128776 | tf_op jit(solution)/shard_map/ppermute | solution.py:1273
  996.5 31.6 %collective-permute-start.146 = (bf16[192,896]{1,0:T(8,128)(2,1)}, bf16[192,896]{1,0:T(8,128)(2,1)S(1)}, u32[]{:S(2)}, u32[]{:S(2)}) collective-permute-start(bf16[192,896]{1,0:T(8,128)(2,1)} %copy-done.155), channel_id=1, source_target_pairs={{0,8},{8,0},{16,24},{24,16},{1,9},{9,1},{17,25},{25,17},{2,10},{10... | collective-permute-start | bytes 1032200 | tf_op jit(solution)/shard_map/ppermute | solution.py:1273
  998.8 30.9 %collective-permute-start.145 = (bf16[192,896]{1,0:T(8,128)(2,1)}, bf16[192,896]{1,0:T(8,128)(2,1)S(1)}, u32[]{:S(2)}, u32[]{:S(2)}) collective-permute-start(bf16[192,896]{1,0:T(8,128)(2,1)} %copy-done.156), channel_id=1, source_target_pairs={{0,8},{8,0},{16,24},{24,16},{1,9},{9,1},{17,25},{25,17},{2,10},{10... | collective-permute-start | bytes 1032200 | tf_op jit(solution)/shard_map/ppermute | solution.py:1273
  1000.6 29.8 %collective-permute-start.147 = (bf16[192,768]{1,0:T(8,128)(2,1)S(1)}, bf16[192,768]{1,0:T(8,128)(2,1)S(1)}, u32[]{:S(2)}, u32[]{:S(2)}) collective-permute-start(bf16[192,768]{1,0:T(8,128)(2,1)S(1)} %get-tuple-element.556.refs_20_.refs_23_), channel_id=1, source_target_pairs={{0,8},{8,0},{16,24},{24,16},{1,9},{9,1},{17,25},{25,17},{2,10},{10... | collective-permute-start | bytes 884744 | tf_op jit(solution)/shard_map/ppermute | solution.py:1273
  1095.9 29.3 %collective-permute-start.163 = (bf16[384,768]{1,0:T(8,128)(2,1)}, bf16[384,768]{1,0:T(8,128)(2,1)}, u32[]{:S(2)}, u32[]{:S(2)}) collective-permute-start(bf16[384,768]{1,0:T(8,128)(2,1)} %copy-done.129), channel_id=1, source_target_pairs={{0,4},{4,0},{1,5},{5,1},{2,6},{6,2},{3,7},{7,3},{8,12},{12,8},{9,1... | collective-permute-start | bytes 1769480 | tf_op jit(solution)/shard_map/ppermute | solution.py:1273
  1123.6 32.8 %collective-permute-start.164 = (bf16[768,896]{1,0:T(8,128)(2,1)}, bf16[768,896]{1,0:T(8,128)(2,1)S(1)}, u32[]{:S(2)}, u32[]{:S(2)}) collective-permute-start(bf16[768,896]{1,0:T(8,128)(2,1)} %get-tuple-element.613.refs_24_), channel_id=1, source_target_pairs={{0,2},{2,0},{1,3},{3,1},{4,6},{6,4},{5,7},{7,5},{8,10},{10,8},{9,1... | collective-permute-start | bytes 4128776 | tf_op jit(solution)/shard_map/ppermute | solution.py:1273
  1124.4 34.1 %collective-permute-start.166 = (bf16[768,896]{1,0:T(8,128)(2,1)}, bf16[768,896]{1,0:T(8,128)(2,1)S(1)}, u32[]{:S(2)}, u32[]{:S(2)}) collective-permute-start(bf16[768,896]{1,0:T(8,128)(2,1)} %get-tuple-element.614.refs_25_), channel_id=1, source_target_pairs={{0,4},{4,0},{1,5},{5,1},{2,6},{6,2},{3,7},{7,3},{8,12},{12,8},{9,1... | collective-permute-start | bytes 4128776 | tf_op jit(solution)/shard_map/ppermute | solution.py:1273
  1249.8 32.5 %collective-permute-start.190 = (bf16[96,896]{1,0:T(8,128)(2,1)S(1)}, bf16[96,896]{1,0:T(8,128)(2,1)S(1)}, u32[]{:S(2)}, u32[]{:S(2)}) collective-permute-start(bf16[96,896]{1,0:T(8,128)(2,1)S(1)} %get-tuple-element.638.refs_10_), channel_id=1, source_target_pairs={{0,16},{8,24},{16,0},{24,8},{1,17},{9,25},{17,1},{25,9},{2,18},{10... | collective-permute-start | bytes 516104 | tf_op jit(solution)/shard_map/ppermute | solution.py:1273
  1249.8 32.4 %collective-permute-start.187 = (f32[3,8,768]{2,1,0:T(8,128)S(1)}, f32[3,8,768]{2,1,0:T(8,128)S(1)}, u32[]{:S(2)}, u32[]{:S(2)}) collective-permute-start(f32[3,8,768]{2,1,0:T(8,128)S(1)} %add.308), channel_id=1, source_target_pairs={{0,16},{8,24},{16,0},{24,8},{1,17},{9,25},{17,1},{25,9},{2,18},{10... | collective-permute-start | bytes 221192 | tf_op jit(solution)/shard_map/ppermute | solution.py:1441
  1252.8 35.8 %collective-permute-start.189 = (bf16[96,896]{1,0:T(8,128)(2,1)S(1)}, bf16[96,896]{1,0:T(8,128)(2,1)}, u32[]{:S(2)}, u32[]{:S(2)}) collective-permute-start(bf16[96,896]{1,0:T(8,128)(2,1)S(1)} %get-tuple-element.636.refs_9_), channel_id=1, source_target_pairs={{0,16},{8,24},{16,0},{24,8},{1,17},{9,25},{17,1},{25,9},{2,18},{10... | collective-permute-start | bytes 516104 | tf_op jit(solution)/shard_map/ppermute | solution.py:1273
  (551 other events, 7166.7 us)
Sparse Core Ops, SparseCore 0:
  18.1 115.9 all-gather.3
  137.6 123.2 all-gather.5
  263.8 100.7 all-gather.7
